TPU v7x, 128 devices: a whole 4x4x4 slice. The times are simulated.
128 devices in a mesh: rep: 4 (over z), row: 32 (over x, y, core).
Axes of the slice: x: 4, y: 4, z: 4, core: 2. Of those that a mesh axis runs over, the one named last changes fastest.
Arguments:
- basis_vecs: bfloat16 [96, 2097152], P('rep', 'row'), may hold values from -12 to 12
- potential: float32 [2097152], P('row'), may hold values from 0.3 to 3
- surface: bfloat16 [256, 256], replicated, may hold values from -0.375 to 0.375
- grid_perm: int32 [2097152], P('row'), may hold values from 0 to 65535, as said below
- kinetic: bfloat16 [256, 256], replicated, may hold values from -0.375 to 0.375
- couplings: int32 [24576, 2], P('row'), may hold values from 0 to 8191, as said below
- coupling_coefficient: float32 [24576], P('row'), may hold values from -6 to 6
- precond: float32 [32, 4, 16384], P('row', 'rep'), may hold values from 0.1 to 4
Outputs:
- new_block: float32 [96, 32, 4, 16384], P(None, 'row', 'rep')
- rayleigh: float32 [96, 96], replicated
Inputs may be any that keep to these rules, and one draw needn't show every extreme that they name: `grid_perm`: each index of row holds 65536 consecutive entries forming a permutation of 0 to 65535. `couplings`: entry a 3 + m has block row a; for m = 0 the block column is a, the other 2 columns lie 1 to 2 blocks from a.
All inputs are finite; a program needn't handle non-finite values.
Results may differ from a plain program's by a relative error of at most 0.0003.
The roundings to bfloat16 on the way count: a program that leaves them out, or rounds other values in their place, can miss the bound.
Values may be sent and summed in bfloat16 or wider, within the bound.
No kernel may reach another device: no remote copies, remote signals or barrier semaphores. Data moves between devices by JAX's collectives and lax.ppermute only.
A program may use at most 192 MiB of HBM per device.

v0:
```python
import jax
import jax.numpy as jnp
from jax import lax
from jax.sharding import PartitionSpec as P

HB = 2
COUPLINGS_PER_ROW = 3


def extended(block, sides, width):
    for axis, dim in sides:
        count = lax.axis_size(axis)
        forward = [(i, i + 1) for i in range(count - 1)]
        backward = [(target, source) for source, target in forward]
        low = lax.ppermute(
            lax.slice_in_dim(block, block.shape[dim] - width, None, axis=dim), axis, forward
        )
        high = lax.ppermute(lax.slice_in_dim(block, 0, width, axis=dim), axis, backward)
        block = jnp.concatenate([low, block, high], axis=dim)
    return block


def grid_work(target_columns, grid_perm, potential, surface):
    block_length = surface.shape[0]
    vec_count = target_columns.shape[0]
    ordered = jnp.take(target_columns, grid_perm, axis=1)
    blocks = ordered.reshape(vec_count, -1, block_length)
    projected = jnp.einsum("cbk,kl->cbl", blocks, surface, preferred_element_type=jnp.float32)
    weighted = (projected * potential.reshape(-1, block_length)).astype(jnp.bfloat16)
    returned = jnp.einsum("cbl,kl->cbk", weighted, surface, preferred_element_type=jnp.float32)
    returned = returned.astype(jnp.bfloat16).reshape(vec_count, -1)
    return jnp.zeros_like(returned).at[:, grid_perm].set(returned)


def surface_pass(target_columns, grid_perm, potential, surface):
    restored = grid_work(target_columns, grid_perm, potential, surface)
    return lax.all_to_all(restored, "row", split_axis=1, concat_axis=1, tiled=True)


def inner_rows(left_side, right_side, highest):
    return lax.dot_general(
        left_side,
        right_side,
        (((1,), (1,)), ((), ())),
        precision=highest,
        preferred_element_type=jnp.float32,
    )


def body(
    basis_vecs, potential, surface, grid_perm, kinetic, couplings, coupling_coefficient, precond
):
    vector_columns, row_count = basis_vecs.shape
    block_length = surface.shape[0]
    total_block_count = row_count // block_length
    pieces = lax.axis_size("row")
    reps = lax.axis_size("rep")
    seg_rows = row_count // (pieces * reps)
    all_vecs = vector_columns * reps
    highest = lax.Precision.HIGHEST
    pot_image = (lambda arrived: surface_pass(arrived, grid_perm, potential, surface))(
        lax.all_to_all(basis_vecs, "row", split_axis=1, concat_axis=1, tiled=True)
    )
    padded = extended(basis_vecs, (("row", 1),), HB * block_length)
    padded_blocks = padded.reshape(vector_columns, total_block_count + 2 * HB, block_length)
    first_block = lax.axis_index("row") * total_block_count - HB
    picked_entries = jnp.take(padded_blocks, couplings[:, 1] - first_block, axis=1)
    picked_entries = picked_entries.reshape(
        vector_columns, total_block_count, COUPLINGS_PER_ROW, block_length
    ).astype(jnp.float32)
    source_rows = jnp.sum(
        picked_entries * coupling_coefficient.reshape(1, total_block_count, COUPLINGS_PER_ROW, 1),
        axis=2,
    ).astype(jnp.bfloat16)
    kinetic_part = jnp.einsum(
        "cbk,kl->cbl", source_rows, kinetic, preferred_element_type=jnp.float32
    ).reshape(vector_columns, row_count)
    image_vecs = (kinetic_part + pot_image.astype(jnp.float32)).astype(jnp.bfloat16)
    basis_moved, image_moved = (
        lax.all_to_all(
            basis_vecs.reshape(vector_columns, pieces, reps, seg_rows),
            "rep",
            split_axis=2,
            concat_axis=0,
            tiled=True,
        ),
        lax.all_to_all(
            image_vecs.reshape(vector_columns, pieces, reps, seg_rows),
            "rep",
            split_axis=2,
            concat_axis=0,
            tiled=True,
        ),
    )
    basis_split = basis_moved.reshape(all_vecs, -1)
    image_split = image_moved.reshape(all_vecs, -1)
    full_rows = row_count * pieces
    gram_part = inner_rows(basis_split, image_split, None)
    rayleigh = lax.psum(gram_part, ("rep", "row")) / full_rows
    basis_wide = basis_split.astype(jnp.float32)
    residual = image_split.astype(jnp.float32) - jnp.dot(rayleigh.T, basis_wide, precision=highest)
    corrected = residual * precond.reshape(1, -1)
    local_gram = inner_rows(corrected, corrected, highest) / full_rows
    lower_factor = jnp.linalg.cholesky(lax.psum(local_gram, ("rep", "row")))
    solved = lax.linalg.triangular_solve(lower_factor, corrected, left_side=True, lower=True)
    return (solved.reshape(solved.shape[0], 1, 1, -1), rayleigh)


def solution(mesh):
    in_specs = (
        P("rep", "row"),
        P("row"),
        P(),
        P("row"),
        P(),
        P("row", None),
        P("row"),
        P("row", "rep", None),
    )
    out_specs = (P(None, "row", "rep", None), P())
    return jax.shard_map(body, mesh=mesh, in_specs=in_specs, out_specs=out_specs, check_vma=False)
```

profile of v0, /device:TPU:1, one launch (start us, length us, event | category | flops | bytes accessed | tf_op | source)
XLA Modules:
  0.0 822.8 jit_solution(6265582723816258944)
XLA Ops:
  0.6 0.0 copy-start
  0.6 0.0 copy-start.5
  0.7 4.0 copy.76
  4.7 8.6 %all-to-all-start = ((bf16[24,32,2048]{2,0,1:T(8,128)(2,1)}), bf16[24,32,2048]{2,0,1:T(8,128)(2,1)S(1)}, u32[]{:S(2)}, u32[]{:S(2)}) async-start(bf16[24,32,2048]{2,0,1:T(8,128)(2,1)} %bitcast.75), calls=%async_computation | async-start | bytes 6291456 | tf_op jit(solution)/shard_map/all_to_all | solution.py:62
  13.3 1.7 mul.37
  15.0 0.0 copy-done.5
  15.0 0.7 compare_and_fusion
  15.7 1.5 broadcast_in_dim.37
  17.2 1.7 broadcast_clamp_fusion
  18.9 34.1 %all-to-all-done = bf16[24,32,2048]{2,0,1:T(8,128)(2,1)S(1)} async-done(((bf16[24,32,2048]{2,0,1:T(8,128)(2,1)}), bf16[24,32,2048]{2,0,1:T(8,128)(2,1)S(1)}, u32[]{:S(2)}, u32[]{:S(2)}) %all-to-all-start) | async-done | bytes 3145760 | tf_op jit(solution)/shard_map/all_to_all | solution.py:62
  53.0 10.9 %copy.45 = bf16[24,32,2048]{0,2,1:T(8,128)(2,1)} copy(bf16[24,32,2048]{2,0,1:T(8,128)(2,1)S(1)} %all-to-all-done) | data formatting | bytes 6291456 | tf_op jit(solution)/shard_map/all_to_all | solution.py:62
  64.0 225.6 %gather_fusion.1 = bf16[65536,24]{1,0:T(8,128)(2,1)} fusion(bf16[24,65536]{0,1:T(8,128)(2,1)} %bitcast.63, s32[65536]{0:T(1024)S(1)} %get-tuple-element.14), kind=kCustom, calls=%fused_computation.1 | custom fusion | bytes 6553600 | tf_op jit(solution)/shard_map/jit(_take)/gather | solution.py:26
  289.6 12.6 %copy.46 = bf16[24,256,256]{2,0,1:T(8,128)(2,1)S(1)} copy(bf16[24,256,256]{0,2,1:T(8,128)(2,1)} %bitcast.72) | data formatting | bytes 6291456 | tf_op jit(solution)/shard_map/jit(_take)/gather | solution.py:26
  302.2 0.0 copy-done
  302.2 0.0 copy-done.6
  302.2 2.0 multiply_convert_fusion
  304.2 1.2 fusion.13
  305.4 11.2 %copy.58 = bf16[24,256,256]{0,2,1:T(8,128)(2,1)} copy(bf16[24,256,256]{2,1,0:T(8,128)(2,1)S(1)} %fusion.13) | data formatting | bytes 6291456 | tf_op jit(solution)/shard_map/reshape | solution.py:31
  316.6 171.9 %scatter_custom_fusion = bf16[24,65536]{0,1:T(8,128)(2,1)} fusion(s32[65536]{0:T(1024)} %get-tuple-element.15, bf16[65536,24]{1,0:T(8,128)(2,1)} %bitcast.73, bf16[]{:T(256)} %constant.82.clone.1), kind=kCustom, calls=%fused_computation.7 | custom fusion | bytes 3146240 | tf_op jit(solution)/shard_map/scatter | solution.py:32
  488.6 14.0 %copy.49 = bf16[24,32,2048]{2,0,1:T(8,128)(2,1)} copy(bf16[24,32,2048]{0,2,1:T(8,128)(2,1)} %bitcast.64) | data formatting | bytes 6291456 | tf_op jit(solution)/shard_map/all_to_all | solution.py:37
  502.6 5.3 all-to-all-start.1
  507.9 0.0 copy-done.3
  507.9 2.2 collective-permute-start.1
  510.1 3.4 collective-permute-start
  513.6 0.0 copy-start.9
  513.6 3.8 reshape.74
  517.4 4.3 copy.52
  521.7 0.2 mul.34
  521.9 0.2 broadcast_in_dim.32
  522.1 25.6 %all-to-all-done.1 = bf16[24,32,2048]{2,0,1:T(8,128)(2,1)} async-done(((bf16[24,32,2048]{2,0,1:T(8,128)(2,1)}), bf16[24,32,2048]{2,0,1:T(8,128)(2,1)}, u32[]{:S(2)}, u32[]{:S(2)}) %all-to-all-start.1) | async-done | bytes 3145760 | tf_op jit(solution)/shard_map/all_to_all | solution.py:37
  547.7 5.2 all-to-all-start.3
  552.9 0.0 collective-permute-done.1
  552.9 0.0 collective-permute-done
  552.9 2.1 pad_maximum_fusion
  555.0 0.2 copy.75
  555.3 5.3 gather_fusion
  560.5 7.2 multiply_reduce_fusion
  567.8 3.9 fusion.6
  571.6 8.1 reshape.71
  579.7 8.3 %reshape.77 = f32[24,32,4,512]{3,2,0,1:T(4,128)} reshape(bf16[24,32,2048]{2,0,1:T(8,128)(2,1)} %all-to-all-done.1) | data formatting | bytes 9437184 | tf_op jit(solution)/shard_map/convert_element_type | solution.py:78
  588.1 11.3 %fusion.3 = bf16[24,32,4,512]{3,1,0,2:T(8,128)(2,1)} fusion(f32[24,32,4,512]{3,2,0,1:T(4,128)} %reshape.77, f32[24,32,4,512]{3,2,1,0:T(4,128)} %reshape.71), kind=kLoop, calls=%fused_computation.10 | loop fusion | flops 3145728 | bytes 15728640 | tf_op jit(solution)/shard_map/convert_element_type | solution.py:78
  599.3 0.0 all-to-all-done.3
  599.3 4.9 all-to-all-start.2
  604.2 3.9 copy.62
  608.1 33.4 %all-to-all-done.2 = bf16[24,32,4,512]{3,1,0,2:T(8,128)(2,1)} async-done(((bf16[24,32,4,512]{3,1,0,2:T(8,128)(2,1)}), bf16[24,32,4,512]{3,1,0,2:T(8,128)(2,1)}, u32[]{:S(2)}, u32[]{:S(2)}) %all-to-all-start.2) | async-done | bytes 3145760 | tf_op jit(solution)/shard_map/all_to_all | solution.py:87
  641.6 4.0 copy.61
  645.5 0.0 copy-start.4
  645.5 1.7 copy-done.4
  647.2 1.0 convolution_bitcast_fusion.1
  648.2 63.8 %psum.14 = f32[96,96]{0,1:T(8,128)S(1)} all-reduce(f32[96,96]{0,1:T(8,128)S(1)} %convolution_bitcast_fusion.1), channel_id=1, replica_groups=mesh['rep'=4,'row'=32] {'rep','row'}, use_global_device_ids=true, to_apply=%region_2.3 | all-reduce | flops 9216 | bytes 73728 | tf_op jit(solution)/shard_map/psum | solution.py:99
  711.9 5.0 fusion
  716.9 0.0 copy-start.2
  716.9 2.7 copy-done.2
  719.6 5.0 convolution_multiply_fusion
  724.7 64.0 %psum.15 = f32[96,96]{0,1:T(8,128)S(1)} all-reduce(f32[96,96]{0,1:T(8,128)S(1)} %convolution_multiply_fusion), channel_id=1, replica_groups=mesh['rep'=4,'row'=32] {'rep','row'}, use_global_device_ids=true, to_apply=%region_3.4 | all-reduce | flops 9216 | bytes 73728 | tf_op jit(solution)/shard_map/psum | solution.py:104
  788.7 0.1 copy.54
  788.8 8.8 %cholesky.16 = f32[96,96]{1,0:T(8,128)S(1)} custom-call(f32[96,96]{1,0:T(8,128)S(1)} %fusion.22), custom_call_target="Cholesky" | custom-call | tf_op jit(solution)/shard_map/jit(cholesky)/cholesky | solution.py:104
  797.6 0.6 compare_reduce_fusion
  798.2 0.7 fusion.20
  798.9 7.4 custom-call.6
  806.3 0.0 copy-start.1
  806.3 7.9 convolution_bitcast_fusion
  814.2 7.5 copy.55
  821.6 0.7 copy.56
  (17 shorter events, 0.1 us)
Async XLA Ops:
  0.6 301.6 %copy-start = (bf16[256,256]{1,0:T(8,128)(2,1)S(1)}, bf16[256,256]{1,0:T(8,128)(2,1)}, u32[]{:S(2)}) copy-start(bf16[256,256]{1,0:T(8,128)(2,1)} %param.10) | copy-start | bytes 393220
  0.6 14.4 %copy-start.5 = (s32[65536]{0:T(1024)S(1)}, s32[65536]{0:T(1024)}, u32[]{:S(2)}) copy-start(s32[65536]{0:T(1024)} %param.11) | copy-start | bytes 786436
  4.7 48.4 %all-to-all-start = ((bf16[24,32,2048]{2,0,1:T(8,128)(2,1)}), bf16[24,32,2048]{2,0,1:T(8,128)(2,1)S(1)}, u32[]{:S(2)}, u32[]{:S(2)}) async-start(bf16[24,32,2048]{2,0,1:T(8,128)(2,1)} %bitcast.75), calls=%async_computation | async-start | bytes 6291456 | tf_op jit(solution)/shard_map/all_to_all | solution.py:62
  289.6 12.6 %copy-start.6 = (f32[256,256]{1,0:T(8,128)S(1)}, f32[256,256]{1,0:T(8,128)}, u32[]{:S(2)}) copy-start(f32[256,256]{1,0:T(8,128)} %mul.37) | copy-start | bytes 786436
  502.6 5.3 copy-start.3
  502.6 10.9 %copy-start.10 = (s32[768,2]{0,1:T(2,128)S(1)}, s32[768,2]{0,1:T(2,128)}, u32[]{:S(2)}) copy-start(s32[768,2]{0,1:T(2,128)} %param.13) | copy-start | bytes 18436
  502.6 45.1 %all-to-all-start.1 = ((bf16[24,32,2048]{2,0,1:T(8,128)(2,1)}), bf16[24,32,2048]{2,0,1:T(8,128)(2,1)}, u32[]{:S(2)}, u32[]{:S(2)}) async-start(bf16[24,32,2048]{2,0,1:T(8,128)(2,1)} %copy.49), calls=%async_computation.1 | async-start | bytes 6291456 | tf_op jit(solution)/shard_map/all_to_all | solution.py:37
  507.9 45.0 %collective-permute-start.1 = (bf16[24,512]{1,0:T(8,128)(2,1)S(1)}, bf16[24,512]{1,0:T(8,128)(2,1)S(1)}, u32[]{:S(2)}, u32[]{:S(2)}) collective-permute-start(bf16[24,512]{1,0:T(8,128)(2,1)S(1)} %get-tuple-element.13), channel_id=1, source_target_pairs={{1,0},{2,1},{3,2},{4,3},{5,4},{6,5},{7,6},{8,7},{9,8},{10,9},{11,1... | collective-permute-start | bytes 73736 | tf_op jit(solution)/shard_map/ppermute | solution.py:18
  510.1 42.8 %collective-permute-start = (bf16[24,512]{1,0:T(8,128)(2,1)S(1)}, bf16[24,512]{1,0:T(8,128)(2,1)S(1)}, u32[]{:S(2)}, u32[]{:S(2)}) collective-permute-start(bf16[24,512]{1,0:T(8,128)(2,1)S(1)} %get-tuple-element.12), channel_id=1, source_target_pairs={{0,1},{1,2},{2,3},{3,4},{4,5},{5,6},{6,7},{7,8},{8,9},{9,10},{10,1... | collective-permute-start | bytes 73736 | tf_op jit(solution)/shard_map/ppermute | solution.py:15
  513.6 8.1 copy-start.9
  547.7 51.6 %all-to-all-start.3 = ((bf16[24,32,4,512]{3,1,0,2:T(8,128)(2,1)}), bf16[24,32,4,512]{3,1,0,2:T(8,128)(2,1)}, u32[]{:S(2)}, u32[]{:S(2)}) async-start(bf16[24,32,4,512]{3,1,0,2:T(8,128)(2,1)} %copy.52), calls=%async_computation.3 | async-start | bytes 6291456 | tf_op jit(solution)/shard_map/all_to_all | solution.py:80
  560.5 7.3 copy-start.7
  599.3 42.2 %all-to-all-start.2 = ((bf16[24,32,4,512]{3,1,0,2:T(8,128)(2,1)}), bf16[24,32,4,512]{3,1,0,2:T(8,128)(2,1)}, u32[]{:S(2)}, u32[]{:S(2)}) async-start(bf16[24,32,4,512]{3,1,0,2:T(8,128)(2,1)} %fusion.3), calls=%async_computation.2 | async-start | bytes 6291456 | tf_op jit(solution)/shard_map/all_to_all | solution.py:87
  641.6 70.4 %copy-start.8 = (f32[1,1,16384]{2,1,0:T(1,128)S(1)}, f32[1,1,16384]{2,1,0:T(1,128)}, u32[]{:S(2)}) copy-start(f32[1,1,16384]{2,1,0:T(1,128)} %param.15) | copy-start | bytes 196612
  645.5 1.7 copy-start.4
  716.9 2.7 copy-start.2
  806.3 16.1 %copy-start.1 = (bf16[256,256]{1,0:T(8,128)(2,1)S(1)}, bf16[256,256]{1,0:T(8,128)(2,1)}, u32[]{:S(2)}) copy-start(bf16[256,256]{1,0:T(8,128)(2,1)} %param.10) | copy-start | bytes 393220
where the time goes:
time: 833 us; the launch traced here: 823 us
  local copies, waits for them, and re-layouts  505 us (61%)
  blocking collectives  128 us (15%)
  waiting for transfers between devices  93.1 us (11%)
  other arithmetic  40.5 us (5%)
  starting transfers between devices  29.5 us (4%)
  matrix products  25.9 us (3%)
    gather x2, local copies, waits for them, and re-layouts, grid_work(): ordered = jnp.take(target_columns, grid_perm, axis=1)  238 us
    scatter x1, local copies, waits for them, and re-layouts, grid_work(): return jnp.zeros_like(returned).at[:, grid_perm].set(returned)  172 us
    psum x1, blocking collectives, body(): lower_factor = jnp.linalg.cholesky(lax.psum(local_gram, ('rep', 'row')))  64 us
    psum x1, blocking collectives, body(): rayleigh = lax.psum(gram_part, ('rep', 'row')) / full_rows  63.8 us
    all_to_all x1, waiting for transfers between devices, body(): lax.all_to_all(basis_vecs, 'row', split_axis=1, concat_axis=1, tiled=True)  34.1 us
    all_to_all x1, waiting for transfers between devices, body(): lax.all_to_all(image_vecs.reshape(vector_columns, pieces, reps, seg_rows)...  33.4 us
    all_to_all x1, waiting for transfers between devices, surface_pass(): lax.all_to_all(restored, 'row', split_axis=1, concat_axis=1, tiled=True)  25.6 us
    unnamed x26, local copies, waits for them, and re-layouts  20.5 us
  transfers between devices with their start and end apart: 6, of which 3 were waited for; matrix products, arithmetic and copies ran while one was open for 8% of the time, Pallas kernels for 0%

commit v1 on v0

v1 whole, which is shorter than its diff:
```python
import functools

import jax
import jax.numpy as jnp
from jax import lax
from jax.experimental import pallas as pl
from jax.experimental.pallas import tpu as pltpu
from jax.sharding import PartitionSpec as P

HB = 2
COUPLINGS_PER_ROW = 3
BLK = 256
PAD = 32
GROUPS = 4
LANES = 128
SPAN = GROUPS * BLK
DEPTH = 4
VMEM_LIMIT = 60 * 2**20
NT = (((1,), (1,)), ((), ()))
WHOLE = pl.BlockSpec(memory_space=pltpu.VMEM)
SCALARS = pl.BlockSpec(memory_space=pltpu.SMEM)


def dot_nt(a, b):
    return lax.dot_general(a, b, NT, preferred_element_type=jnp.float32)


def dot_exact(a, b):
    return jnp.dot(a, b, precision=lax.Precision.HIGHEST, preferred_element_type=jnp.float32)


def iota(shape, dim):
    return lax.broadcasted_iota(jnp.int32, shape, dim)


def three_parts(x):
    high = x.astype(jnp.bfloat16)
    rest = x - high.astype(jnp.float32)
    middle = rest.astype(jnp.bfloat16)
    low = (rest - middle.astype(jnp.float32)).astype(jnp.bfloat16)
    return [high, middle, low]


def inverse_kernel(reps, perm_ref, out_ref, acc_ref):
    blocks = perm_ref.shape[0]
    acc_ref[...] = jnp.zeros_like(acc_ref)
    step = 4
    rows = iota((BLK, BLK), 0)
    lane = iota((BLK, BLK), 1).astype(jnp.float32)

    @pl.loop(0, blocks // 8)
    def _(i):
        tile = perm_ref[pl.ds(pl.multiple_of(i * 8, 8), 8), :]
        high = tile >> 8
        low = tile & 255
        for part in range(8 // step):
            left, right = [], []
            for k in range(step):
                at = part * step + k
                hit = rows == high[at:at + 1, :]
                number = (i * 8 + at).astype(jnp.float32)
                left.append(jnp.concatenate(
                    [jnp.where(hit, number, 0.0), jnp.where(hit, lane, 0.0)], axis=0
                ).astype(jnp.bfloat16))
                right.append(jnp.where(rows == low[at:at + 1, :], 1.0, 0.0).astype(jnp.bfloat16))
            acc_ref[...] += dot_nt(jnp.concatenate(left, axis=1), jnp.concatenate(right, axis=1))

    per_rep = 8 // reps
    for d in range(blocks // 8):
        tile = acc_ref[d * 8:(d + 1) * 8, :] * 256.0 + acc_ref[BLK + d * 8:BLK + (d + 1) * 8, :]
        tile = tile.astype(jnp.int32)
        for b in range(reps):
            start = b * (blocks // reps) + d * per_rep
            out_ref[start:start + per_rep, :] = tile[b * per_rep:(b + 1) * per_rep, :]


def inverse_of(perm, reps):
    blocks = perm.shape[0] // BLK
    return pl.pallas_call(
        functools.partial(inverse_kernel, reps),
        out_shape=jax.ShapeDtypeStruct((blocks, BLK), jnp.int32),
        in_specs=[WHOLE],
        out_specs=WHOLE,
        scratch_shapes=[pltpu.VMEM((2 * BLK, BLK), jnp.float32)],
        compiler_params=pltpu.CompilerParams(vmem_limit_bytes=VMEM_LIMIT),
        cost_estimate=pl.CostEstimate(
            flops=4 * BLK * BLK * blocks * BLK, bytes_accessed=8 * blocks * BLK, transcendentals=0
        ),
    )(perm.reshape(blocks, BLK)).reshape(-1)


def stream(index_ref, count, slots, sems, table_ref, rows_refs, work):
    sublane = iota((8, LANES), 0)

    def fetch(i, slot):
        start = pl.multiple_of(jnp.minimum(i, count - 1) * SPAN, SPAN)
        return pltpu.make_async_copy(index_ref.at[pl.ds(start, SPAN)], slots[slot], sems.at[slot])

    def gather(slot, rows_ref):
        def tile(first):
            value = None
            for t in range(8):
                at = slots[slot][first + t]
                row = jnp.broadcast_to(table_ref[pl.ds(at, 1), :], (8, LANES))
                value = row if value is None else jnp.where(sublane == t, row, value)
            return value

        for first in range(0, SPAN, 16):
            both = jnp.concatenate([tile(first), tile(first + 8)], axis=0)
            rows_ref[first:first + 16, :] = both.astype(jnp.bfloat16)

    def begin():
        for slot in range(DEPTH):
            fetch(slot, slot).start()

    def run():
        fetch(0, 0).wait()
        gather(0, rows_refs[0])
        fetch(DEPTH, 0).start()

        @pl.loop(0, count // DEPTH)
        def _(j):
            for s in range(DEPTH):
                i = j * DEPTH + s
                slot = (s + 1) % DEPTH
                fetch(i + 1, slot).wait()
                gather(slot, rows_refs[(s + 1) % 2])
                work(i, rows_refs[s % 2])
                fetch(i + 1 + DEPTH, slot).start()

        for slot in range(DEPTH):
            fetch(count, slot).wait()

    return begin, run


def surface_kernel(
    x_ref, perm_ref, back_ref, pot_ref, surf_ref, out_ref,
    table_ref, packed_ref, even_ref, odd_ref, *rest
):
    slots, sems = rest[:-1], rest[-1]
    pieces, vecs, width = x_ref.shape
    points = table_ref.shape[0]
    per_group = pieces // GROUPS
    group_rows = points // GROUPS
    row, column = iota((LANES, GROUPS * LANES), 0), iota((LANES, GROUPS * LANES), 1)
    fold = jnp.where(
        (row // PAD == column // LANES) & (row % PAD == column % PAD), 1.0, 0.0
    ).astype(jnp.bfloat16)
    unit = jnp.where(iota((BLK, BLK), 0) == iota((BLK, BLK), 1), 1.0, 0.0).astype(jnp.bfloat16)
    lane_group = iota((BLK, LANES), 1) // PAD
    count = points // SPAN

    def folded(rows_ref):
        wide = jnp.concatenate([rows_ref[q * BLK:(q + 1) * BLK, :] for q in range(GROUPS)], axis=1)
        return dot_nt(fold, wide)

    def spread(rows, starts):
        for q in range(GROUPS):
            table_ref[pl.ds(pl.multiple_of(starts[q], BLK), BLK), :] = jnp.where(
                lane_group == q, rows, 0.0
            )

    def to_grid_and_back(i, rows_ref):
        values = folded(rows_ref).astype(jnp.bfloat16)
        projected = jnp.dot(values, surf_ref[...], preferred_element_type=jnp.float32)
        weighted = jnp.concatenate([
            projected[q * PAD:(q + 1) * PAD] * pot_ref[pl.ds(i * GROUPS + q, 1), :]
            for q in range(GROUPS)
        ], axis=0).astype(jnp.bfloat16)
        returned = dot_nt(surf_ref[...], weighted).astype(jnp.bfloat16).astype(jnp.float32)
        packed_ref[pl.ds(pl.multiple_of(i * BLK, BLK), BLK), :] = returned

    def to_basis(i, rows_ref):
        values = folded(rows_ref).astype(jnp.bfloat16)
        per_piece = out_ref.shape[2] // BLK
        for q in range(GROUPS):
            at = (q % per_piece) * BLK
            out_ref[i * (GROUPS // per_piece) + q // per_piece, :, at:at + BLK] = values[
                q * PAD:q * PAD + vecs
            ]

    begin, run = stream(perm_ref, count, slots, sems, table_ref, (even_ref, odd_ref), to_grid_and_back)
    begin()
    chunk = 512

    @pl.loop(0, per_group)
    def _(d):
        for c in range(0, width, chunk):
            parts = []
            for q in range(GROUPS):
                parts.append(x_ref[q * per_group + d, :, c:c + chunk].astype(jnp.float32))
                parts.append(jnp.zeros((PAD - vecs, chunk), jnp.float32))
            stacked = jnp.concatenate(parts, axis=0).astype(jnp.bfloat16)
            for h in range(0, chunk, BLK):
                rows = dot_nt(unit, stacked[:, h:h + BLK])
                spread(rows, [q * group_rows + d * width + c + h for q in range(GROUPS)])

    run()
    begin, run = stream(back_ref, count, slots, sems, table_ref, (even_ref, odd_ref), to_basis)
    begin()

    @pl.loop(0, count)
    def _(i):
        rows = packed_ref[pl.ds(pl.multiple_of(i * BLK, BLK), BLK), :]
        spread(rows, [i * SPAN + q * BLK for q in range(GROUPS)])

    run()


def surface_pass(arrived, perm, back, potential, surface, reps):
    pieces, vecs, width = arrived.shape
    points = perm.shape[0]
    return pl.pallas_call(
        surface_kernel,
        out_shape=jax.ShapeDtypeStruct((pieces * reps, vecs, width // reps), jnp.bfloat16),
        in_specs=[WHOLE] * 5,
        out_specs=WHOLE,
        scratch_shapes=[
            pltpu.VMEM((points, LANES), jnp.float32),
            pltpu.VMEM((points // GROUPS, LANES), jnp.float32),
            pltpu.VMEM((SPAN, LANES), jnp.bfloat16),
            pltpu.VMEM((SPAN, LANES), jnp.bfloat16),
        ] + [pltpu.SMEM((SPAN,), jnp.int32)] * DEPTH + [pltpu.SemaphoreType.DMA((DEPTH,))],
        compiler_params=pltpu.CompilerParams(vmem_limit_bytes=VMEM_LIMIT),
        cost_estimate=pl.CostEstimate(
            flops=4 * vecs * points * BLK, bytes_accessed=300_000_000, transcendentals=0
        ),
    )(arrived, perm, back, potential.reshape(-1, BLK), surface)


def source_kernel(vecs_ref, low_ref, high_ref, column_ref, weight_ref, out_ref, wide_ref):
    reps = out_ref.shape[0]
    edge = low_ref.shape[1]
    rows = vecs_ref.shape[1]
    blocks = rows // BLK
    piece_blocks = out_ref.shape[3] * reps // (blocks * BLK)
    wide_ref[:, 0:edge] = low_ref[...]
    wide_ref[:, edge + rows:] = high_ref[...]
    per_piece = 8
    per_rep = per_piece // reps

    @pl.loop(0, blocks // per_piece)
    def _(j):
        start = pl.multiple_of(j * per_piece * BLK, per_piece * BLK)
        wide_ref[:, pl.ds(edge + start, per_piece * BLK)] = vecs_ref[:, pl.ds(start, per_piece * BLK)]

    @pl.loop(0, blocks // per_piece)
    def _(j):
        for k in range(per_piece):
            a = j * per_piece + k
            total = None
            for m in range(COUPLINGS_PER_ROW):
                c = a * COUPLINGS_PER_ROW + m
                at = pl.multiple_of(column_ref[c] * BLK, BLK)
                term = wide_ref[:, pl.ds(at, BLK)].astype(jnp.float32) * weight_ref[c]
                total = term if total is None else total + term
            to = pl.ds(pl.multiple_of(j * per_rep * BLK, per_rep * BLK) + (k % per_rep) * BLK, BLK)
            here = pl.multiple_of(a * BLK, BLK)
            out_ref[k // per_rep, 0, :, to] = vecs_ref[:, pl.ds(here, BLK)]
            out_ref[k // per_rep, 1, :, to] = total.astype(jnp.bfloat16)


def source_of(basis_vecs, low, high, columns, weights, reps):
    vecs, rows = basis_vecs.shape
    return pl.pallas_call(
        source_kernel,
        out_shape=jax.ShapeDtypeStruct((reps, 2, vecs, rows // reps), jnp.bfloat16),
        in_specs=[WHOLE, WHOLE, WHOLE, SCALARS, SCALARS],
        out_specs=WHOLE,
        scratch_shapes=[pltpu.VMEM((vecs, rows + 2 * low.shape[1]), jnp.bfloat16)],
        compiler_params=pltpu.CompilerParams(vmem_limit_bytes=VMEM_LIMIT),
        cost_estimate=pl.CostEstimate(
            flops=6 * vecs * rows, bytes_accessed=12 * vecs * rows, transcendentals=0
        ),
    )(basis_vecs, low, high, columns, weights)


def image_kernel(moved_ref, pot_ref, kinetic_ref, precond_ref, image_ref, sums_ref, left_ref, right_ref):
    step = pl.program_id(0)
    reps, _, vecs, width = moved_ref.shape
    segment = pot_ref.shape[3]
    count = reps * vecs

    @pl.when(step == 0)
    def _():
        left_ref[...] = jnp.zeros_like(left_ref)
        right_ref[...] = jnp.zeros_like(right_ref)

    for s in range(width // segment):
        at = slice(s * segment, (s + 1) * segment)

        def joined(k):
            parts = [moved_ref[b, k, :, at].astype(jnp.float32) for b in range(reps)]
            return jnp.concatenate(parts, axis=0)

        vectors = joined(0)
        source = joined(1).astype(jnp.bfloat16)
        kin = jnp.concatenate([
            jnp.dot(source[:, h:h + BLK], kinetic_ref[...], preferred_element_type=jnp.float32)
            for h in range(0, segment, BLK)
        ], axis=1)
        pot = jnp.concatenate([pot_ref[b, s].astype(jnp.float32) for b in range(reps)], axis=0)
        image = (kin + pot).astype(jnp.bfloat16)
        image_ref[:, at] = image
        scale = precond_ref[0:1, at]
        square = scale * scale
        vectors_16 = vectors.astype(jnp.bfloat16)
        both = jnp.concatenate([image, vectors_16], axis=0)
        image_parts = three_parts(image.astype(jnp.float32) * square)
        vector_parts = three_parts(vectors * square)
        left_ref[...] += dot_nt(jnp.concatenate(image_parts, axis=0), both)
        right_ref[...] += dot_nt(jnp.concatenate([vectors_16] + vector_parts, axis=0), both)

    @pl.when(step == pl.num_programs(0) - 1)
    def _():
        left = left_ref[0:count] + left_ref[count:2 * count] + left_ref[2 * count:3 * count]
        right = (
            right_ref[count:2 * count] + right_ref[2 * count:3 * count] + right_ref[3 * count:4 * count]
        )
        sums_ref[0] = right_ref[0:count, 0:count]
        sums_ref[1] = left[:, 0:count]
        sums_ref[2] = left[:, count:2 * count]
        sums_ref[3] = right[:, count:2 * count]


def image_of(moved, pot, kinetic, precond, steps):
    reps, _, vecs, rows = moved.shape
    width = rows // steps
    count = reps * vecs
    pieces = pot.shape[1] // steps
    return pl.pallas_call(
        image_kernel,
        grid=(steps,),
        out_shape=(
            jax.ShapeDtypeStruct((count, rows), jnp.bfloat16),
            jax.ShapeDtypeStruct((4, count, count), jnp.float32),
        ),
        in_specs=[
            pl.BlockSpec((reps, 2, vecs, width), lambda i: (0, 0, 0, i)),
            pl.BlockSpec((reps, pieces, vecs, pot.shape[3]), lambda i: (0, i, 0, 0)),
            pl.BlockSpec((BLK, BLK), lambda i: (0, 0)),
            pl.BlockSpec((1, width), lambda i: (0, i)),
        ],
        out_specs=(
            pl.BlockSpec((count, width), lambda i: (0, i)),
            pl.BlockSpec((4, count, count), lambda i: (0, 0, 0)),
        ),
        scratch_shapes=[
            pltpu.VMEM((3 * count, 2 * count), jnp.float32),
            pltpu.VMEM((4 * count, 2 * count), jnp.float32),
        ],
        compiler_params=pltpu.CompilerParams(vmem_limit_bytes=VMEM_LIMIT),
        cost_estimate=pl.CostEstimate(
            flops=28 * count * count * rows, bytes_accessed=8 * count * rows, transcendentals=0
        ),
    )(moved, pot, kinetic, precond)


def solve_kernel(full_rows, sums_ref, moved_ref, image_ref, precond_ref, out_ref, rayleigh_ref, mix_ref):
    count = image_ref.shape[0]
    reps, _, vecs, width = moved_ref.shape

    @pl.when(pl.program_id(0) == 0)
    def _():
        rayleigh = sums_ref[0] / full_rows
        rayleigh_ref[...] = rayleigh
        turned = rayleigh.T
        cross = dot_exact(sums_ref[2], rayleigh)
        last = dot_exact(turned, dot_exact(sums_ref[3], rayleigh))
        gram = (sums_ref[1] - cross - cross.T + last) / full_rows
        pad = jnp.zeros((count, LANES - count), jnp.float32)
        row, column = iota((count, LANES), 0), iota((count, LANES), 1)
        left = jnp.concatenate([gram, pad], axis=1)
        right = jnp.where(row == column, 1.0, 0.0)
        for j in range(count):
            pivot_left, pivot_right = left[j:j + 1, :], right[j:j + 1, :]
            ratio = left[:, j:j + 1] / pivot_left[:, j:j + 1]
            ratio = jnp.where(row[:, 0:1] > j, ratio, 0.0)
            left = left - ratio * pivot_left
            right = right - ratio * pivot_right
        diagonal = jnp.sum(jnp.where(row == column, left, 0.0), axis=1, keepdims=True)
        inverse = (right * lax.rsqrt(diagonal))[:, 0:count]
        parts = three_parts(inverse) + three_parts(-dot_exact(inverse, turned))
        for k in range(3):
            mix_ref[k * count:(k + 1) * count, 0:count] = parts[k]
            mix_ref[k * count:(k + 1) * count, count:2 * count] = parts[3 + k]

    vectors = jnp.concatenate(
        [moved_ref[b, 0].astype(jnp.float32) for b in range(reps)], axis=0
    ).astype(jnp.bfloat16)
    both = jnp.concatenate([image_ref[...], vectors], axis=0)
    chunk = 512
    for s in range(0, width, chunk):
        parts = jnp.dot(mix_ref[...], both[:, s:s + chunk], preferred_element_type=jnp.float32)
        total = (parts[2 * count:] + parts[count:2 * count]) + parts[0:count]
        out_ref[:, s:s + chunk] = total * precond_ref[0:1, s:s + chunk]


def solved_of(sums, moved, image, precond, full_rows, steps):
    reps, _, vecs, rows = moved.shape
    width = rows // steps
    count = reps * vecs
    return pl.pallas_call(
        functools.partial(solve_kernel, full_rows),
        grid=(steps,),
        out_shape=(
            jax.ShapeDtypeStruct((count, rows), jnp.float32),
            jax.ShapeDtypeStruct((count, count), jnp.float32),
        ),
        in_specs=[
            pl.BlockSpec((4, count, count), lambda i: (0, 0, 0)),
            pl.BlockSpec((reps, 1, vecs, width), lambda i: (0, 0, 0, i)),
            pl.BlockSpec((count, width), lambda i: (0, i)),
            pl.BlockSpec((1, width), lambda i: (0, i)),
        ],
        out_specs=(
            pl.BlockSpec((count, width), lambda i: (0, i)),
            pl.BlockSpec((count, count), lambda i: (0, 0)),
        ),
        scratch_shapes=[pltpu.VMEM((3 * count, 2 * count), jnp.bfloat16)],
        compiler_params=pltpu.CompilerParams(vmem_limit_bytes=VMEM_LIMIT),
        cost_estimate=pl.CostEstimate(
            flops=12 * count * count * rows, bytes_accessed=8 * count * rows, transcendentals=0
        ),
    )(sums, moved, image, precond)


def sum_over_devices(x):
    def turned(axis, stride, shift):
        size = lax.axis_size(axis)
        pairs = []
        for i in range(size):
            digit = (i // stride) % 4
            pairs.append((i, i + ((digit + shift) % 4 - digit) * stride))
        return lax.ppermute(x, axis, pairs)

    x = x + lax.ppermute(x, "row", [(i, i ^ 1) for i in range(lax.axis_size("row"))])
    for axis, stride in (("rep", 1), ("row", 8), ("row", 2)):
        up, down, across = (turned(axis, stride, shift) for shift in (1, 3, 2))
        x = (x + across) + (up + down)
    return x


def body(
    basis_vecs, potential, surface, grid_perm, kinetic, couplings, coupling_coefficient, precond
):
    vecs, rows = basis_vecs.shape
    pieces = lax.axis_size("row")
    reps = lax.axis_size("rep")
    width = rows // pieces
    blocks = rows // BLK
    edge = HB * BLK
    forward = [(i, i + 1) for i in range(pieces - 1)]
    backward = [(i + 1, i) for i in range(pieces - 1)]
    low = lax.ppermute(basis_vecs[:, rows - edge:], "row", forward)
    high = lax.ppermute(basis_vecs[:, :edge], "row", backward)
    by_piece = basis_vecs.reshape(vecs, pieces, width).transpose(1, 0, 2)
    arrived = lax.all_to_all(by_piece, "row", split_axis=0, concat_axis=0, tiled=True)
    columns = couplings[:, 1] - (lax.axis_index("row") * blocks - HB)
    by_rep = source_of(basis_vecs, low, high, columns, coupling_coefficient, reps)
    moved = lax.all_to_all(by_rep, "rep", split_axis=0, concat_axis=0, tiled=True)
    back = inverse_of(grid_perm, reps)
    restored = surface_pass(arrived, grid_perm, back, potential, surface, reps)
    pot = lax.all_to_all(restored, ("rep", "row"), split_axis=0, concat_axis=0, tiled=True)
    pot = pot.reshape(reps, pieces, vecs, width // reps)
    scale = precond.reshape(1, -1)
    image, sums = image_of(moved, pot, kinetic, scale, 8)
    count = reps * vecs
    sums = sum_over_devices(sums.reshape(4 * count, count)).reshape(4, count, count)
    solved, rayleigh = solved_of(sums, moved, image, scale, float(rows * pieces), 8)
    return (solved.reshape(count, 1, 1, -1), rayleigh)


def solution(mesh):
    in_specs = (
        P("rep", "row"),
        P("row"),
        P(),
        P("row"),
        P(),
        P("row", None),
        P("row"),
        P("row", "rep", None),
    )
    out_specs = (P(None, "row", "rep", None), P())
    return jax.shard_map(body, mesh=mesh, in_specs=in_specs, out_specs=out_specs, check_vma=False)
```

time: 833 us -> 363 us (0.44)
  local copies, waits for them, and re-layouts: 505 us -> 20.5 us
  Pallas kernels: 0 us -> 202 us
  blocking collectives: 128 us -> 50.9 us
  waiting for transfers between devices: 93.1 us -> 54.4 us
  other arithmetic: 40.5 us -> 2.38 us
  matrix products: 25.9 us -> 0 us
    gather x3 -> x0, local copies, waits for them, and re-layouts: 243 us -> none  [the longest x2 238 us: grid_work(): ordered = jnp.take(target_columns, grid_perm, axis=1)]
    pallas_call x0 -> x5, Pallas kernels: none -> 202 us  [the longest x1 133 us: surface_pass(): pl.pallas_call(surface_kernel, out_shape=jax.ShapeDtypeStruct((pieces * r...]
    scatter x1 -> x0, local copies, waits for them, and re-layouts: 172 us -> none  [grid_work(): return jnp.zeros_like(returned).at[:, grid_perm].set(returned)]
    psum x2 -> x0, blocking collectives: 128 us -> none  [the longest x1 64 us: body(): lower_factor = jnp.linalg.cholesky(lax.psum(local_gram, ('rep', 'row')))]
    all_to_all x4 -> x2, waiting for transfers between devices: 93.1 us -> 0.01 us  [the longest x1 0.01 us: body(): lax.all_to_all(by_piece, 'row', split_axis=0, concat_axis=0, tiled=True)]
    ppermute x2 -> x12, waiting for transfers between devices: 0.01 us -> 54.4 us  [the longest x1 30.6 us: body(): high = lax.ppermute(basis_vecs[:, :edge], 'row', backward)]
    all_to_all x0 -> x1, blocking collectives: none -> 50.9 us  [body(): lax.all_to_all(restored, ('rep', 'row'), split_axis=0, concat_axis=0, til...]
    all_to_all x3 -> x0, local copies, waits for them, and re-layouts: 29 us -> none  [the longest x2 15 us: body(): lax.all_to_all(basis_vecs, 'row', split_axis=1, concat_axis=1, tiled=True)]
  transfers between devices with their start and end apart: 6 -> 14, of which waited for: 3 -> 9; matrix products, arithmetic and copies ran while one was open for 8% -> 2% of each run, Pallas kernels for 0% -> 47%
where the time goes in v1:
time: 363 us; the launch traced here: 358 us
  Pallas kernels  202 us (56%)
  waiting for transfers between devices  54.4 us (15%)
  blocking collectives  50.9 us (14%)
  starting transfers between devices  27.1 us (7%)
  local copies, waits for them, and re-layouts  20.5 us (6%)
    pallas_call x1, Pallas kernels, surface_pass(): pl.pallas_call(surface_kernel, out_shape=jax.ShapeDtypeStruct((pieces * r...  133 us
    all_to_all x1, blocking collectives, body(): lax.all_to_all(restored, ('rep', 'row'), split_axis=0, concat_axis=0, til...  50.9 us
    ppermute x1, waiting for transfers between devices, body(): high = lax.ppermute(basis_vecs[:, :edge], 'row', backward)  30.6 us
    pallas_call x1, Pallas kernels, inverse_of(): pl.pallas_call(functools.partial(inverse_kernel, reps), out_shape=jax.Sha...  28.8 us
    ppermute x9, waiting for transfers between devices, turned(): return lax.ppermute(x, axis, pairs)  22.5 us
    pallas_call x1, Pallas kernels, solved_of(): pl.pallas_call(functools.partial(solve_kernel, full_rows), grid=(steps,),...  17.8 us
    pallas_call x1, Pallas kernels, image_of(): pl.pallas_call(image_kernel, grid=(steps,), out_shape=(jax.ShapeDtypeStru...  15.8 us
    unnamed x12, local copies, waits for them, and re-layouts  13.2 us
  transfers between devices with their start and end apart: 14, of which 9 were waited for; matrix products, arithmetic and copies ran while one was open for 2% of the time, Pallas kernels for 47%

profile of v1, /device:TPU:1, one launch (start us, length us, event | category | flops | bytes accessed | tf_op | source)
XLA Modules:
  0.0 358.3 jit_solution(17101607440756114676)
XLA Ops:
  0.6 4.0 %copy.16 = bf16[3,32,8,2048]{3,2,0,1:T(8,128)(2,1)} copy(bf16[3,32,8,2048]{3,2,1,0:T(8,128)(2,1)} %bitcast.15) | data formatting | bytes 6291456 | tf_op jit(solution)/shard_map/reshape | solution.py:458
  4.6 0.0 copy-start.4
  4.6 8.7 %all-to-all-start.1 = ((bf16[32,24,2048]{2,1,0:T(8,128)(2,1)}), bf16[32,24,2048]{2,1,0:T(8,128)(2,1)S(1)}, u32[]{:S(2)}, u32[]{:S(2)}) async-start(bf16[32,24,2048]{2,1,0:T(8,128)(2,1)} %bitcast.16), calls=%async_computation.1 | async-start | bytes 6291456 | tf_op jit(solution)/shard_map/all_to_all | solution.py:459
  13.3 0.8 fusion
  14.1 2.1 collective-permute-start.1
  16.2 3.4 collective-permute-start
  19.6 0.0 copy-done.4
  19.7 0.6 subtract_reduce_fusion.column_ref
  20.3 30.6 %collective-permute-done.1.high_ref = bf16[24,512]{1,0:T(8,128)(2,1)S(1)} collective-permute-done((bf16[24,512]{1,0:T(8,128)(2,1)S(1)}, bf16[24,512]{1,0:T(8,128)(2,1)S(1)}, u32[]{:S(2)}, u32[]{:S(2)}) %collective-permute-start.1) | collective-permute-done | bytes 24608 | tf_op jit(solution)/shard_map/ppermute | solution.py:457
  50.9 0.0 copy-start.2
  50.9 0.0 collective-permute-done.low_ref
  50.9 0.6 copy-done.2
  51.5 0.0 copy-start.3
  51.5 0.6 copy-done.3
  52.1 7.4 %shard_map.95 = bf16[4,2,24,16384]{3,2,1,0:T(8,128)(2,1)} custom-call(bf16[24,65536]{1,0:T(8,128)(2,1)} %vecs_ref.1, bf16[24,512]{1,0:T(8,128)(2,1)} %copy-done.3, bf16[24,512]{1,0:T(8,128)(2,1)} %copy-done.2, s32[768]{0:T(1024)} %subtract_reduce_fusion.column_ref, f32[768]{0:T(1024)} %weight_ref.1), custom_call_target="tpu_custom_call" | custom-call | flops 9437184 | bytes 18874368 | tf_op jit(solution)/shard_map/pallas_call | solution.py:266
  59.5 0.0 copy-start.1
  59.5 0.0 all-to-all-done.1.x_ref
  59.5 0.0 copy-start
  59.5 1.7 copy-done
  61.2 5.3 %all-to-all-start = ((bf16[4,2,24,16384]{3,2,1,0:T(8,128)(2,1)}), bf16[4,2,24,16384]{3,2,1,0:T(8,128)(2,1)}, u32[]{:S(2)}, u32[]{:S(2)}) async-start(bf16[4,2,24,16384]{3,2,1,0:T(8,128)(2,1)} %shard_map.95), calls=%async_computation | async-start | bytes 12582912 | tf_op jit(solution)/shard_map/all_to_all | solution.py:462
  66.4 1.8 reshape.36.pot_ref
  68.2 0.0 copy-done.1
  68.2 0.8 reshape.34.perm_ref
  69.0 28.8 %shard_map.96 = s32[256,256]{1,0:T(8,128)} custom-call(s32[256,256]{1,0:T(8,128)} %reshape.34.perm_ref), custom_call_target="tpu_custom_call" | custom-call | flops 17179869184 | bytes 524288 | tf_op jit(solution)/shard_map/pallas_call | solution.py:79
  97.8 1.8 copy.14
  99.6 132.6 %shard_map.97 = bf16[128,24,512]{2,1,0:T(8,128)(2,1)} custom-call(bf16[32,24,2048]{2,1,0:T(8,128)(2,1)} %copy-done, s32[65536]{0:T(1024)} %perm_ref.1, s32[65536]{0:T(1024)} %bitcast.19, f32[256,256]{1,0:T(8,128)} %reshape.36.pot_ref, bf16[256,256]{1,0:T(8,128)(2,1)} %surf_ref.1), custom_call_target="tpu_custom_call" | custom-call | flops 1610612736 | bytes 300000000 | tf_op jit(solution)/shard_map/pallas_call | solution.py:214
  232.3 0.0 all-to-all-done.moved_ref
  232.3 50.9 %all_to_all.15 = bf16[128,24,512]{2,1,0:T(8,128)(2,1)} all-to-all(bf16[128,24,512]{2,1,0:T(8,128)(2,1)} %shard_map.97), channel_id=1, replica_groups=mesh['rep'=4,'row'=32] {'rep','row'}, dimensions={0} | all-to-all | bytes 6291456 | tf_op jit(solution)/shard_map/all_to_all | solution.py:465
  283.1 15.8 %shard_map.98 = (bf16[96,16384]{1,0:T(8,128)(2,1)}, f32[4,96,96]{2,1,0:T(8,128)}) custom-call(bf16[4,2,24,16384]{3,2,1,0:T(8,128)(2,1)} %all-to-all-done.moved_ref, bf16[4,32,24,512]{3,2,1,0:T(8,128)(2,1)} %bitcast.18, bf16[256,256]{1,0:T(8,128)(2,1)} %kinetic_ref.1, f32[1,16384]{1,0:T(1,128)} %bitcast.23), custom_call_target="tpu_custom_call" | custom-call | flops 4227858432 | bytes 12582912 | tf_op jit(solution)/shard_map/pallas_call | solution.py:332
  298.9 0.8 collective-permute-start.2
  299.7 1.3 collective-permute-done.2
  301.0 1.0 bitcast_add_fusion
  302.0 0.4 collective-permute-start.5
  302.4 1.1 collective-permute-start.4
  303.5 0.6 collective-permute-start.3
  304.1 4.0 %collective-permute-done.5 = f32[384,96]{1,0:T(8,128)S(1)} collective-permute-done((f32[384,96]{1,0:T(8,128)S(1)}, f32[384,96]{1,0:T(8,128)S(1)}, u32[]{:S(2)}, u32[]{:S(2)}) %collective-permute-start.5) | collective-permute-done | bytes 147488 | tf_op jit(solution)/shard_map/ppermute | solution.py:436
  308.1 1.9 collective-permute-done.4
  310.0 3.0 collective-permute-done.3
  313.1 1.4 collective-permute-start.8
  314.5 0.1 collective-permute-start.7
  314.6 1.2 collective-permute-start.6
  315.8 1.9 collective-permute-done.8
  317.7 5.6 %collective-permute-done.7 = f32[384,96]{1,0:T(8,128)S(1)} collective-permute-done((f32[384,96]{1,0:T(8,128)S(1)}, f32[384,96]{1,0:T(8,128)S(1)}, u32[]{:S(2)}, u32[]{:S(2)}) %collective-permute-start.7) | collective-permute-done | bytes 147488 | tf_op jit(solution)/shard_map/ppermute | solution.py:436
  323.3 0.0 collective-permute-done.6
  323.3 0.1 collective-permute-start.11
  323.4 1.5 collective-permute-start.10
  324.9 0.4 collective-permute-start.9
  325.2 2.7 collective-permute-done.11
  327.9 3.4 collective-permute-done.10
  331.3 0.0 collective-permute-done.9
  331.3 0.7 add_add_fusion
  332.1 17.8 %shard_map.99 = (f32[96,16384]{1,0:T(8,128)}, f32[96,96]{1,0:T(8,128)}) custom-call(f32[4,96,96]{2,1,0:T(8,128)} %bitcast.20, bf16[4,2,24,16384]{3,2,1,0:T(8,128)(2,1)} %all-to-all-done.moved_ref, bf16[96,16384]{1,0:T(8,128)(2,1)} %get-tuple-element.7.image_ref, f32[1,16384]{1,0:T(1,128)} %bitcast.24), custom_call_target="tpu_custom_call" | custom-call | flops 1811939328 | bytes 12582912 | tf_op jit(solution)/shard_map/pallas_call | solution.py:404
  349.8 8.5 %copy.12 = f32[96,1,1,16384]{3,2,1,0:T(1,128)} copy(f32[96,1,1,16384]{3,0,2,1:T(8,128)} %bitcast.17) | data formatting | bytes 12582912
  (2 shorter events, 0.1 us)
Async XLA Ops:
  4.6 15.1 %copy-start.4 = (s32[768,2]{0,1:T(2,128)S(1)}, s32[768,2]{0,1:T(2,128)}, u32[]{:S(2)}) copy-start(s32[768,2]{0,1:T(2,128)} %param.13) | copy-start | bytes 18436
  4.6 54.9 %all-to-all-start.1 = ((bf16[32,24,2048]{2,1,0:T(8,128)(2,1)}), bf16[32,24,2048]{2,1,0:T(8,128)(2,1)S(1)}, u32[]{:S(2)}, u32[]{:S(2)}) async-start(bf16[32,24,2048]{2,1,0:T(8,128)(2,1)} %bitcast.16), calls=%async_computation.1 | async-start | bytes 6291456 | tf_op jit(solution)/shard_map/all_to_all | solution.py:459
  14.1 36.8 %collective-permute-start.1 = (bf16[24,512]{1,0:T(8,128)(2,1)S(1)}, bf16[24,512]{1,0:T(8,128)(2,1)S(1)}, u32[]{:S(2)}, u32[]{:S(2)}) collective-permute-start(bf16[24,512]{1,0:T(8,128)(2,1)S(1)} %get-tuple-element.14), channel_id=1, source_target_pairs={{1,0},{2,1},{3,2},{4,3},{5,4},{6,5},{7,6},{8,7},{9,8},{10,9},{11,1... | collective-permute-start | bytes 73736 | tf_op jit(solution)/shard_map/ppermute | solution.py:457
  16.2 34.7 %collective-permute-start = (bf16[24,512]{1,0:T(8,128)(2,1)S(1)}, bf16[24,512]{1,0:T(8,128)(2,1)S(1)}, u32[]{:S(2)}, u32[]{:S(2)}) collective-permute-start(bf16[24,512]{1,0:T(8,128)(2,1)S(1)} %get-tuple-element.15), channel_id=1, source_target_pairs={{0,1},{1,2},{2,3},{3,4},{4,5},{5,6},{6,7},{7,8},{8,9},{9,10},{10,1... | collective-permute-start | bytes 73736 | tf_op jit(solution)/shard_map/ppermute | solution.py:456
  50.9 0.6 copy-start.2
  51.5 0.6 copy-start.3
  59.5 8.7 %copy-start.1 = (s32[65536]{0:T(1024)S(1)}, s32[65536]{0:T(1024)}, u32[]{:S(2)}) copy-start(s32[65536]{0:T(1024)} %perm_ref.1) | copy-start | bytes 786436
  59.5 1.7 copy-start
  61.2 171.1 %all-to-all-start = ((bf16[4,2,24,16384]{3,2,1,0:T(8,128)(2,1)}), bf16[4,2,24,16384]{3,2,1,0:T(8,128)(2,1)}, u32[]{:S(2)}, u32[]{:S(2)}) async-start(bf16[4,2,24,16384]{3,2,1,0:T(8,128)(2,1)} %shard_map.95), calls=%async_computation | async-start | bytes 12582912 | tf_op jit(solution)/shard_map/all_to_all | solution.py:462
  298.9 2.1 collective-permute-start.2
  302.0 6.2 %collective-permute-start.5 = (f32[384,96]{1,0:T(8,128)S(1)}, f32[384,96]{1,0:T(8,128)S(1)}, u32[]{:S(2)}, u32[]{:S(2)}) collective-permute-start(f32[384,96]{1,0:T(8,128)S(1)} %bitcast_add_fusion), channel_id=1, source_target_pairs={{0,96},{32,0},{64,32},{96,64},{1,97},{33,1},{65,33},{97,65},{2,98}... | collective-permute-start | bytes 442376 | tf_op jit(solution)/shard_map/ppermute | solution.py:436
  302.4 7.6 %collective-permute-start.4 = (f32[384,96]{1,0:T(8,128)S(1)}, f32[384,96]{1,0:T(8,128)S(1)}, u32[]{:S(2)}, u32[]{:S(2)}) collective-permute-start(f32[384,96]{1,0:T(8,128)S(1)} %bitcast_add_fusion), channel_id=1, source_target_pairs={{0,32},{32,64},{64,96},{96,0},{1,33},{33,65},{65,97},{97,1},{2,34}... | collective-permute-start | bytes 442376 | tf_op jit(solution)/shard_map/ppermute | solution.py:436
  303.5 9.6 %collective-permute-start.3 = (f32[384,96]{1,0:T(8,128)S(1)}, f32[384,96]{1,0:T(8,128)S(1)}, u32[]{:S(2)}, u32[]{:S(2)}) collective-permute-start(f32[384,96]{1,0:T(8,128)S(1)} %bitcast_add_fusion), channel_id=1, source_target_pairs={{0,64},{32,96},{64,0},{96,32},{1,65},{33,97},{65,1},{97,33},{2,66}... | collective-permute-start | bytes 442376 | tf_op jit(solution)/shard_map/ppermute | solution.py:436
  313.1 4.6 %collective-permute-start.8 = (f32[384,96]{1,0:T(8,128)S(1)}, f32[384,96]{1,0:T(8,128)S(1)}, u32[]{:S(2)}, u32[]{:S(2)}) collective-permute-start(f32[384,96]{1,0:T(8,128)S(1)} %add_add_fusion.2), channel_id=1, source_target_pairs={{0,24},{1,25},{2,26},{3,27},{4,28},{5,29},{6,30},{7,31},{8,0},{9,1... | collective-permute-start | bytes 442376 | tf_op jit(solution)/shard_map/ppermute | solution.py:436
  314.5 8.8 %collective-permute-start.7 = (f32[384,96]{1,0:T(8,128)S(1)}, f32[384,96]{1,0:T(8,128)S(1)}, u32[]{:S(2)}, u32[]{:S(2)}) collective-permute-start(f32[384,96]{1,0:T(8,128)S(1)} %add_add_fusion.2), channel_id=1, source_target_pairs={{0,8},{1,9},{2,10},{3,11},{4,12},{5,13},{6,14},{7,15},{8,16},{9,17... | collective-permute-start | bytes 442376 | tf_op jit(solution)/shard_map/ppermute | solution.py:436
  314.6 8.7 %collective-permute-start.6 = (f32[384,96]{1,0:T(8,128)S(1)}, f32[384,96]{1,0:T(8,128)S(1)}, u32[]{:S(2)}, u32[]{:S(2)}) collective-permute-start(f32[384,96]{1,0:T(8,128)S(1)} %add_add_fusion.2), channel_id=1, source_target_pairs={{0,16},{1,17},{2,18},{3,19},{4,20},{5,21},{6,22},{7,23},{8,24},{9,... | collective-permute-start | bytes 442376 | tf_op jit(solution)/shard_map/ppermute | solution.py:436
  323.3 4.6 %collective-permute-start.11 = (f32[384,96]{1,0:T(8,128)S(1)}, f32[384,96]{1,0:T(8,128)S(1)}, u32[]{:S(2)}, u32[]{:S(2)}) collective-permute-start(f32[384,96]{1,0:T(8,128)S(1)} %add_add_fusion.1), channel_id=1, source_target_pairs={{0,6},{1,7},{2,0},{3,1},{4,2},{5,3},{6,4},{7,5},{8,14},{9,15},{10,... | collective-permute-start | bytes 442376 | tf_op jit(solution)/shard_map/ppermute | solution.py:436
  323.4 7.9 %collective-permute-start.10 = (f32[384,96]{1,0:T(8,128)S(1)}, f32[384,96]{1,0:T(8,128)S(1)}, u32[]{:S(2)}, u32[]{:S(2)}) collective-permute-start(f32[384,96]{1,0:T(8,128)S(1)} %add_add_fusion.1), channel_id=1, source_target_pairs={{0,2},{1,3},{2,4},{3,5},{4,6},{5,7},{6,0},{7,1},{8,10},{9,11},{10,... | collective-permute-start | bytes 442376 | tf_op jit(solution)/shard_map/ppermute | solution.py:436
  324.9 6.5 %collective-permute-start.9 = (f32[384,96]{1,0:T(8,128)S(1)}, f32[384,96]{1,0:T(8,128)S(1)}, u32[]{:S(2)}, u32[]{:S(2)}) collective-permute-start(f32[384,96]{1,0:T(8,128)S(1)} %add_add_fusion.1), channel_id=1, source_target_pairs={{0,4},{1,5},{2,6},{3,7},{4,0},{5,1},{6,2},{7,3},{8,12},{9,13},{10,... | collective-permute-start | bytes 442376 | tf_op jit(solution)/shard_map/ppermute | solution.py:436

commit v2 on v1

--- a/solution.py
+++ b/solution.py
@@ -14,7 +14,6 @@
 GROUPS = 4
 LANES = 128
 SPAN = GROUPS * BLK
-DEPTH = 4
 VMEM_LIMIT = 60 * 2**20
 NT = (((1,), (1,)), ((), ()))
 WHOLE = pl.BlockSpec(memory_space=pltpu.VMEM)
@@ -41,7 +40,7 @@
     return [high, middle, low]
 
 
-def inverse_kernel(reps, perm_ref, out_ref, acc_ref):
+def inverse_kernel(reps, perm_ref, out_ref, back_ref, acc_ref):
     blocks = perm_ref.shape[0]
     acc_ref[...] = jnp.zeros_like(acc_ref)
     step = 4
@@ -65,80 +64,91 @@
                 right.append(jnp.where(rows == low[at:at + 1, :], 1.0, 0.0).astype(jnp.bfloat16))
             acc_ref[...] += dot_nt(jnp.concatenate(left, axis=1), jnp.concatenate(right, axis=1))
 
+    acc_ref[0:BLK, :] = acc_ref[0:BLK, :] * 256.0 + acc_ref[BLK:2 * BLK, :]
     per_rep = 8 // reps
     for d in range(blocks // 8):
-        tile = acc_ref[d * 8:(d + 1) * 8, :] * 256.0 + acc_ref[BLK + d * 8:BLK + (d + 1) * 8, :]
-        tile = tile.astype(jnp.int32)
+        tile = acc_ref[d * 8:(d + 1) * 8, :]
         for b in range(reps):
-            start = b * (blocks // reps) + d * per_rep
-            out_ref[start:start + per_rep, :] = tile[b * per_rep:(b + 1) * per_rep, :]
-
-
-def inverse_of(perm, reps):
+            start = BLK + b * (blocks // reps) + d * per_rep
+            acc_ref[start:start + per_rep, :] = tile[b * per_rep:(b + 1) * per_rep, :]
+    half = blocks // 2
+    for k in range(2):
+        out_ref[k * BLK:(k + 1) * BLK, :] = perm_ref[k * half:(k + 1) * half, :].T
+        back_ref[k * BLK:(k + 1) * BLK, :] = acc_ref[
+            BLK + k * half:BLK + (k + 1) * half, :
+        ].T.astype(jnp.int32)
+
+
+def index_streams(perm, reps):
     blocks = perm.shape[0] // BLK
-    return pl.pallas_call(
+    streams = jax.ShapeDtypeStruct((2 * BLK, blocks // 2), jnp.int32)
+    out, back = pl.pallas_call(
         functools.partial(inverse_kernel, reps),
-        out_shape=jax.ShapeDtypeStruct((blocks, BLK), jnp.int32),
+        out_shape=(streams, streams),
         in_specs=[WHOLE],
-        out_specs=WHOLE,
+        out_specs=(WHOLE, WHOLE),
         scratch_shapes=[pltpu.VMEM((2 * BLK, BLK), jnp.float32)],
         compiler_params=pltpu.CompilerParams(vmem_limit_bytes=VMEM_LIMIT),
         cost_estimate=pl.CostEstimate(
             flops=4 * BLK * BLK * blocks * BLK, bytes_accessed=8 * blocks * BLK, transcendentals=0
         ),
-    )(perm.reshape(blocks, BLK)).reshape(-1)
-
-
-def stream(index_ref, count, slots, sems, table_ref, rows_refs, work):
+    )(perm.reshape(blocks, BLK))
+    return out.reshape(-1), back.reshape(-1)
+
+
+def stream(index_ref, streams, sem, table_ref, rows_refs, work):
     sublane = iota((8, LANES), 0)
-
-    def fetch(i, slot):
-        start = pl.multiple_of(jnp.minimum(i, count - 1) * SPAN, SPAN)
-        return pltpu.make_async_copy(index_ref.at[pl.ds(start, SPAN)], slots[slot], sems.at[slot])
-
-    def gather(slot, rows_ref):
-        def tile(first):
+    size = streams[0].shape[0]
+    half = size // 8
+    count = half // 2
+    copies = [
+        pltpu.make_async_copy(index_ref.at[pl.ds(k * size, size)], held, sem.at[k])
+        for k, held in enumerate(streams)
+    ]
+
+    def gather(i, rows_ref):
+        def tile(held, places):
             value = None
             for t in range(8):
-                at = slots[slot][first + t]
-                row = jnp.broadcast_to(table_ref[pl.ds(at, 1), :], (8, LANES))
+                row = jnp.broadcast_to(table_ref[pl.ds(held[places[t]], 1), :], (8, LANES))
                 value = row if value is None else jnp.where(sublane == t, row, value)
             return value
 
-        for first in range(0, SPAN, 16):
-            both = jnp.concatenate([tile(first), tile(first + 8)], axis=0)
-            rows_ref[first:first + 16, :] = both.astype(jnp.bfloat16)
+        for part in range(2):
+            places = [t * half + 2 * i + part for t in range(8)]
+            for k in range(0, len(streams), 2):
+                both = jnp.concatenate([tile(held, places) for held in streams[k:k + 2]], axis=0)
+                first = part * len(streams) * 8 + k * 8
+                rows_ref[first:first + 16, :] = both.astype(jnp.bfloat16)
 
     def begin():
-        for slot in range(DEPTH):
-            fetch(slot, slot).start()
+        for copy in copies:
+            copy.start()
 
     def run():
-        fetch(0, 0).wait()
+        for copy in copies:
+            copy.wait()
         gather(0, rows_refs[0])
-        fetch(DEPTH, 0).start()
-
-        @pl.loop(0, count // DEPTH)
+
+        @pl.loop(0, count // 2)
         def _(j):
-            for s in range(DEPTH):
-                i = j * DEPTH + s
-                slot = (s + 1) % DEPTH
-                fetch(i + 1, slot).wait()
-                gather(slot, rows_refs[(s + 1) % 2])
+            for s in range(2):
+                i = j * 2 + s
+                gather(jnp.minimum(i + 1, count - 1), rows_refs[(s + 1) % 2])
                 work(i, rows_refs[s % 2])
-                fetch(i + 1 + DEPTH, slot).start()
-
-        for slot in range(DEPTH):
-            fetch(count, slot).wait()
 
     return begin, run
+
+
+def blocks_of(i, blocks):
+    return [2 * i, 2 * i + blocks // 2, 2 * i + 1, 2 * i + 1 + blocks // 2]
 
 
 def surface_kernel(
     x_ref, perm_ref, back_ref, pot_ref, surf_ref, out_ref,
     table_ref, packed_ref, even_ref, odd_ref, *rest
 ):
-    slots, sems = rest[:-1], rest[-1]
+    streams, sem = rest[:-1], rest[-1]
     pieces, vecs, width = x_ref.shape
     points = table_ref.shape[0]
     per_group = pieces // GROUPS
@@ -150,6 +160,7 @@
     unit = jnp.where(iota((BLK, BLK), 0) == iota((BLK, BLK), 1), 1.0, 0.0).astype(jnp.bfloat16)
     lane_group = iota((BLK, LANES), 1) // PAD
     count = points // SPAN
+    blocks = points // BLK
 
     def folded(rows_ref):
         wide = jnp.concatenate([rows_ref[q * BLK:(q + 1) * BLK, :] for q in range(GROUPS)], axis=1)
@@ -165,8 +176,8 @@
         values = folded(rows_ref).astype(jnp.bfloat16)
         projected = jnp.dot(values, surf_ref[...], preferred_element_type=jnp.float32)
         weighted = jnp.concatenate([
-            projected[q * PAD:(q + 1) * PAD] * pot_ref[pl.ds(i * GROUPS + q, 1), :]
-            for q in range(GROUPS)
+            projected[q * PAD:(q + 1) * PAD] * pot_ref[pl.ds(block, 1), :]
+            for q, block in enumerate(blocks_of(i, blocks))
         ], axis=0).astype(jnp.bfloat16)
         returned = dot_nt(surf_ref[...], weighted).astype(jnp.bfloat16).astype(jnp.float32)
         packed_ref[pl.ds(pl.multiple_of(i * BLK, BLK), BLK), :] = returned
@@ -175,12 +186,12 @@
         values = folded(rows_ref).astype(jnp.bfloat16)
         per_piece = out_ref.shape[2] // BLK
         for q in range(GROUPS):
-            at = (q % per_piece) * BLK
-            out_ref[i * (GROUPS // per_piece) + q // per_piece, :, at:at + BLK] = values[
+            at = (q // per_piece) * BLK
+            out_ref[i + (q % per_piece) * (out_ref.shape[0] // per_piece), :, at:at + BLK] = values[
                 q * PAD:q * PAD + vecs
             ]
 
-    begin, run = stream(perm_ref, count, slots, sems, table_ref, (even_ref, odd_ref), to_grid_and_back)
+    begin, run = stream(perm_ref, streams, sem, table_ref, (even_ref, odd_ref), to_grid_and_back)
     begin()
     chunk = 512
 
@@ -197,13 +208,13 @@
                 spread(rows, [q * group_rows + d * width + c + h for q in range(GROUPS)])
 
     run()
-    begin, run = stream(back_ref, count, slots, sems, table_ref, (even_ref, odd_ref), to_basis)
+    begin, run = stream(back_ref, streams, sem, table_ref, (even_ref, odd_ref), to_basis)
     begin()
 
     @pl.loop(0, count)
     def _(i):
         rows = packed_ref[pl.ds(pl.multiple_of(i * BLK, BLK), BLK), :]
-        spread(rows, [i * SPAN + q * BLK for q in range(GROUPS)])
+        spread(rows, [block * BLK for block in blocks_of(i, blocks)])
 
     run()
 
@@ -221,7 +232,7 @@
             pltpu.VMEM((points // GROUPS, LANES), jnp.float32),
             pltpu.VMEM((SPAN, LANES), jnp.bfloat16),
             pltpu.VMEM((SPAN, LANES), jnp.bfloat16),
-        ] + [pltpu.SMEM((SPAN,), jnp.int32)] * DEPTH + [pltpu.SemaphoreType.DMA((DEPTH,))],
+        ] + [pltpu.SMEM((4 * BLK,), jnp.int32)] * 64 + [pltpu.SemaphoreType.DMA((64,))],
         compiler_params=pltpu.CompilerParams(vmem_limit_bytes=VMEM_LIMIT),
         cost_estimate=pl.CostEstimate(
             flops=4 * vecs * points * BLK, bytes_accessed=300_000_000, transcendentals=0
@@ -276,7 +287,52 @@
     )(basis_vecs, low, high, columns, weights)
 
 
-def image_kernel(moved_ref, pot_ref, kinetic_ref, precond_ref, image_ref, sums_ref, left_ref, right_ref):
+def vector_kernel(moved_ref, precond_ref, sums_ref, total_ref):
+    step = pl.program_id(0)
+    reps, _, vecs, width = moved_ref.shape
+    count = reps * vecs
+
+    @pl.when(step == 0)
+    def _():
+        total_ref[...] = jnp.zeros_like(total_ref)
+
+    for s in range(0, width, 512):
+        at = slice(s, s + 512)
+        parts = [moved_ref[b, 0, :, at].astype(jnp.float32) for b in range(reps)]
+        vectors = jnp.concatenate(parts, axis=0)
+        scale = precond_ref[0:1, at]
+        left = jnp.concatenate(three_parts(vectors * (scale * scale)), axis=0)
+        total_ref[...] += dot_nt(left, vectors.astype(jnp.bfloat16))
+
+    @pl.when(step == pl.num_programs(0) - 1)
+    def _():
+        sums_ref[...] = (
+            total_ref[0:count] + total_ref[count:2 * count] + total_ref[2 * count:3 * count]
+        )
+
+
+def vector_sums(moved, precond, steps):
+    reps, _, vecs, rows = moved.shape
+    width = rows // steps
+    count = reps * vecs
+    return pl.pallas_call(
+        vector_kernel,
+        grid=(steps,),
+        out_shape=jax.ShapeDtypeStruct((count, count), jnp.float32),
+        in_specs=[
+            pl.BlockSpec((reps, 1, vecs, width), lambda i: (0, 0, 0, i)),
+            pl.BlockSpec((1, width), lambda i: (0, i)),
+        ],
+        out_specs=pl.BlockSpec((count, count), lambda i: (0, 0)),
+        scratch_shapes=[pltpu.VMEM((3 * count, count), jnp.float32)],
+        compiler_params=pltpu.CompilerParams(vmem_limit_bytes=VMEM_LIMIT),
+        cost_estimate=pl.CostEstimate(
+            flops=6 * count * count * rows, bytes_accessed=2 * count * rows, transcendentals=0
+        ),
+    )(moved, precond)
+
+
+def image_kernel(moved_ref, pot_ref, kinetic_ref, precond_ref, image_ref, sums_ref, total_ref):
     step = pl.program_id(0)
     reps, _, vecs, width = moved_ref.shape
     segment = pot_ref.shape[3]
@@ -284,44 +340,44 @@
 
     @pl.when(step == 0)
     def _():
-        left_ref[...] = jnp.zeros_like(left_ref)
-        right_ref[...] = jnp.zeros_like(right_ref)
+        total_ref[...] = jnp.zeros_like(total_ref)
+
+    def joined(k, at):
+        parts = [moved_ref[b, k, :, at].astype(jnp.float32) for b in range(reps)]
+        return jnp.concatenate(parts, axis=0).astype(jnp.bfloat16)
+
+    source = joined(1, slice(0, width))
+    blocks = [source[:, h:h + BLK] for h in range(0, width, BLK)]
+    kin_blocks = jnp.dot(
+        jnp.concatenate(blocks, axis=0), kinetic_ref[...], preferred_element_type=jnp.float32
+    )
+    per_segment = segment // BLK
 
     for s in range(width // segment):
         at = slice(s * segment, (s + 1) * segment)
-
-        def joined(k):
-            parts = [moved_ref[b, k, :, at].astype(jnp.float32) for b in range(reps)]
-            return jnp.concatenate(parts, axis=0)
-
-        vectors = joined(0)
-        source = joined(1).astype(jnp.bfloat16)
+        vectors = joined(0, at)
         kin = jnp.concatenate([
-            jnp.dot(source[:, h:h + BLK], kinetic_ref[...], preferred_element_type=jnp.float32)
-            for h in range(0, segment, BLK)
+            kin_blocks[h * count:(h + 1) * count]
+            for h in range(s * per_segment, (s + 1) * per_segment)
         ], axis=1)
         pot = jnp.concatenate([pot_ref[b, s].astype(jnp.float32) for b in range(reps)], axis=0)
         image = (kin + pot).astype(jnp.bfloat16)
         image_ref[:, at] = image
         scale = precond_ref[0:1, at]
-        square = scale * scale
-        vectors_16 = vectors.astype(jnp.bfloat16)
-        both = jnp.concatenate([image, vectors_16], axis=0)
-        image_parts = three_parts(image.astype(jnp.float32) * square)
-        vector_parts = three_parts(vectors * square)
-        left_ref[...] += dot_nt(jnp.concatenate(image_parts, axis=0), both)
-        right_ref[...] += dot_nt(jnp.concatenate([vectors_16] + vector_parts, axis=0), both)
+        scaled = three_parts(image.astype(jnp.float32) * (scale * scale))
+        left = jnp.concatenate(scaled + [image], axis=0)
+        total_ref[...] += dot_nt(left, jnp.concatenate([image, vectors], axis=0))
 
     @pl.when(step == pl.num_programs(0) - 1)
     def _():
-        left = left_ref[0:count] + left_ref[count:2 * count] + left_ref[2 * count:3 * count]
-        right = (
-            right_ref[count:2 * count] + right_ref[2 * count:3 * count] + right_ref[3 * count:4 * count]
+        scaled = total_ref[0:count] + total_ref[count:2 * count] + total_ref[2 * count:3 * count]
+        own, cross = scaled[:, 0:count], scaled[:, count:2 * count]
+        plain = total_ref[3 * count:4 * count, count:2 * count]
+        sums_ref[0:count, :] = jnp.concatenate([own, cross[:, 0:PAD]], axis=1)
+        sums_ref[count:2 * count, :] = jnp.concatenate([plain, cross[:, PAD:2 * PAD]], axis=1)
+        sums_ref[2 * count:, :] = jnp.concatenate(
+            [cross[b * vecs:(b + 1) * vecs, 2 * PAD:3 * PAD] for b in range(reps)], axis=1
         )
-        sums_ref[0] = right_ref[0:count, 0:count]
-        sums_ref[1] = left[:, 0:count]
-        sums_ref[2] = left[:, count:2 * count]
-        sums_ref[3] = right[:, count:2 * count]
 
 
 def image_of(moved, pot, kinetic, precond, steps):
@@ -329,12 +385,13 @@
     width = rows // steps
     count = reps * vecs
     pieces = pot.shape[1] // steps
+    packed = (2 * count + vecs, LANES)
     return pl.pallas_call(
         image_kernel,
         grid=(steps,),
         out_shape=(
             jax.ShapeDtypeStruct((count, rows), jnp.bfloat16),
-            jax.ShapeDtypeStruct((4, count, count), jnp.float32),
+            jax.ShapeDtypeStruct(packed, jnp.float32),
         ),
         in_specs=[
             pl.BlockSpec((reps, 2, vecs, width), lambda i: (0, 0, 0, i)),
@@ -344,31 +401,34 @@
         ],
         out_specs=(
             pl.BlockSpec((count, width), lambda i: (0, i)),
-            pl.BlockSpec((4, count, count), lambda i: (0, 0, 0)),
-        ),
-        scratch_shapes=[
-            pltpu.VMEM((3 * count, 2 * count), jnp.float32),
-            pltpu.VMEM((4 * count, 2 * count), jnp.float32),
-        ],
+            pl.BlockSpec(packed, lambda i: (0, 0)),
+        ),
+        scratch_shapes=[pltpu.VMEM((4 * count, 2 * count), jnp.float32)],
         compiler_params=pltpu.CompilerParams(vmem_limit_bytes=VMEM_LIMIT),
         cost_estimate=pl.CostEstimate(
-            flops=28 * count * count * rows, bytes_accessed=8 * count * rows, transcendentals=0
+            flops=16 * count * count * rows, bytes_accessed=8 * count * rows, transcendentals=0
         ),
     )(moved, pot, kinetic, precond)
 
 
-def solve_kernel(full_rows, sums_ref, moved_ref, image_ref, precond_ref, out_ref, rayleigh_ref, mix_ref):
+def solve_kernel(full_rows, sums_ref, vector_sums_ref, moved_ref, image_ref, precond_ref, out_ref, rayleigh_ref, mix_ref):
     count = image_ref.shape[0]
     reps, _, vecs, width = moved_ref.shape
 
     @pl.when(pl.program_id(0) == 0)
     def _():
-        rayleigh = sums_ref[0] / full_rows
+        turned = sums_ref[count:2 * count, 0:count] / full_rows
+        rayleigh = turned.T
         rayleigh_ref[...] = rayleigh
-        turned = rayleigh.T
-        cross = dot_exact(sums_ref[2], rayleigh)
-        last = dot_exact(turned, dot_exact(sums_ref[3], rayleigh))
-        gram = (sums_ref[1] - cross - cross.T + last) / full_rows
+        third = jnp.concatenate([
+            sums_ref[2 * count:, b * PAD:(b + 1) * PAD] for b in range(reps)
+        ], axis=0)
+        mixed = jnp.concatenate(
+            [sums_ref[0:count, count:], sums_ref[count:2 * count, count:], third], axis=1
+        )
+        cross = dot_exact(mixed, rayleigh)
+        last = dot_exact(turned, dot_exact(vector_sums_ref[...], rayleigh))
+        gram = (sums_ref[0:count, 0:count] - cross - cross.T + last) / full_rows
         pad = jnp.zeros((count, LANES - count), jnp.float32)
         row, column = iota((count, LANES), 0), iota((count, LANES), 1)
         left = jnp.concatenate([gram, pad], axis=1)
@@ -394,10 +454,10 @@
     for s in range(0, width, chunk):
         parts = jnp.dot(mix_ref[...], both[:, s:s + chunk], preferred_element_type=jnp.float32)
         total = (parts[2 * count:] + parts[count:2 * count]) + parts[0:count]
-        out_ref[:, s:s + chunk] = total * precond_ref[0:1, s:s + chunk]
-
-
-def solved_of(sums, moved, image, precond, full_rows, steps):
+        out_ref[:, 0, s:s + chunk] = total * precond_ref[0:1, s:s + chunk]
+
+
+def solved_of(sums, vector_sums, moved, image, precond, full_rows, steps):
     reps, _, vecs, rows = moved.shape
     width = rows // steps
     count = reps * vecs
@@ -405,17 +465,18 @@
         functools.partial(solve_kernel, full_rows),
         grid=(steps,),
         out_shape=(
-            jax.ShapeDtypeStruct((count, rows), jnp.float32),
+            jax.ShapeDtypeStruct((count, 1, rows), jnp.float32),
             jax.ShapeDtypeStruct((count, count), jnp.float32),
         ),
         in_specs=[
-            pl.BlockSpec((4, count, count), lambda i: (0, 0, 0)),
+            pl.BlockSpec(sums.shape, lambda i: (0, 0)),
+            pl.BlockSpec((count, count), lambda i: (0, 0)),
             pl.BlockSpec((reps, 1, vecs, width), lambda i: (0, 0, 0, i)),
             pl.BlockSpec((count, width), lambda i: (0, i)),
             pl.BlockSpec((1, width), lambda i: (0, i)),
         ],
         out_specs=(
-            pl.BlockSpec((count, width), lambda i: (0, i)),
+            pl.BlockSpec((count, 1, width), lambda i: (0, 0, i)),
             pl.BlockSpec((count, count), lambda i: (0, 0)),
         ),
         scratch_shapes=[pltpu.VMEM((3 * count, 2 * count), jnp.bfloat16)],
@@ -423,7 +484,7 @@
         cost_estimate=pl.CostEstimate(
             flops=12 * count * count * rows, bytes_accessed=8 * count * rows, transcendentals=0
         ),
-    )(sums, moved, image, precond)
+    )(sums, vector_sums, moved, image, precond)
 
 
 def sum_over_devices(x):
@@ -459,17 +520,18 @@
     arrived = lax.all_to_all(by_piece, "row", split_axis=0, concat_axis=0, tiled=True)
     columns = couplings[:, 1] - (lax.axis_index("row") * blocks - HB)
     by_rep = source_of(basis_vecs, low, high, columns, coupling_coefficient, reps)
+    out, back = index_streams(grid_perm, reps)
+    by_rep, out, back = lax.optimization_barrier((by_rep, out, back))
     moved = lax.all_to_all(by_rep, "rep", split_axis=0, concat_axis=0, tiled=True)
-    back = inverse_of(grid_perm, reps)
-    restored = surface_pass(arrived, grid_perm, back, potential, surface, reps)
+    restored = surface_pass(arrived, out, back, potential, surface, reps)
     pot = lax.all_to_all(restored, ("rep", "row"), split_axis=0, concat_axis=0, tiled=True)
     pot = pot.reshape(reps, pieces, vecs, width // reps)
     scale = precond.reshape(1, -1)
+    of_vectors = sum_over_devices(vector_sums(moved, scale, 8))
     image, sums = image_of(moved, pot, kinetic, scale, 8)
-    count = reps * vecs
-    sums = sum_over_devices(sums.reshape(4 * count, count)).reshape(4, count, count)
-    solved, rayleigh = solved_of(sums, moved, image, scale, float(rows * pieces), 8)
-    return (solved.reshape(count, 1, 1, -1), rayleigh)
+    sums = sum_over_devices(sums)
+    solved, rayleigh = solved_of(sums, of_vectors, moved, image, scale, float(rows * pieces), 8)
+    return (solved.reshape(reps * vecs, 1, 1, -1), rayleigh)
 
 
 def solution(mesh):

time: 363 us -> 308 us (0.85)
  waiting for transfers between devices: 54.4 us -> 11.9 us
  local copies, waits for them, and re-layouts: 20.5 us -> 9.22 us
  Pallas kernels: 202 us -> 191 us
  starting transfers between devices: 27.1 us -> 34.7 us
    ppermute x1, waiting for transfers between devices: 30.6 us -> 0.73 us  [body(): high = lax.ppermute(basis_vecs[:, :edge], 'row', backward)]
    pallas_call x1, Pallas kernels: 133 us -> 118 us  [surface_pass(): pl.pallas_call(surface_kernel, out_shape=jax.ShapeDtypeStruct((pieces * r...]
    ppermute x9 -> x18, waiting for transfers between devices: 22.5 us -> 9.78 us  [turned(): return lax.ppermute(x, axis, pairs)]
    unnamed x12 -> x14, local copies, waits for them, and re-layouts: 13.2 us -> 2.96 us
    pallas_call x1 -> x2, Pallas kernels: 28.8 us -> 36.3 us  [the longest x1 29.1 us: index_streams(): pl.pallas_call(functools.partial(inverse_kernel, reps), out_shape=(stream...]
    ppermute x9 -> x18, starting transfers between devices: 6.76 us -> 14.3 us  [turned(): return lax.ppermute(x, axis, pairs)]
    pallas_call x1, Pallas kernels: 15.8 us -> 10.8 us  [image_of(): pl.pallas_call(image_kernel, grid=(steps,), out_shape=(jax.ShapeDtypeStru...]
  transfers between devices with their start and end apart: 14 -> 24, of which waited for: 9 -> 9; matrix products, arithmetic and copies ran while one was open for 2% -> 1% of each run, Pallas kernels for 47% -> 53%
where the time goes in v2:
time: 308 us; the launch traced here: 303 us
  Pallas kernels  191 us (62%)
  blocking collectives  53.1 us (17%)
  starting transfers between devices  34.7 us (11%)
  waiting for transfers between devices  11.9 us (4%)
  local copies, waits for them, and re-layouts  9.22 us (3%)
    pallas_call x1, Pallas kernels, surface_pass(): pl.pallas_call(surface_kernel, out_shape=jax.ShapeDtypeStruct((pieces * r...  118 us
    all_to_all x1, blocking collectives, body(): lax.all_to_all(restored, ('rep', 'row'), split_axis=0, concat_axis=0, til...  53.1 us
    pallas_call x1, Pallas kernels, index_streams(): pl.pallas_call(functools.partial(inverse_kernel, reps), out_shape=(stream...  29.1 us
    pallas_call x1, Pallas kernels, solved_of(): pl.pallas_call(functools.partial(solve_kernel, full_rows), grid=(steps,),...  17.8 us
    ppermute x18, starting transfers between devices, turned(): return lax.ppermute(x, axis, pairs)  14.3 us
    pallas_call x1, Pallas kernels, image_of(): pl.pallas_call(image_kernel, grid=(steps,), out_shape=(jax.ShapeDtypeStru...  10.8 us
    ppermute x18, waiting for transfers between devices, turned(): return lax.ppermute(x, axis, pairs)  9.78 us
    all_to_all x1, starting transfers between devices, body(): lax.all_to_all(by_piece, 'row', split_axis=0, concat_axis=0, tiled=True)  8.72 us
  transfers between devices with their start and end apart: 24, of which 9 were waited for; matrix products, arithmetic and copies ran while one was open for 1% of the time, Pallas kernels for 53%

profile of v2, /device:TPU:1, one launch (start us, length us, event | category | flops | bytes accessed | tf_op | source)
XLA Modules:
  0.0 303.2 jit_solution(15341143954342738805)
XLA Ops:
  0.6 3.9 %copy.15 = bf16[3,32,8,2048]{3,2,0,1:T(8,128)(2,1)} copy(bf16[3,32,8,2048]{3,2,1,0:T(8,128)(2,1)} %bitcast.14) | data formatting | bytes 6291456 | tf_op jit(solution)/shard_map/reshape | solution.py:519
  4.6 8.7 %all-to-all-start.1 = ((bf16[32,24,2048]{2,1,0:T(8,128)(2,1)}), bf16[32,24,2048]{2,1,0:T(8,128)(2,1)S(1)}, u32[]{:S(2)}, u32[]{:S(2)}) async-start(bf16[32,24,2048]{2,1,0:T(8,128)(2,1)} %bitcast.15), calls=%async_computation.1 | async-start | bytes 6291456 | tf_op jit(solution)/shard_map/all_to_all | solution.py:520
  13.3 0.8 fusion
  14.1 2.1 collective-permute-start.1
  16.2 3.4 %collective-permute-start = (bf16[24,512]{1,0:T(8,128)(2,1)S(1)}, bf16[24,512]{1,0:T(8,128)(2,1)S(1)}, u32[]{:S(2)}, u32[]{:S(2)}) collective-permute-start(bf16[24,512]{1,0:T(8,128)(2,1)S(1)} %get-tuple-element.25), channel_id=1, source_target_pairs={{0,1},{1,2},{2,3},{3,4},{4,5},{5,6},{6,7},{7,8},{8,9},{9,10},{10,1... | collective-permute-start | bytes 73736 | tf_op jit(solution)/shard_map/ppermute | solution.py:517
  19.6 0.8 reshape.30.perm_ref
  20.4 29.1 %shard_map.96 = (s32[512,128]{1,0:T(8,128)}, s32[512,128]{1,0:T(8,128)}) custom-call(s32[256,256]{1,0:T(8,128)} %reshape.30.perm_ref), custom_call_target="tpu_custom_call" | custom-call | flops 17179869184 | bytes 524288 | tf_op jit(solution)/shard_map/pallas_call | solution.py:85
  49.5 0.6 subtract_reduce_fusion.column_ref
  50.1 0.7 collective-permute-done.1.high_ref
  50.9 0.0 collective-permute-done.low_ref
  50.9 0.6 copy-done.4
  51.5 0.6 copy-done.5
  52.1 7.4 %shard_map.95 = bf16[4,2,24,16384]{3,2,1,0:T(8,128)(2,1)} custom-call(bf16[24,65536]{1,0:T(8,128)(2,1)} %vecs_ref.1, bf16[24,512]{1,0:T(8,128)(2,1)} %copy-done.5, bf16[24,512]{1,0:T(8,128)(2,1)} %copy-done.4, s32[768]{0:T(1024)} %subtract_reduce_fusion.column_ref, f32[768]{0:T(1024)} %weight_ref.1), custom_call_target="tpu_custom_call" | custom-call | flops 9437184 | bytes 18874368 | tf_op jit(solution)/shard_map/pallas_call | solution.py:277
  59.5 0.0 all-to-all-done.1.x_ref
  59.5 1.7 copy-done
  61.2 5.3 %all-to-all-start = ((bf16[4,2,24,16384]{3,2,1,0:T(8,128)(2,1)}), bf16[4,2,24,16384]{3,2,1,0:T(8,128)(2,1)}, u32[]{:S(2)}, u32[]{:S(2)}) async-start(bf16[4,2,24,16384]{3,2,1,0:T(8,128)(2,1)} %shard_map.95), calls=%async_computation | async-start | bytes 12582912 | tf_op jit(solution)/shard_map/all_to_all | solution.py:525
  66.5 0.8 reshape.34.pot_ref
  67.3 118.4 %shard_map.97 = bf16[128,24,512]{2,1,0:T(8,128)(2,1)} custom-call(bf16[32,24,2048]{2,1,0:T(8,128)(2,1)} %copy-done, s32[65536]{0:T(1024)} %bitcast.20, s32[65536]{0:T(1024)} %bitcast.21, f32[256,256]{1,0:T(8,128)} %reshape.34.pot_ref, bf16[256,256]{1,0:T(8,128)(2,1)} %surf_ref.1), custom_call_target="tpu_custom_call" | custom-call | flops 1610612736 | bytes 300000000 | tf_op jit(solution)/shard_map/pallas_call | solution.py:225
  185.7 0.0 all-to-all-done.moved_ref
  185.7 53.1 %all_to_all.15 = bf16[128,24,512]{2,1,0:T(8,128)(2,1)} all-to-all(bf16[128,24,512]{2,1,0:T(8,128)(2,1)} %shard_map.97), channel_id=1, replica_groups=mesh['rep'=4,'row'=32] {'rep','row'}, dimensions={0} | all-to-all | bytes 6291456 | tf_op jit(solution)/shard_map/all_to_all | solution.py:527
  238.9 10.8 %shard_map.98 = (bf16[96,16384]{1,0:T(8,128)(2,1)}, f32[216,128]{1,0:T(8,128)}) custom-call(bf16[4,2,24,16384]{3,2,1,0:T(8,128)(2,1)} %all-to-all-done.moved_ref, bf16[4,32,24,512]{3,2,1,0:T(8,128)(2,1)} %bitcast.16, bf16[256,256]{1,0:T(8,128)(2,1)} %kinetic_ref.1, f32[1,16384]{1,0:T(1,128)} %bitcast.17), custom_call_target="tpu_custom_call" | custom-call | flops 2415919104 | bytes 12582912 | tf_op jit(solution)/shard_map/pallas_call | solution.py:389
  249.6 0.9 collective-permute-start.2
  250.5 7.2 %shard_map.99 = f32[96,96]{1,0:T(8,128)} custom-call(bf16[4,2,24,16384]{3,2,1,0:T(8,128)(2,1)} %all-to-all-done.moved_ref, f32[1,16384]{1,0:T(1,128)} %bitcast.18), custom_call_target="tpu_custom_call" | custom-call | flops 905969664 | bytes 3145728 | tf_op jit(solution)/shard_map/pallas_call | solution.py:318
  257.7 0.0 collective-permute-start.12
  257.7 1.4 collective-permute-done.12
  259.1 0.8 add.71
  259.9 0.4 collective-permute-start.15
  260.3 1.1 collective-permute-start.14
  261.4 0.7 collective-permute-start.13
  262.1 0.0 collective-permute-done.2
  262.1 2.1 collective-permute-start.5
  264.2 0.0 collective-permute-start.4
  264.2 0.0 collective-permute-done.15
  264.2 1.7 collective-permute-start.3
  265.9 0.0 collective-permute-done.14
  265.9 0.0 collective-permute-done.13
  266.0 0.9 collective-permute-start.18
  266.9 0.6 collective-permute-start.17
  267.5 0.0 collective-permute-done.5
  267.5 0.6 collective-permute-start.16
  268.1 2.7 collective-permute-done.4
  270.8 0.0 collective-permute-done.3
  270.9 0.5 collective-permute-start.8
  271.4 1.0 collective-permute-start.7
  272.4 0.7 collective-permute-start.6
  273.1 0.0 collective-permute-done.17
  273.1 0.0 collective-permute-done.16
  273.2 0.2 collective-permute-start.21
  273.3 1.4 collective-permute-start.20
  274.7 0.6 collective-permute-done.8
  275.3 0.1 collective-permute-start.19
  275.5 0.9 collective-permute-done.7
  276.4 1.6 collective-permute-done.6
  278.0 0.1 collective-permute-start.11
  278.1 1.5 collective-permute-start.10
  279.5 0.0 collective-permute-done.21
  279.6 0.6 collective-permute-start.9
  280.2 0.0 collective-permute-done.20
  280.2 0.6 add_add_fusion.3.vector_sums_ref
  280.8 0.8 collective-permute-done.11
  281.7 1.3 collective-permute-done.10
  283.0 1.8 collective-permute-done.9
  284.8 0.7 add_add_fusion.sums_ref
  285.4 17.8 %shard_map.100 = (f32[96,1,16384]{2,1,0:T(1,128)}, f32[96,96]{1,0:T(8,128)}) custom-call(f32[216,128]{1,0:T(8,128)} %add_add_fusion.sums_ref, f32[96,96]{1,0:T(8,128)} %add_add_fusion.3.vector_sums_ref, bf16[4,2,24,16384]{3,2,1,0:T(8,128)(2,1)} %all-to-all-done.moved_ref, bf16[96,16384]{1,0:T(8,128)(2,1)} %get-tuple-element.17.image_ref, f32[1,16384]{1,0:T(1,128)} %bitcast.19), custom_call_target="tpu_custom_call" | custom-call | flops 1811939328 | bytes 12582912 | tf_op jit(solution)/shard_map/pallas_call | solution.py:464
  (18 shorter events, 0.1 us)
Async XLA Ops:
  4.6 15.1 %copy-start.1 = (s32[65536]{0:T(1024)S(1)}, s32[65536]{0:T(1024)}, u32[]{:S(2)}) copy-start(s32[65536]{0:T(1024)} %param.11) | copy-start | bytes 786436
  4.6 54.9 %all-to-all-start.1 = ((bf16[32,24,2048]{2,1,0:T(8,128)(2,1)}), bf16[32,24,2048]{2,1,0:T(8,128)(2,1)S(1)}, u32[]{:S(2)}, u32[]{:S(2)}) async-start(bf16[32,24,2048]{2,1,0:T(8,128)(2,1)} %bitcast.15), calls=%async_computation.1 | async-start | bytes 6291456 | tf_op jit(solution)/shard_map/all_to_all | solution.py:520
  14.1 36.8 %collective-permute-start.1 = (bf16[24,512]{1,0:T(8,128)(2,1)S(1)}, bf16[24,512]{1,0:T(8,128)(2,1)S(1)}, u32[]{:S(2)}, u32[]{:S(2)}) collective-permute-start(bf16[24,512]{1,0:T(8,128)(2,1)S(1)} %get-tuple-element.24), channel_id=1, source_target_pairs={{1,0},{2,1},{3,2},{4,3},{5,4},{6,5},{7,6},{8,7},{9,8},{10,9},{11,1... | collective-permute-start | bytes 73736 | tf_op jit(solution)/shard_map/ppermute | solution.py:518
  16.2 34.7 %collective-permute-start = (bf16[24,512]{1,0:T(8,128)(2,1)S(1)}, bf16[24,512]{1,0:T(8,128)(2,1)S(1)}, u32[]{:S(2)}, u32[]{:S(2)}) collective-permute-start(bf16[24,512]{1,0:T(8,128)(2,1)S(1)} %get-tuple-element.25), channel_id=1, source_target_pairs={{0,1},{1,2},{2,3},{3,4},{4,5},{5,6},{6,7},{7,8},{8,9},{9,10},{10,1... | collective-permute-start | bytes 73736 | tf_op jit(solution)/shard_map/ppermute | solution.py:517
  20.4 29.1 %copy-start.6 = (s32[768,2]{0,1:T(2,128)S(1)}, s32[768,2]{0,1:T(2,128)}, u32[]{:S(2)}) copy-start(s32[768,2]{0,1:T(2,128)} %param.13) | copy-start | bytes 18436
  50.9 0.6 copy-start.4
  51.5 0.6 copy-start.5
  59.5 7.0 %copy-start.2 = (f32[65536]{0:T(1024)S(1)}, f32[65536]{0:T(1024)}, u32[]{:S(2)}) copy-start(f32[65536]{0:T(1024)} %param.9) | copy-start | bytes 786436
  59.5 1.7 copy-start
  61.2 124.5 %all-to-all-start = ((bf16[4,2,24,16384]{3,2,1,0:T(8,128)(2,1)}), bf16[4,2,24,16384]{3,2,1,0:T(8,128)(2,1)}, u32[]{:S(2)}, u32[]{:S(2)}) async-start(bf16[4,2,24,16384]{3,2,1,0:T(8,128)(2,1)} %shard_map.95), calls=%async_computation | async-start | bytes 12582912 | tf_op jit(solution)/shard_map/all_to_all | solution.py:525
  249.6 12.5 %copy-start.3 = (f32[216,128]{1,0:T(8,128)S(1)}, f32[216,128]{1,0:T(8,128)}, u32[]{:S(2)}) copy-start(f32[216,128]{1,0:T(8,128)} %get-tuple-element.16) | copy-start | bytes 331780
  249.6 12.5 %collective-permute-start.2 = (f32[216,128]{1,0:T(8,128)}, f32[216,128]{1,0:T(8,128)S(1)}, u32[]{:S(2)}, u32[]{:S(2)}) collective-permute-start(f32[216,128]{1,0:T(8,128)} %get-tuple-element.16), channel_id=1, source_target_pairs={{0,1},{1,0},{2,3},{3,2},{4,5},{5,4},{6,7},{7,6},{8,9},{9,8},{10,11... | collective-permute-start | bytes 331784 | tf_op jit(solution)/shard_map/ppermute | solution.py:499
  257.7 1.4 collective-permute-start.12
  259.9 4.3 %collective-permute-start.15 = (f32[96,96]{1,0:T(8,128)S(1)}, f32[96,96]{1,0:T(8,128)S(1)}, u32[]{:S(2)}, u32[]{:S(2)}) collective-permute-start(f32[96,96]{1,0:T(8,128)S(1)} %add.71), channel_id=1, source_target_pairs={{0,96},{32,0},{64,32},{96,64},{1,97},{33,1},{65,33},{97,65},{2,98}... | collective-permute-start | bytes 110600 | tf_op jit(solution)/shard_map/ppermute | solution.py:497
  260.3 5.6 %collective-permute-start.14 = (f32[96,96]{1,0:T(8,128)S(1)}, f32[96,96]{1,0:T(8,128)S(1)}, u32[]{:S(2)}, u32[]{:S(2)}) collective-permute-start(f32[96,96]{1,0:T(8,128)S(1)} %add.71), channel_id=1, source_target_pairs={{0,32},{32,64},{64,96},{96,0},{1,33},{33,65},{65,97},{97,1},{2,34}... | collective-permute-start | bytes 110600 | tf_op jit(solution)/shard_map/ppermute | solution.py:497
  261.4 4.5 %collective-permute-start.13 = (f32[96,96]{1,0:T(8,128)S(1)}, f32[96,96]{1,0:T(8,128)S(1)}, u32[]{:S(2)}, u32[]{:S(2)}) collective-permute-start(f32[96,96]{1,0:T(8,128)S(1)} %add.71), channel_id=1, source_target_pairs={{0,64},{32,96},{64,0},{96,32},{1,65},{33,97},{65,1},{97,33},{2,66}... | collective-permute-start | bytes 110600 | tf_op jit(solution)/shard_map/ppermute | solution.py:497
  262.1 5.4 %collective-permute-start.5 = (f32[216,128]{1,0:T(8,128)S(1)}, f32[216,128]{1,0:T(8,128)S(1)}, u32[]{:S(2)}, u32[]{:S(2)}) collective-permute-start(f32[216,128]{1,0:T(8,128)S(1)} %add.61), channel_id=1, source_target_pairs={{0,96},{32,0},{64,32},{96,64},{1,97},{33,1},{65,33},{97,65},{2,98}... | collective-permute-start | bytes 331784 | tf_op jit(solution)/shard_map/ppermute | solution.py:497
  264.2 6.6 %collective-permute-start.4 = (f32[216,128]{1,0:T(8,128)S(1)}, f32[216,128]{1,0:T(8,128)S(1)}, u32[]{:S(2)}, u32[]{:S(2)}) collective-permute-start(f32[216,128]{1,0:T(8,128)S(1)} %add.61), channel_id=1, source_target_pairs={{0,32},{32,64},{64,96},{96,0},{1,33},{33,65},{65,97},{97,1},{2,34}... | collective-permute-start | bytes 331784 | tf_op jit(solution)/shard_map/ppermute | solution.py:497
  264.2 6.6 %collective-permute-start.3 = (f32[216,128]{1,0:T(8,128)S(1)}, f32[216,128]{1,0:T(8,128)S(1)}, u32[]{:S(2)}, u32[]{:S(2)}) collective-permute-start(f32[216,128]{1,0:T(8,128)S(1)} %add.61), channel_id=1, source_target_pairs={{0,64},{32,96},{64,0},{96,32},{1,65},{33,97},{65,1},{97,33},{2,66}... | collective-permute-start | bytes 331784 | tf_op jit(solution)/shard_map/ppermute | solution.py:497
  266.0 6.4 %collective-permute-start.18 = (f32[96,96]{1,0:T(8,128)S(1)}, f32[96,96]{1,0:T(8,128)S(1)}, u32[]{:S(2)}, u32[]{:S(2)}) collective-permute-start(f32[96,96]{1,0:T(8,128)S(1)} %add_add_fusion.5), channel_id=1, source_target_pairs={{0,24},{1,25},{2,26},{3,27},{4,28},{5,29},{6,30},{7,31},{8,0},{9,1... | collective-permute-start | bytes 110600 | tf_op jit(solution)/shard_map/ppermute | solution.py:497
  266.9 6.3 %collective-permute-start.17 = (f32[96,96]{1,0:T(8,128)S(1)}, f32[96,96]{1,0:T(8,128)S(1)}, u32[]{:S(2)}, u32[]{:S(2)}) collective-permute-start(f32[96,96]{1,0:T(8,128)S(1)} %add_add_fusion.5), channel_id=1, source_target_pairs={{0,8},{1,9},{2,10},{3,11},{4,12},{5,13},{6,14},{7,15},{8,16},{9,17... | collective-permute-start | bytes 110600 | tf_op jit(solution)/shard_map/ppermute | solution.py:497
  267.5 5.6 %collective-permute-start.16 = (f32[96,96]{1,0:T(8,128)S(1)}, f32[96,96]{1,0:T(8,128)S(1)}, u32[]{:S(2)}, u32[]{:S(2)}) collective-permute-start(f32[96,96]{1,0:T(8,128)S(1)} %add_add_fusion.5), channel_id=1, source_target_pairs={{0,16},{1,17},{2,18},{3,19},{4,20},{5,21},{6,22},{7,23},{8,24},{9,... | collective-permute-start | bytes 110600 | tf_op jit(solution)/shard_map/ppermute | solution.py:497
  270.9 4.4 %collective-permute-start.8 = (f32[216,128]{1,0:T(8,128)S(1)}, f32[216,128]{1,0:T(8,128)S(1)}, u32[]{:S(2)}, u32[]{:S(2)}) collective-permute-start(f32[216,128]{1,0:T(8,128)S(1)} %add_add_fusion.2), channel_id=1, source_target_pairs={{0,24},{1,25},{2,26},{3,27},{4,28},{5,29},{6,30},{7,31},{8,0},{9,1... | collective-permute-start | bytes 331784 | tf_op jit(solution)/shard_map/ppermute | solution.py:497
  271.4 5.0 %collective-permute-start.7 = (f32[216,128]{1,0:T(8,128)S(1)}, f32[216,128]{1,0:T(8,128)S(1)}, u32[]{:S(2)}, u32[]{:S(2)}) collective-permute-start(f32[216,128]{1,0:T(8,128)S(1)} %add_add_fusion.2), channel_id=1, source_target_pairs={{0,8},{1,9},{2,10},{3,11},{4,12},{5,13},{6,14},{7,15},{8,16},{9,17... | collective-permute-start | bytes 331784 | tf_op jit(solution)/shard_map/ppermute | solution.py:497
  272.4 5.6 %collective-permute-start.6 = (f32[216,128]{1,0:T(8,128)S(1)}, f32[216,128]{1,0:T(8,128)S(1)}, u32[]{:S(2)}, u32[]{:S(2)}) collective-permute-start(f32[216,128]{1,0:T(8,128)S(1)} %add_add_fusion.2), channel_id=1, source_target_pairs={{0,16},{1,17},{2,18},{3,19},{4,20},{5,21},{6,22},{7,23},{8,24},{9,... | collective-permute-start | bytes 331784 | tf_op jit(solution)/shard_map/ppermute | solution.py:497
  273.2 6.4 %collective-permute-start.21 = (f32[96,96]{1,0:T(8,128)S(1)}, f32[96,96]{1,0:T(8,128)S(1)}, u32[]{:S(2)}, u32[]{:S(2)}) collective-permute-start(f32[96,96]{1,0:T(8,128)S(1)} %add_add_fusion.4), channel_id=1, source_target_pairs={{0,6},{1,7},{2,0},{3,1},{4,2},{5,3},{6,4},{7,5},{8,14},{9,15},{10,... | collective-permute-start | bytes 110600 | tf_op jit(solution)/shard_map/ppermute | solution.py:497
  273.3 6.9 %collective-permute-start.20 = (f32[96,96]{1,0:T(8,128)S(1)}, f32[96,96]{1,0:T(8,128)S(1)}, u32[]{:S(2)}, u32[]{:S(2)}) collective-permute-start(f32[96,96]{1,0:T(8,128)S(1)} %add_add_fusion.4), channel_id=1, source_target_pairs={{0,2},{1,3},{2,4},{3,5},{4,6},{5,7},{6,0},{7,1},{8,10},{9,11},{10,... | collective-permute-start | bytes 110600 | tf_op jit(solution)/shard_map/ppermute | solution.py:497
  275.3 4.9 %collective-permute-start.19 = (f32[96,96]{1,0:T(8,128)S(1)}, f32[96,96]{1,0:T(8,128)S(1)}, u32[]{:S(2)}, u32[]{:S(2)}) collective-permute-start(f32[96,96]{1,0:T(8,128)S(1)} %add_add_fusion.4), channel_id=1, source_target_pairs={{0,4},{1,5},{2,6},{3,7},{4,0},{5,1},{6,2},{7,3},{8,12},{9,13},{10,... | collective-permute-start | bytes 110600 | tf_op jit(solution)/shard_map/ppermute | solution.py:497
  278.0 3.7 %collective-permute-start.11 = (f32[216,128]{1,0:T(8,128)S(1)}, f32[216,128]{1,0:T(8,128)S(1)}, u32[]{:S(2)}, u32[]{:S(2)}) collective-permute-start(f32[216,128]{1,0:T(8,128)S(1)} %add_add_fusion.1), channel_id=1, source_target_pairs={{0,6},{1,7},{2,0},{3,1},{4,2},{5,3},{6,4},{7,5},{8,14},{9,15},{10,... | collective-permute-start | bytes 331784 | tf_op jit(solution)/shard_map/ppermute | solution.py:497
  278.1 4.9 %collective-permute-start.10 = (f32[216,128]{1,0:T(8,128)S(1)}, f32[216,128]{1,0:T(8,128)S(1)}, u32[]{:S(2)}, u32[]{:S(2)}) collective-permute-start(f32[216,128]{1,0:T(8,128)S(1)} %add_add_fusion.1), channel_id=1, source_target_pairs={{0,2},{1,3},{2,4},{3,5},{4,6},{5,7},{6,0},{7,1},{8,10},{9,11},{10,... | collective-permute-start | bytes 331784 | tf_op jit(solution)/shard_map/ppermute | solution.py:497
  279.6 5.2 %collective-permute-start.9 = (f32[216,128]{1,0:T(8,128)S(1)}, f32[216,128]{1,0:T(8,128)S(1)}, u32[]{:S(2)}, u32[]{:S(2)}) collective-permute-start(f32[216,128]{1,0:T(8,128)S(1)} %add_add_fusion.1), channel_id=1, source_target_pairs={{0,4},{1,5},{2,6},{3,7},{4,0},{5,1},{6,2},{7,3},{8,12},{9,13},{10,... | collective-permute-start | bytes 331784 | tf_op jit(solution)/shard_map/ppermute | solution.py:497

commit v3 on v2

--- a/solution.py
+++ b/solution.py
@@ -40,38 +40,54 @@
     return [high, middle, low]
 
 
-def inverse_kernel(reps, perm_ref, out_ref, back_ref, acc_ref):
+def inverse_kernel(reps, perm_ref, power_ref, out_ref, back_ref, acc_ref):
     blocks = perm_ref.shape[0]
-    acc_ref[...] = jnp.zeros_like(acc_ref)
+    half = blocks // 2
     step = 4
     rows = iota((BLK, BLK), 0)
-    lane = iota((BLK, BLK), 1).astype(jnp.float32)
-
-    @pl.loop(0, blocks // 8)
-    def _(i):
-        tile = perm_ref[pl.ds(pl.multiple_of(i * 8, 8), 8), :]
-        high = tile >> 8
-        low = tile & 255
-        for part in range(8 // step):
-            left, right = [], []
-            for k in range(step):
-                at = part * step + k
-                hit = rows == high[at:at + 1, :]
-                number = (i * 8 + at).astype(jnp.float32)
-                left.append(jnp.concatenate(
-                    [jnp.where(hit, number, 0.0), jnp.where(hit, lane, 0.0)], axis=0
-                ).astype(jnp.bfloat16))
-                right.append(jnp.where(rows == low[at:at + 1, :], 1.0, 0.0).astype(jnp.bfloat16))
-            acc_ref[...] += dot_nt(jnp.concatenate(left, axis=1), jnp.concatenate(right, axis=1))
-
-    acc_ref[0:BLK, :] = acc_ref[0:BLK, :] * 256.0 + acc_ref[BLK:2 * BLK, :]
+    lane = iota((1, BLK), 1)
+    code = jnp.where(lane < 128, lane + 128, -lane).astype(jnp.float32)
+
+    for part in range(2):
+        mine = slice(part * BLK, (part + 1) * BLK)
+        acc_ref[mine, :] = jnp.zeros((BLK, BLK), jnp.float32)
+
+        @pl.loop(0, half // 8)
+        def _(i):
+            tile = perm_ref[pl.ds(pl.multiple_of(part * half + i * 8, 8), 8), :]
+            high = tile >> 8
+            low = tile & 255
+            for first in range(0, 8, step):
+                left, right = [], []
+                for k in range(first, first + step):
+                    value = code * power_ref[i * 8 + k]
+                    left.append(
+                        jnp.where(rows == high[k:k + 1, :], value, 0.0).astype(jnp.bfloat16)
+                    )
+                    right.append(
+                        jnp.where(rows == low[k:k + 1, :], 1.0, 0.0).astype(jnp.bfloat16)
+                    )
+                acc_ref[mine, :] += dot_nt(
+                    jnp.concatenate(left, axis=1), jnp.concatenate(right, axis=1)
+                )
+
+    for r in range(0, BLK, 32):
+        late = acc_ref[BLK + r:BLK + r + 32, :]
+        held = acc_ref[r:r + 32, :] + late
+        size = jnp.abs(held)
+        number = jnp.where(late != 0.0, 32768.0, 0.0) + jnp.where(held < 0.0, 128.0, 0.0)
+        for bit in (64, 32, 16, 8, 4, 2, 1):
+            above = size >= 2.0 ** (bit - 57)
+            size = jnp.where(above, size * 2.0 ** -bit, size)
+            number = number + jnp.where(above, bit * 256.0, 0.0)
+        acc_ref[r:r + 32, :] = number + (size * 2.0 ** 64 - 128.0)
+
     per_rep = 8 // reps
     for d in range(blocks // 8):
         tile = acc_ref[d * 8:(d + 1) * 8, :]
         for b in range(reps):
             start = BLK + b * (blocks // reps) + d * per_rep
             acc_ref[start:start + per_rep, :] = tile[b * per_rep:(b + 1) * per_rep, :]
-    half = blocks // 2
     for k in range(2):
         out_ref[k * BLK:(k + 1) * BLK, :] = perm_ref[k * half:(k + 1) * half, :].T
         back_ref[k * BLK:(k + 1) * BLK, :] = acc_ref[
@@ -82,17 +98,18 @@
 def index_streams(perm, reps):
     blocks = perm.shape[0] // BLK
     streams = jax.ShapeDtypeStruct((2 * BLK, blocks // 2), jnp.int32)
+    powers = jnp.asarray([2.0 ** (k - 64) for k in range(blocks // 2)], jnp.float32)
     out, back = pl.pallas_call(
         functools.partial(inverse_kernel, reps),
         out_shape=(streams, streams),
-        in_specs=[WHOLE],
+        in_specs=[WHOLE, SCALARS],
         out_specs=(WHOLE, WHOLE),
         scratch_shapes=[pltpu.VMEM((2 * BLK, BLK), jnp.float32)],
         compiler_params=pltpu.CompilerParams(vmem_limit_bytes=VMEM_LIMIT),
         cost_estimate=pl.CostEstimate(
-            flops=4 * BLK * BLK * blocks * BLK, bytes_accessed=8 * blocks * BLK, transcendentals=0
-        ),
-    )(perm.reshape(blocks, BLK))
+            flops=2 * BLK * BLK * blocks * BLK, bytes_accessed=8 * blocks * BLK, transcendentals=0
+        ),
+    )(perm.reshape(blocks, BLK), powers)
     return out.reshape(-1), back.reshape(-1)
 
 
@@ -287,52 +304,10 @@
     )(basis_vecs, low, high, columns, weights)
 
 
-def vector_kernel(moved_ref, precond_ref, sums_ref, total_ref):
-    step = pl.program_id(0)
-    reps, _, vecs, width = moved_ref.shape
-    count = reps * vecs
-
-    @pl.when(step == 0)
-    def _():
-        total_ref[...] = jnp.zeros_like(total_ref)
-
-    for s in range(0, width, 512):
-        at = slice(s, s + 512)
-        parts = [moved_ref[b, 0, :, at].astype(jnp.float32) for b in range(reps)]
-        vectors = jnp.concatenate(parts, axis=0)
-        scale = precond_ref[0:1, at]
-        left = jnp.concatenate(three_parts(vectors * (scale * scale)), axis=0)
-        total_ref[...] += dot_nt(left, vectors.astype(jnp.bfloat16))
-
-    @pl.when(step == pl.num_programs(0) - 1)
-    def _():
-        sums_ref[...] = (
-            total_ref[0:count] + total_ref[count:2 * count] + total_ref[2 * count:3 * count]
-        )
-
-
-def vector_sums(moved, precond, steps):
-    reps, _, vecs, rows = moved.shape
-    width = rows // steps
-    count = reps * vecs
-    return pl.pallas_call(
-        vector_kernel,
-        grid=(steps,),
-        out_shape=jax.ShapeDtypeStruct((count, count), jnp.float32),
-        in_specs=[
-            pl.BlockSpec((reps, 1, vecs, width), lambda i: (0, 0, 0, i)),
-            pl.BlockSpec((1, width), lambda i: (0, i)),
-        ],
-        out_specs=pl.BlockSpec((count, count), lambda i: (0, 0)),
-        scratch_shapes=[pltpu.VMEM((3 * count, count), jnp.float32)],
-        compiler_params=pltpu.CompilerParams(vmem_limit_bytes=VMEM_LIMIT),
-        cost_estimate=pl.CostEstimate(
-            flops=6 * count * count * rows, bytes_accessed=2 * count * rows, transcendentals=0
-        ),
-    )(moved, precond)
-
-
-def image_kernel(moved_ref, pot_ref, kinetic_ref, precond_ref, image_ref, sums_ref, total_ref):
+def image_kernel(
+    core_ref, moved_ref, pot_ref, kinetic_ref, precond_ref,
+    image_ref, keep_ref, give_ref, total_ref, vector_ref, sums_ref
+):
     step = pl.program_id(0)
     reps, _, vecs, width = moved_ref.shape
     segment = pot_ref.shape[3]
@@ -341,6 +316,7 @@
     @pl.when(step == 0)
     def _():
         total_ref[...] = jnp.zeros_like(total_ref)
+        vector_ref[...] = jnp.zeros_like(vector_ref)
 
     def joined(k, at):
         parts = [moved_ref[b, k, :, at].astype(jnp.float32) for b in range(reps)]
@@ -364,36 +340,53 @@
         image = (kin + pot).astype(jnp.bfloat16)
         image_ref[:, at] = image
         scale = precond_ref[0:1, at]
-        scaled = three_parts(image.astype(jnp.float32) * (scale * scale))
+        square = scale * scale
+        scaled = three_parts(image.astype(jnp.float32) * square)
         left = jnp.concatenate(scaled + [image], axis=0)
         total_ref[...] += dot_nt(left, jnp.concatenate([image, vectors], axis=0))
+        scaled = three_parts(vectors.astype(jnp.float32) * square)
+        vector_ref[...] += dot_nt(jnp.concatenate(scaled, axis=0), vectors)
 
     @pl.when(step == pl.num_programs(0) - 1)
     def _():
         scaled = total_ref[0:count] + total_ref[count:2 * count] + total_ref[2 * count:3 * count]
         own, cross = scaled[:, 0:count], scaled[:, count:2 * count]
         plain = total_ref[3 * count:4 * count, count:2 * count]
+        vector = vector_ref[0:count] + vector_ref[count:2 * count] + vector_ref[2 * count:3 * count]
+        row, column = iota((count, count), 0), iota((count, count), 1)
+        own = jnp.where(row <= column, own, vector)
+        diagonal = jnp.sum(jnp.where(row == column, vector, 0.0), axis=0, keepdims=True)
         sums_ref[0:count, :] = jnp.concatenate([own, cross[:, 0:PAD]], axis=1)
         sums_ref[count:2 * count, :] = jnp.concatenate([plain, cross[:, PAD:2 * PAD]], axis=1)
-        sums_ref[2 * count:, :] = jnp.concatenate(
+        sums_ref[2 * count:2 * count + vecs, :] = jnp.concatenate(
             [cross[b * vecs:(b + 1) * vecs, 2 * PAD:3 * PAD] for b in range(reps)], axis=1
         )
-
-
-def image_of(moved, pot, kinetic, precond, steps):
+        sums_ref[2 * count + vecs:, :] = jnp.broadcast_to(
+            jnp.concatenate([diagonal, jnp.zeros((1, PAD), jnp.float32)], axis=1), (8, LANES)
+        )
+        size = keep_ref.shape[0]
+        core = core_ref[0]
+        keep_ref[...] = sums_ref[pl.ds(pl.multiple_of(core * size, 8), size), :]
+        give_ref[...] = sums_ref[pl.ds(pl.multiple_of((1 - core) * size, 8), size), :]
+
+
+def image_of(core, moved, pot, kinetic, precond, steps):
     reps, _, vecs, rows = moved.shape
     width = rows // steps
     count = reps * vecs
     pieces = pot.shape[1] // steps
-    packed = (2 * count + vecs, LANES)
+    packed = (2 * count + vecs + 8, LANES)
+    half = (packed[0] // 2, LANES)
     return pl.pallas_call(
         image_kernel,
         grid=(steps,),
         out_shape=(
             jax.ShapeDtypeStruct((count, rows), jnp.bfloat16),
-            jax.ShapeDtypeStruct(packed, jnp.float32),
+            jax.ShapeDtypeStruct(half, jnp.float32),
+            jax.ShapeDtypeStruct(half, jnp.float32),
         ),
         in_specs=[
+            SCALARS,
             pl.BlockSpec((reps, 2, vecs, width), lambda i: (0, 0, 0, i)),
             pl.BlockSpec((reps, pieces, vecs, pot.shape[3]), lambda i: (0, i, 0, 0)),
             pl.BlockSpec((BLK, BLK), lambda i: (0, 0)),
@@ -401,46 +394,73 @@
         ],
         out_specs=(
             pl.BlockSpec((count, width), lambda i: (0, i)),
-            pl.BlockSpec(packed, lambda i: (0, 0)),
-        ),
-        scratch_shapes=[pltpu.VMEM((4 * count, 2 * count), jnp.float32)],
+            pl.BlockSpec(half, lambda i: (0, 0)),
+            pl.BlockSpec(half, lambda i: (0, 0)),
+        ),
+        scratch_shapes=[
+            pltpu.VMEM((4 * count, 2 * count), jnp.float32),
+            pltpu.VMEM((3 * count, count), jnp.float32),
+            pltpu.VMEM(packed, jnp.float32),
+        ],
         compiler_params=pltpu.CompilerParams(vmem_limit_bytes=VMEM_LIMIT),
         cost_estimate=pl.CostEstimate(
-            flops=16 * count * count * rows, bytes_accessed=8 * count * rows, transcendentals=0
-        ),
-    )(moved, pot, kinetic, precond)
-
-
-def solve_kernel(full_rows, sums_ref, vector_sums_ref, moved_ref, image_ref, precond_ref, out_ref, rayleigh_ref, mix_ref):
+            flops=22 * count * count * rows, bytes_accessed=8 * count * rows, transcendentals=0
+        ),
+    )(core, moved, pot, kinetic, precond)
+
+
+def solve_kernel(
+    full_rows, core_ref, mine_ref, other_ref, moved_ref, image_ref, precond_ref,
+    out_ref, rayleigh_ref, mix_ref, sums_ref
+):
     count = image_ref.shape[0]
     reps, _, vecs, width = moved_ref.shape
 
     @pl.when(pl.program_id(0) == 0)
     def _():
+        size = mine_ref.shape[0]
+        core = core_ref[0]
+        sums_ref[pl.ds(pl.multiple_of(core * size, 8), size), :] = mine_ref[...]
+        sums_ref[pl.ds(pl.multiple_of((1 - core) * size, 8), size), :] = other_ref[...]
+        row, column = iota((count, count), 0), iota((count, count), 1)
+        shared = sums_ref[0:count, 0:count]
+        shared_t = shared.T
+        own = jnp.where(row <= column, shared, shared_t)
+        vector = jnp.where(row <= column, shared_t, shared)
+        diagonal = sums_ref[2 * count + vecs:2 * count + vecs + 1, 0:count]
+        vector = jnp.where(row == column, diagonal, vector)
         turned = sums_ref[count:2 * count, 0:count] / full_rows
         rayleigh = turned.T
         rayleigh_ref[...] = rayleigh
         third = jnp.concatenate([
-            sums_ref[2 * count:, b * PAD:(b + 1) * PAD] for b in range(reps)
+            sums_ref[2 * count:2 * count + vecs, b * PAD:(b + 1) * PAD] for b in range(reps)
         ], axis=0)
         mixed = jnp.concatenate(
             [sums_ref[0:count, count:], sums_ref[count:2 * count, count:], third], axis=1
         )
         cross = dot_exact(mixed, rayleigh)
-        last = dot_exact(turned, dot_exact(vector_sums_ref[...], rayleigh))
-        gram = (sums_ref[0:count, 0:count] - cross - cross.T + last) / full_rows
+        last = dot_exact(turned, dot_exact(vector, rayleigh))
+        gram = (own - cross - cross.T + last) / full_rows
         pad = jnp.zeros((count, LANES - count), jnp.float32)
         row, column = iota((count, LANES), 0), iota((count, LANES), 1)
         left = jnp.concatenate([gram, pad], axis=1)
         right = jnp.where(row == column, 1.0, 0.0)
-        for j in range(count):
-            pivot_left, pivot_right = left[j:j + 1, :], right[j:j + 1, :]
-            ratio = left[:, j:j + 1] / pivot_left[:, j:j + 1]
-            ratio = jnp.where(row[:, 0:1] > j, ratio, 0.0)
-            left = left - ratio * pivot_left
-            right = right - ratio * pivot_right
+        for j in range(0, count, 2):
+            first, second = left[j:j + 1, :], left[j + 1:j + 2, :]
+            a, b, c = first[:, j:j + 1], first[:, j + 1:j + 2], second[:, j + 1:j + 2]
+            over = 1.0 / (a * c - b * b)
+            below = row[:, 0:1] > j + 1
+            one, two = left[:, j:j + 1], left[:, j + 1:j + 2]
+            ratio_one = jnp.where(below, (one * c - two * b) * over, 0.0)
+            ratio_two = jnp.where(below, (two * a - one * b) * over, 0.0)
+            left = left - (ratio_one * first + ratio_two * second)
+            right = right - (ratio_one * right[j:j + 1, :] + ratio_two * right[j + 1:j + 2, :])
         diagonal = jnp.sum(jnp.where(row == column, left, 0.0), axis=1, keepdims=True)
-        inverse = (right * lax.rsqrt(diagonal))[:, 0:count]
+        beside = jnp.sum(jnp.where(row == column + 1, left, 0.0), axis=1, keepdims=True)
+        diagonal = jnp.broadcast_to(diagonal, left.shape)
+        ratio = jnp.where(row % 2 == 1, beside / pltpu.roll(diagonal, 1, 0), 0.0)
+        right = right - ratio * pltpu.roll(right, 1, 0)
+        inverse = (right * lax.rsqrt(diagonal - ratio * beside))[:, 0:count]
         parts = three_parts(inverse) + three_parts(-dot_exact(inverse, turned))
         for k in range(3):
             mix_ref[k * count:(k + 1) * count, 0:count] = parts[k]
@@ -457,7 +477,7 @@
         out_ref[:, 0, s:s + chunk] = total * precond_ref[0:1, s:s + chunk]
 
 
-def solved_of(sums, vector_sums, moved, image, precond, full_rows, steps):
+def solved_of(core, mine, other, moved, image, precond, full_rows, steps):
     reps, _, vecs, rows = moved.shape
     width = rows // steps
     count = reps * vecs
@@ -469,8 +489,9 @@
             jax.ShapeDtypeStruct((count, count), jnp.float32),
         ),
         in_specs=[
-            pl.BlockSpec(sums.shape, lambda i: (0, 0)),
-            pl.BlockSpec((count, count), lambda i: (0, 0)),
+            SCALARS,
+            pl.BlockSpec(mine.shape, lambda i: (0, 0)),
+            pl.BlockSpec(mine.shape, lambda i: (0, 0)),
             pl.BlockSpec((reps, 1, vecs, width), lambda i: (0, 0, 0, i)),
             pl.BlockSpec((count, width), lambda i: (0, i)),
             pl.BlockSpec((1, width), lambda i: (0, i)),
@@ -479,28 +500,31 @@
             pl.BlockSpec((count, 1, width), lambda i: (0, 0, i)),
             pl.BlockSpec((count, count), lambda i: (0, 0)),
         ),
-        scratch_shapes=[pltpu.VMEM((3 * count, 2 * count), jnp.bfloat16)],
+        scratch_shapes=[
+            pltpu.VMEM((3 * count, 2 * count), jnp.bfloat16),
+            pltpu.VMEM((2 * mine.shape[0], LANES), jnp.float32),
+        ],
         compiler_params=pltpu.CompilerParams(vmem_limit_bytes=VMEM_LIMIT),
         cost_estimate=pl.CostEstimate(
             flops=12 * count * count * rows, bytes_accessed=8 * count * rows, transcendentals=0
         ),
-    )(sums, vector_sums, moved, image, precond)
-
-
-def sum_over_devices(x):
-    def turned(axis, stride, shift):
-        size = lax.axis_size(axis)
+    )(core, mine, other, moved, image, precond)
+
+
+def sum_over_devices(keep, give):
+    def turned(x, axis, stride, shift):
         pairs = []
-        for i in range(size):
+        for i in range(lax.axis_size(axis)):
             digit = (i // stride) % 4
             pairs.append((i, i + ((digit + shift) % 4 - digit) * stride))
         return lax.ppermute(x, axis, pairs)
 
-    x = x + lax.ppermute(x, "row", [(i, i ^ 1) for i in range(lax.axis_size("row"))])
+    swap = [(i, i ^ 1) for i in range(lax.axis_size("row"))]
+    x = keep + lax.ppermute(give, "row", swap)
     for axis, stride in (("rep", 1), ("row", 8), ("row", 2)):
-        up, down, across = (turned(axis, stride, shift) for shift in (1, 3, 2))
+        up, down, across = (turned(x, axis, stride, shift) for shift in (1, 3, 2))
         x = (x + across) + (up + down)
-    return x
+    return x, lax.ppermute(x, "row", swap)
 
 
 def body(
@@ -527,10 +551,10 @@
     pot = lax.all_to_all(restored, ("rep", "row"), split_axis=0, concat_axis=0, tiled=True)
     pot = pot.reshape(reps, pieces, vecs, width // reps)
     scale = precond.reshape(1, -1)
-    of_vectors = sum_over_devices(vector_sums(moved, scale, 8))
-    image, sums = image_of(moved, pot, kinetic, scale, 8)
-    sums = sum_over_devices(sums)
-    solved, rayleigh = solved_of(sums, of_vectors, moved, image, scale, float(rows * pieces), 8)
+    core = (lax.axis_index("row") % 2).reshape(1)
+    image, keep, give = image_of(core, moved, pot, kinetic, scale, 8)
+    mine, other = sum_over_devices(keep, give)
+    solved, rayleigh = solved_of(core, mine, other, moved, image, scale, float(rows * pieces), 8)
     return (solved.reshape(reps * vecs, 1, 1, -1), rayleigh)
 
 

time: 308 us -> 300 us (0.974); the launches traced: 303 us -> 299 us
  waiting for transfers between devices: 11.9 us -> 67.4 us
  blocking collectives: 53.1 us -> 0 us
  Pallas kernels: 191 us -> 178 us
  starting transfers between devices: 34.7 us -> 40.2 us
    all_to_all x1 -> x0, blocking collectives: 53.1 us -> none  [body(): lax.all_to_all(restored, ('rep', 'row'), split_axis=0, concat_axis=0, til...]
    all_to_all x0 -> x1, waiting for transfers between devices: none -> 41.9 us  [body(): lax.all_to_all(restored, ('rep', 'row'), split_axis=0, concat_axis=0, til...]
    ppermute x1, waiting for transfers between devices: 0.73 us -> 10.8 us  [body(): high = lax.ppermute(basis_vecs[:, :edge], 'row', backward)]
    pallas_call x1, Pallas kernels: 29.1 us -> 19.1 us  [index_streams(): pl.pallas_call(functools.partial(inverse_kernel, reps), out_shape=(stream...]
    all_to_all x0 -> x1, starting transfers between devices: none -> 8.84 us  [body(): lax.all_to_all(restored, ('rep', 'row'), split_axis=0, concat_axis=0, til...]
    ppermute x18 -> x9, starting transfers between devices: 14.3 us -> 6.05 us  [turned(): return lax.ppermute(x, axis, pairs)]
    pallas_call x1 -> x0, Pallas kernels: 7.21 us -> none  [vector_sums(): pl.pallas_call(vector_kernel, grid=(steps,), out_shape=jax.ShapeDtypeStru...]
    ppermute x2, starting transfers between devices: 0.89 us -> 5.73 us  [the longest x1 4.9 us: sum_over_devices(): return (x, lax.ppermute(x, 'row', swap))]
  transfers between devices with their start and end apart: 24 -> 16, of which waited for: 9 -> 13; matrix products, arithmetic and copies ran while one was open for 1% -> 1% of each run, Pallas kernels for 53% -> 48%
where the time goes in v3:
time: 300 us; the launch traced here: 299 us
  Pallas kernels  178 us (59%)
  waiting for transfers between devices  67.4 us (22%)
  starting transfers between devices  40.2 us (13%)
  local copies, waits for them, and re-layouts  11.5 us (4%)
    pallas_call x1, Pallas kernels, surface_pass(): pl.pallas_call(surface_kernel, out_shape=jax.ShapeDtypeStruct((pieces * r...  118 us
    all_to_all x1, waiting for transfers between devices, body(): lax.all_to_all(restored, ('rep', 'row'), split_axis=0, concat_axis=0, til...  41.9 us
    pallas_call x1, Pallas kernels, solved_of(): pl.pallas_call(functools.partial(solve_kernel, full_rows), grid=(steps,),...  20.3 us
    pallas_call x1, Pallas kernels, index_streams(): pl.pallas_call(functools.partial(inverse_kernel, reps), out_shape=(stream...  19.1 us
    ppermute x9, waiting for transfers between devices, turned(): return lax.ppermute(x, axis, pairs)  12.7 us
    pallas_call x1, Pallas kernels, image_of(): pl.pallas_call(image_kernel, grid=(steps,), out_shape=(jax.ShapeDtypeStru...  12.5 us
    ppermute x1, waiting for transfers between devices, body(): high = lax.ppermute(basis_vecs[:, :edge], 'row', backward)  10.8 us
    all_to_all x1, starting transfers between devices, body(): lax.all_to_all(restored, ('rep', 'row'), split_axis=0, concat_axis=0, til...  8.84 us
  transfers between devices with their start and end apart: 16, of which 13 were waited for; matrix products, arithmetic and copies ran while one was open for 1% of the time, Pallas kernels for 48%

profile of v3, /device:TPU:1, one launch (start us, length us, event | category | flops | bytes accessed | tf_op | source)
XLA Modules:
  0.0 299.0 jit_solution(1396797558511563052)
XLA Ops:
  0.6 3.9 %copy.16 = bf16[3,32,8,2048]{3,2,0,1:T(8,128)(2,1)} copy(bf16[3,32,8,2048]{3,2,1,0:T(8,128)(2,1)} %bitcast.15) | data formatting | bytes 6291456 | tf_op jit(solution)/shard_map/reshape | solution.py:543
  4.6 0.0 copy-start.2
  4.6 8.7 %all-to-all-start.1 = ((bf16[32,24,2048]{2,1,0:T(8,128)(2,1)}), bf16[32,24,2048]{2,1,0:T(8,128)(2,1)S(1)}, u32[]{:S(2)}, u32[]{:S(2)}) async-start(bf16[32,24,2048]{2,1,0:T(8,128)(2,1)} %bitcast.16), calls=%async_computation.1 | async-start | bytes 6291456 | tf_op jit(solution)/shard_map/all_to_all | solution.py:544
  13.3 0.8 fusion
  14.1 2.1 collective-permute-start.1
  16.2 3.4 %collective-permute-start = (bf16[24,512]{1,0:T(8,128)(2,1)S(1)}, bf16[24,512]{1,0:T(8,128)(2,1)S(1)}, u32[]{:S(2)}, u32[]{:S(2)}) collective-permute-start(bf16[24,512]{1,0:T(8,128)(2,1)S(1)} %get-tuple-element.27), channel_id=1, source_target_pairs={{0,1},{1,2},{2,3},{3,4},{4,5},{5,6},{6,7},{7,8},{8,9},{9,10},{10,1... | collective-permute-start | bytes 73736 | tf_op jit(solution)/shard_map/ppermute | solution.py:541
  19.6 0.0 copy-done.2
  19.6 0.8 reshape.34.perm_ref
  20.4 0.0 copy-start.8
  20.4 19.1 %shard_map.105 = (s32[512,128]{1,0:T(8,128)}, s32[512,128]{1,0:T(8,128)}) custom-call(s32[256,256]{1,0:T(8,128)} %reshape.34.perm_ref, f32[128]{0:T(128)} %constant.23.clone.power_ref), custom_call_target="tpu_custom_call" | custom-call | flops 8589934592 | bytes 524288 | tf_op jit(solution)/shard_map/pallas_call | solution.py:102
  39.5 0.0 copy-done.8
  39.5 0.6 subtract_reduce_fusion.column_ref
  40.1 10.8 %collective-permute-done.1.high_ref = bf16[24,512]{1,0:T(8,128)(2,1)S(1)} collective-permute-done((bf16[24,512]{1,0:T(8,128)(2,1)S(1)}, bf16[24,512]{1,0:T(8,128)(2,1)S(1)}, u32[]{:S(2)}, u32[]{:S(2)}) %collective-permute-start.1) | collective-permute-done | bytes 24608 | tf_op jit(solution)/shard_map/ppermute | solution.py:542
  50.9 0.0 copy-start.6
  50.9 0.0 collective-permute-done.low_ref
  50.9 0.6 copy-done.6
  51.5 0.0 copy-start.7
  51.5 0.6 copy-done.7
  52.1 7.4 %shard_map.104 = bf16[4,2,24,16384]{3,2,1,0:T(8,128)(2,1)} custom-call(bf16[24,65536]{1,0:T(8,128)(2,1)} %vecs_ref.1, bf16[24,512]{1,0:T(8,128)(2,1)} %copy-done.7, bf16[24,512]{1,0:T(8,128)(2,1)} %copy-done.6, s32[768]{0:T(1024)} %subtract_reduce_fusion.column_ref, f32[768]{0:T(1024)} %weight_ref.1), custom_call_target="tpu_custom_call" | custom-call | flops 9437184 | bytes 18874368 | tf_op jit(solution)/shard_map/pallas_call | solution.py:294
  59.4 0.0 copy-start.3
  59.4 0.0 all-to-all-done.1.x_ref
  59.4 0.0 copy-start
  59.5 1.7 copy-done
  61.2 5.3 %all-to-all-start = ((bf16[4,2,24,16384]{3,2,1,0:T(8,128)(2,1)}), bf16[4,2,24,16384]{3,2,1,0:T(8,128)(2,1)}, u32[]{:S(2)}, u32[]{:S(2)}) async-start(bf16[4,2,24,16384]{3,2,1,0:T(8,128)(2,1)} %shard_map.104), calls=%async_computation | async-start | bytes 12582912 | tf_op jit(solution)/shard_map/all_to_all | solution.py:549
  66.4 0.0 copy-done.3
  66.5 0.8 reshape.38.pot_ref
  67.2 118.4 %shard_map.106 = bf16[128,24,512]{2,1,0:T(8,128)(2,1)} custom-call(bf16[32,24,2048]{2,1,0:T(8,128)(2,1)} %copy-done, s32[65536]{0:T(1024)} %bitcast.18, s32[65536]{0:T(1024)} %bitcast.19, f32[256,256]{1,0:T(8,128)} %reshape.38.pot_ref, bf16[256,256]{1,0:T(8,128)(2,1)} %surf_ref.1), custom_call_target="tpu_custom_call" | custom-call | flops 1610612736 | bytes 300000000 | tf_op jit(solution)/shard_map/pallas_call | solution.py:242
  185.6 0.0 all-to-all-done.moved_ref
  185.7 8.8 %all-to-all-start.2 = ((bf16[128,24,512]{2,1,0:T(8,128)(2,1)}), bf16[128,24,512]{2,1,0:T(8,128)(2,1)S(1)}, u32[]{:S(2)}, u32[]{:S(2)}) async-start(bf16[128,24,512]{2,1,0:T(8,128)(2,1)} %shard_map.106), calls=%async_computation.2 | async-start | bytes 6291456 | tf_op jit(solution)/shard_map/all_to_all | solution.py:551
  194.5 41.9 %all-to-all-done.2 = bf16[128,24,512]{2,1,0:T(8,128)(2,1)S(1)} async-done(((bf16[128,24,512]{2,1,0:T(8,128)(2,1)}), bf16[128,24,512]{2,1,0:T(8,128)(2,1)S(1)}, u32[]{:S(2)}, u32[]{:S(2)}) %all-to-all-start.2) | async-done | bytes 3145760 | tf_op jit(solution)/shard_map/all_to_all | solution.py:551
  236.4 0.0 copy-start.1
  236.4 1.7 copy-done.1
  238.1 12.5 %shard_map.107 = (bf16[96,16384]{1,0:T(8,128)(2,1)}, f32[112,128]{1,0:T(8,128)}, f32[112,128]{1,0:T(8,128)}) custom-call(s32[1]{0:T(128)} %bitcast.core_ref, bf16[4,2,24,16384]{3,2,1,0:T(8,128)(2,1)} %all-to-all-done.moved_ref, bf16[4,32,24,512]{3,2,1,0:T(8,128)(2,1)} %bitcast.17, bf16[256,256]{1,0:T(8,128)(2,1)} %kinetic_ref.1, f32[1,16384]{1,0:T(1,128)} %bitcast.20), custom_call_target="tpu_custom_call" | custom-call | flops 3321888768 | bytes 12582912 | tf_op jit(solution)/shard_map/pallas_call | solution.py:380
  250.6 0.8 collective-permute-start.2
  251.5 1.1 collective-permute-done.2
  252.6 0.8 add.36
  253.4 0.4 collective-permute-start.5
  253.8 1.1 collective-permute-start.4
  254.9 0.7 collective-permute-start.3
  255.5 0.9 collective-permute-done.5
  256.4 1.6 collective-permute-done.4
  258.0 1.5 collective-permute-done.3
  259.5 0.9 collective-permute-start.8
  260.4 0.6 collective-permute-start.7
  261.0 0.6 collective-permute-start.6
  261.7 0.9 collective-permute-done.8
  262.6 2.0 collective-permute-done.7
  264.6 1.5 collective-permute-done.6
  266.1 0.1 collective-permute-start.11
  266.2 1.5 collective-permute-start.10
  267.7 0.2 collective-permute-start.9
  267.9 1.3 collective-permute-done.11
  269.2 1.3 collective-permute-done.10
  270.5 1.7 collective-permute-done.9
  272.2 0.0 copy-start.4
  272.2 4.9 %collective-permute-start.12 = (f32[112,128]{1,0:T(8,128)S(1)}, f32[112,128]{1,0:T(8,128)S(1)}, u32[]{:S(2)}, u32[]{:S(2)}) collective-permute-start(f32[112,128]{1,0:T(8,128)S(1)} %add_add_fusion.mine_ref), channel_id=1, source_target_pairs={{0,1},{1,0},{2,3},{3,2},{4,5},{5,4},{6,7},{7,6},{8,9},{9,8},{10,11... | collective-permute-start | bytes 172040 | tf_op jit(solution)/shard_map/ppermute | solution.py:527
  277.1 0.9 collective-permute-done.12.other_ref
  278.0 0.0 copy-start.5
  278.0 0.0 copy-done.4
  278.0 0.6 copy-done.5
  278.6 20.3 %shard_map.108 = (f32[96,1,16384]{2,1,0:T(1,128)}, f32[96,96]{1,0:T(8,128)}) custom-call(s32[1]{0:T(128)} %bitcast.core_ref, f32[112,128]{1,0:T(8,128)} %copy-done.4, f32[112,128]{1,0:T(8,128)} %copy-done.5, bf16[4,2,24,16384]{3,2,1,0:T(8,128)(2,1)} %all-to-all-done.moved_ref, bf16[96,16384]{1,0:T(8,128)(2,1)} %get-tuple-element.19.image_ref, ...), custom_call_target="tpu_custom_call" | custom-call | flops 1811939328 | bytes 12582912 | tf_op jit(solution)/shard_map/pallas_call | solution.py:484
  (3 shorter events, 0.0 us)
Async XLA Ops:
  4.6 15.1 %copy-start.2 = (s32[65536]{0:T(1024)S(1)}, s32[65536]{0:T(1024)}, u32[]{:S(2)}) copy-start(s32[65536]{0:T(1024)} %param.12) | copy-start | bytes 786436
  4.6 54.9 %all-to-all-start.1 = ((bf16[32,24,2048]{2,1,0:T(8,128)(2,1)}), bf16[32,24,2048]{2,1,0:T(8,128)(2,1)S(1)}, u32[]{:S(2)}, u32[]{:S(2)}) async-start(bf16[32,24,2048]{2,1,0:T(8,128)(2,1)} %bitcast.16), calls=%async_computation.1 | async-start | bytes 6291456 | tf_op jit(solution)/shard_map/all_to_all | solution.py:544
  14.1 36.8 %collective-permute-start.1 = (bf16[24,512]{1,0:T(8,128)(2,1)S(1)}, bf16[24,512]{1,0:T(8,128)(2,1)S(1)}, u32[]{:S(2)}, u32[]{:S(2)}) collective-permute-start(bf16[24,512]{1,0:T(8,128)(2,1)S(1)} %get-tuple-element.26), channel_id=1, source_target_pairs={{1,0},{2,1},{3,2},{4,3},{5,4},{6,5},{7,6},{8,7},{9,8},{10,9},{11,1... | collective-permute-start | bytes 73736 | tf_op jit(solution)/shard_map/ppermute | solution.py:542
  16.2 34.7 %collective-permute-start = (bf16[24,512]{1,0:T(8,128)(2,1)S(1)}, bf16[24,512]{1,0:T(8,128)(2,1)S(1)}, u32[]{:S(2)}, u32[]{:S(2)}) collective-permute-start(bf16[24,512]{1,0:T(8,128)(2,1)S(1)} %get-tuple-element.27), channel_id=1, source_target_pairs={{0,1},{1,2},{2,3},{3,4},{4,5},{5,6},{6,7},{7,8},{8,9},{9,10},{10,1... | collective-permute-start | bytes 73736 | tf_op jit(solution)/shard_map/ppermute | solution.py:541
  20.4 19.1 %copy-start.8 = (s32[768,2]{0,1:T(2,128)S(1)}, s32[768,2]{0,1:T(2,128)}, u32[]{:S(2)}) copy-start(s32[768,2]{0,1:T(2,128)} %param.14) | copy-start | bytes 18436
  50.9 0.6 copy-start.6
  51.5 0.6 copy-start.7
  59.4 7.0 %copy-start.3 = (f32[65536]{0:T(1024)S(1)}, f32[65536]{0:T(1024)}, u32[]{:S(2)}) copy-start(f32[65536]{0:T(1024)} %param.10) | copy-start | bytes 786436
  59.4 1.7 copy-start
  61.2 124.5 %all-to-all-start = ((bf16[4,2,24,16384]{3,2,1,0:T(8,128)(2,1)}), bf16[4,2,24,16384]{3,2,1,0:T(8,128)(2,1)}, u32[]{:S(2)}, u32[]{:S(2)}) async-start(bf16[4,2,24,16384]{3,2,1,0:T(8,128)(2,1)} %shard_map.104), calls=%async_computation | async-start | bytes 12582912 | tf_op jit(solution)/shard_map/all_to_all | solution.py:549
  185.7 50.8 %all-to-all-start.2 = ((bf16[128,24,512]{2,1,0:T(8,128)(2,1)}), bf16[128,24,512]{2,1,0:T(8,128)(2,1)S(1)}, u32[]{:S(2)}, u32[]{:S(2)}) async-start(bf16[128,24,512]{2,1,0:T(8,128)(2,1)} %shard_map.106), calls=%async_computation.2 | async-start | bytes 6291456 | tf_op jit(solution)/shard_map/all_to_all | solution.py:551
  236.4 1.7 copy-start.1
  250.6 1.9 collective-permute-start.2
  253.4 3.0 %collective-permute-start.5 = (f32[112,128]{1,0:T(8,128)S(1)}, f32[112,128]{1,0:T(8,128)S(1)}, u32[]{:S(2)}, u32[]{:S(2)}) collective-permute-start(f32[112,128]{1,0:T(8,128)S(1)} %add.36), channel_id=1, source_target_pairs={{0,96},{32,0},{64,32},{96,64},{1,97},{33,1},{65,33},{97,65},{2,98}... | collective-permute-start | bytes 172040 | tf_op jit(solution)/shard_map/ppermute | solution.py:520
  253.8 4.2 %collective-permute-start.4 = (f32[112,128]{1,0:T(8,128)S(1)}, f32[112,128]{1,0:T(8,128)S(1)}, u32[]{:S(2)}, u32[]{:S(2)}) collective-permute-start(f32[112,128]{1,0:T(8,128)S(1)} %add.36), channel_id=1, source_target_pairs={{0,32},{32,64},{64,96},{96,0},{1,33},{33,65},{65,97},{97,1},{2,34}... | collective-permute-start | bytes 172040 | tf_op jit(solution)/shard_map/ppermute | solution.py:520
  254.9 4.6 %collective-permute-start.3 = (f32[112,128]{1,0:T(8,128)S(1)}, f32[112,128]{1,0:T(8,128)S(1)}, u32[]{:S(2)}, u32[]{:S(2)}) collective-permute-start(f32[112,128]{1,0:T(8,128)S(1)} %add.36), channel_id=1, source_target_pairs={{0,64},{32,96},{64,0},{96,32},{1,65},{33,97},{65,1},{97,33},{2,66}... | collective-permute-start | bytes 172040 | tf_op jit(solution)/shard_map/ppermute | solution.py:520
  259.5 3.1 %collective-permute-start.8 = (f32[112,128]{1,0:T(8,128)S(1)}, f32[112,128]{1,0:T(8,128)S(1)}, u32[]{:S(2)}, u32[]{:S(2)}) collective-permute-start(f32[112,128]{1,0:T(8,128)S(1)} %add_add_fusion.2), channel_id=1, source_target_pairs={{0,24},{1,25},{2,26},{3,27},{4,28},{5,29},{6,30},{7,31},{8,0},{9,1... | collective-permute-start | bytes 172040 | tf_op jit(solution)/shard_map/ppermute | solution.py:520
  260.4 4.2 %collective-permute-start.7 = (f32[112,128]{1,0:T(8,128)S(1)}, f32[112,128]{1,0:T(8,128)S(1)}, u32[]{:S(2)}, u32[]{:S(2)}) collective-permute-start(f32[112,128]{1,0:T(8,128)S(1)} %add_add_fusion.2), channel_id=1, source_target_pairs={{0,8},{1,9},{2,10},{3,11},{4,12},{5,13},{6,14},{7,15},{8,16},{9,17... | collective-permute-start | bytes 172040 | tf_op jit(solution)/shard_map/ppermute | solution.py:520
  261.0 5.1 %collective-permute-start.6 = (f32[112,128]{1,0:T(8,128)S(1)}, f32[112,128]{1,0:T(8,128)S(1)}, u32[]{:S(2)}, u32[]{:S(2)}) collective-permute-start(f32[112,128]{1,0:T(8,128)S(1)} %add_add_fusion.2), channel_id=1, source_target_pairs={{0,16},{1,17},{2,18},{3,19},{4,20},{5,21},{6,22},{7,23},{8,24},{9,... | collective-permute-start | bytes 172040 | tf_op jit(solution)/shard_map/ppermute | solution.py:520
  266.1 3.1 %collective-permute-start.11 = (f32[112,128]{1,0:T(8,128)S(1)}, f32[112,128]{1,0:T(8,128)S(1)}, u32[]{:S(2)}, u32[]{:S(2)}) collective-permute-start(f32[112,128]{1,0:T(8,128)S(1)} %add_add_fusion.1), channel_id=1, source_target_pairs={{0,6},{1,7},{2,0},{3,1},{4,2},{5,3},{6,4},{7,5},{8,14},{9,15},{10,... | collective-permute-start | bytes 172040 | tf_op jit(solution)/shard_map/ppermute | solution.py:520
  266.2 4.3 %collective-permute-start.10 = (f32[112,128]{1,0:T(8,128)S(1)}, f32[112,128]{1,0:T(8,128)S(1)}, u32[]{:S(2)}, u32[]{:S(2)}) collective-permute-start(f32[112,128]{1,0:T(8,128)S(1)} %add_add_fusion.1), channel_id=1, source_target_pairs={{0,2},{1,3},{2,4},{3,5},{4,6},{5,7},{6,0},{7,1},{8,10},{9,11},{10,... | collective-permute-start | bytes 172040 | tf_op jit(solution)/shard_map/ppermute | solution.py:520
  267.7 4.5 %collective-permute-start.9 = (f32[112,128]{1,0:T(8,128)S(1)}, f32[112,128]{1,0:T(8,128)S(1)}, u32[]{:S(2)}, u32[]{:S(2)}) collective-permute-start(f32[112,128]{1,0:T(8,128)S(1)} %add_add_fusion.1), channel_id=1, source_target_pairs={{0,4},{1,5},{2,6},{3,7},{4,0},{5,1},{6,2},{7,3},{8,12},{9,13},{10,... | collective-permute-start | bytes 172040 | tf_op jit(solution)/shard_map/ppermute | solution.py:520
  272.2 5.8 %copy-start.4 = (f32[112,128]{1,0:T(8,128)}, f32[112,128]{1,0:T(8,128)S(1)}, u32[]{:S(2)}) copy-start(f32[112,128]{1,0:T(8,128)S(1)} %add_add_fusion.mine_ref) | copy-start | bytes 172036
  272.2 5.8 %collective-permute-start.12 = (f32[112,128]{1,0:T(8,128)S(1)}, f32[112,128]{1,0:T(8,128)S(1)}, u32[]{:S(2)}, u32[]{:S(2)}) collective-permute-start(f32[112,128]{1,0:T(8,128)S(1)} %add_add_fusion.mine_ref), channel_id=1, source_target_pairs={{0,1},{1,0},{2,3},{3,2},{4,5},{5,4},{6,7},{7,6},{8,9},{9,8},{10,11... | collective-permute-start | bytes 172040 | tf_op jit(solution)/shard_map/ppermute | solution.py:527
  278.0 0.6 copy-start.5

commit v4 on v3

--- a/solution.py
+++ b/solution.py
@@ -257,12 +257,12 @@
     )(arrived, perm, back, potential.reshape(-1, BLK), surface)
 
 
-def source_kernel(vecs_ref, low_ref, high_ref, column_ref, weight_ref, out_ref, wide_ref):
-    reps = out_ref.shape[0]
+def source_kernel(rep_ref, vecs_ref, low_ref, high_ref, column_ref, weight_ref, *rest):
+    outs, wide_ref = rest[:-1], rest[-1]
+    reps = len(outs)
     edge = low_ref.shape[1]
     rows = vecs_ref.shape[1]
     blocks = rows // BLK
-    piece_blocks = out_ref.shape[3] * reps // (blocks * BLK)
     wide_ref[:, 0:edge] = low_ref[...]
     wide_ref[:, edge + rows:] = high_ref[...]
     per_piece = 8
@@ -275,84 +275,132 @@
 
     @pl.loop(0, blocks // per_piece)
     def _(j):
-        for k in range(per_piece):
-            a = j * per_piece + k
-            total = None
-            for m in range(COUPLINGS_PER_ROW):
-                c = a * COUPLINGS_PER_ROW + m
-                at = pl.multiple_of(column_ref[c] * BLK, BLK)
-                term = wide_ref[:, pl.ds(at, BLK)].astype(jnp.float32) * weight_ref[c]
-                total = term if total is None else total + term
-            to = pl.ds(pl.multiple_of(j * per_rep * BLK, per_rep * BLK) + (k % per_rep) * BLK, BLK)
-            here = pl.multiple_of(a * BLK, BLK)
-            out_ref[k // per_rep, 0, :, to] = vecs_ref[:, pl.ds(here, BLK)]
-            out_ref[k // per_rep, 1, :, to] = total.astype(jnp.bfloat16)
-
-
-def source_of(basis_vecs, low, high, columns, weights, reps):
+        for s in range(reps):
+            to_rep = (rep_ref[0] + (reps - s)) % reps
+            for h in range(per_rep):
+                a = j * per_piece + to_rep * per_rep + h
+                total = None
+                for m in range(COUPLINGS_PER_ROW):
+                    c = a * COUPLINGS_PER_ROW + m
+                    at = pl.multiple_of(column_ref[c] * BLK, BLK)
+                    term = wide_ref[:, pl.ds(at, BLK)].astype(jnp.float32) * weight_ref[c]
+                    total = term if total is None else total + term
+                to = pl.ds(pl.multiple_of((j * per_rep + h) * BLK, BLK), BLK)
+                outs[s][0, :, to] = vecs_ref[:, pl.ds(pl.multiple_of(a * BLK, BLK), BLK)]
+                outs[s][1, :, to] = total.astype(jnp.bfloat16)
+
+
+def source_of(rep, basis_vecs, low, high, columns, weights, reps):
     vecs, rows = basis_vecs.shape
     return pl.pallas_call(
         source_kernel,
-        out_shape=jax.ShapeDtypeStruct((reps, 2, vecs, rows // reps), jnp.bfloat16),
-        in_specs=[WHOLE, WHOLE, WHOLE, SCALARS, SCALARS],
-        out_specs=WHOLE,
+        out_shape=(jax.ShapeDtypeStruct((2, vecs, rows // reps), jnp.bfloat16),) * reps,
+        in_specs=[SCALARS, WHOLE, WHOLE, WHOLE, SCALARS, SCALARS],
+        out_specs=(WHOLE,) * reps,
         scratch_shapes=[pltpu.VMEM((vecs, rows + 2 * low.shape[1]), jnp.bfloat16)],
         compiler_params=pltpu.CompilerParams(vmem_limit_bytes=VMEM_LIMIT),
         cost_estimate=pl.CostEstimate(
             flops=6 * vecs * rows, bytes_accessed=12 * vecs * rows, transcendentals=0
         ),
-    )(basis_vecs, low, high, columns, weights)
-
-
-def image_kernel(
-    core_ref, moved_ref, pot_ref, kinetic_ref, precond_ref,
-    image_ref, keep_ref, give_ref, total_ref, vector_ref, sums_ref
-):
+    )(rep, basis_vecs, low, high, columns, weights)
+
+
+def vector_kernel(rep_ref, *refs):
+    parts = refs[:-6]
+    kinetic_ref, precond_ref, vectors_ref, kin_ref, sums_ref, total_ref = refs[-6:]
     step = pl.program_id(0)
-    reps, _, vecs, width = moved_ref.shape
-    segment = pot_ref.shape[3]
+    reps = len(parts)
+    _, vecs, width = parts[0].shape
     count = reps * vecs
 
     @pl.when(step == 0)
     def _():
         total_ref[...] = jnp.zeros_like(total_ref)
-        vector_ref[...] = jnp.zeros_like(vector_ref)
-
-    def joined(k, at):
-        parts = [moved_ref[b, k, :, at].astype(jnp.float32) for b in range(reps)]
-        return jnp.concatenate(parts, axis=0).astype(jnp.bfloat16)
-
-    source = joined(1, slice(0, width))
+
+    def ordered(k):
+        for s, part in enumerate(parts):
+            group = (rep_ref[0] + s) % reps
+            start = pl.multiple_of(group * vecs, 8)
+            kin_ref[pl.ds(start, vecs), :] = part[k].astype(jnp.float32)
+        return kin_ref[...]
+
+    vectors = ordered(0)
+    vectors_16 = vectors.astype(jnp.bfloat16)
+    vectors_ref[...] = vectors_16
+    scale = precond_ref[...]
+    left = jnp.concatenate(three_parts(vectors * (scale * scale)), axis=0)
+    total_ref[...] += dot_nt(left, vectors_16)
+    source = ordered(1).astype(jnp.bfloat16)
     blocks = [source[:, h:h + BLK] for h in range(0, width, BLK)]
-    kin_blocks = jnp.dot(
-        jnp.concatenate(blocks, axis=0), kinetic_ref[...], preferred_element_type=jnp.float32
-    )
-    per_segment = segment // BLK
+    kin = jnp.dot(jnp.concatenate(blocks, axis=0), kinetic_ref[...], preferred_element_type=jnp.float32)
+    for h in range(width // BLK):
+        kin_ref[:, h * BLK:(h + 1) * BLK] = kin[h * count:(h + 1) * count]
+
+    @pl.when(step == pl.num_programs(0) - 1)
+    def _():
+        sums_ref[...] = (
+            total_ref[0:count] + total_ref[count:2 * count] + total_ref[2 * count:3 * count]
+        )
+
+
+def vectors_of(rep, parts, kinetic, precond, steps):
+    reps = len(parts)
+    _, vecs, rows = parts[0].shape
+    width = rows // steps
+    count = reps * vecs
+    return pl.pallas_call(
+        vector_kernel,
+        grid=(steps,),
+        out_shape=(
+            jax.ShapeDtypeStruct((count, rows), jnp.bfloat16),
+            jax.ShapeDtypeStruct((count, rows), jnp.float32),
+            jax.ShapeDtypeStruct((count, count), jnp.float32),
+        ),
+        in_specs=[SCALARS] + [pl.BlockSpec((2, vecs, width), lambda i: (0, 0, i))] * reps + [
+            pl.BlockSpec((BLK, BLK), lambda i: (0, 0)),
+            pl.BlockSpec((1, width), lambda i: (0, i)),
+        ],
+        out_specs=(
+            pl.BlockSpec((count, width), lambda i: (0, i)),
+            pl.BlockSpec((count, width), lambda i: (0, i)),
+            pl.BlockSpec((count, count), lambda i: (0, 0)),
+        ),
+        scratch_shapes=[pltpu.VMEM((3 * count, count), jnp.float32)],
+        compiler_params=pltpu.CompilerParams(vmem_limit_bytes=VMEM_LIMIT),
+        cost_estimate=pl.CostEstimate(
+            flops=12 * count * count * rows, bytes_accessed=8 * count * rows, transcendentals=0
+        ),
+    )(rep, *parts, kinetic, precond)
+
+
+def image_kernel(
+    core_ref, vectors_ref, kin_ref, vector_sums_ref, pot_ref, precond_ref,
+    image_ref, keep_ref, give_ref, total_ref, sums_ref
+):
+    step = pl.program_id(0)
+    count, width = vectors_ref.shape
+    reps, _, vecs, segment = pot_ref.shape
+
+    @pl.when(step == 0)
+    def _():
+        total_ref[...] = jnp.zeros_like(total_ref)
 
     for s in range(width // segment):
         at = slice(s * segment, (s + 1) * segment)
-        vectors = joined(0, at)
-        kin = jnp.concatenate([
-            kin_blocks[h * count:(h + 1) * count]
-            for h in range(s * per_segment, (s + 1) * per_segment)
-        ], axis=1)
         pot = jnp.concatenate([pot_ref[b, s].astype(jnp.float32) for b in range(reps)], axis=0)
-        image = (kin + pot).astype(jnp.bfloat16)
+        image = (kin_ref[:, at] + pot).astype(jnp.bfloat16)
         image_ref[:, at] = image
         scale = precond_ref[0:1, at]
-        square = scale * scale
-        scaled = three_parts(image.astype(jnp.float32) * square)
+        scaled = three_parts(image.astype(jnp.float32) * (scale * scale))
         left = jnp.concatenate(scaled + [image], axis=0)
-        total_ref[...] += dot_nt(left, jnp.concatenate([image, vectors], axis=0))
-        scaled = three_parts(vectors.astype(jnp.float32) * square)
-        vector_ref[...] += dot_nt(jnp.concatenate(scaled, axis=0), vectors)
+        total_ref[...] += dot_nt(left, jnp.concatenate([image, vectors_ref[:, at]], axis=0))
 
     @pl.when(step == pl.num_programs(0) - 1)
     def _():
         scaled = total_ref[0:count] + total_ref[count:2 * count] + total_ref[2 * count:3 * count]
         own, cross = scaled[:, 0:count], scaled[:, count:2 * count]
         plain = total_ref[3 * count:4 * count, count:2 * count]
-        vector = vector_ref[0:count] + vector_ref[count:2 * count] + vector_ref[2 * count:3 * count]
+        vector = vector_sums_ref[...]
         row, column = iota((count, count), 0), iota((count, count), 1)
         own = jnp.where(row <= column, own, vector)
         diagonal = jnp.sum(jnp.where(row == column, vector, 0.0), axis=0, keepdims=True)
@@ -370,11 +418,10 @@
         give_ref[...] = sums_ref[pl.ds(pl.multiple_of((1 - core) * size, 8), size), :]
 
 
-def image_of(core, moved, pot, kinetic, precond, steps):
-    reps, _, vecs, rows = moved.shape
+def image_of(core, vectors, kin, vector_sums, pot, precond, steps):
+    count, rows = vectors.shape
+    reps, pieces, vecs, segment = pot.shape
     width = rows // steps
-    count = reps * vecs
-    pieces = pot.shape[1] // steps
     packed = (2 * count + vecs + 8, LANES)
     half = (packed[0] // 2, LANES)
     return pl.pallas_call(
@@ -387,9 +434,10 @@
         ),
         in_specs=[
             SCALARS,
-            pl.BlockSpec((reps, 2, vecs, width), lambda i: (0, 0, 0, i)),
-            pl.BlockSpec((reps, pieces, vecs, pot.shape[3]), lambda i: (0, i, 0, 0)),
-            pl.BlockSpec((BLK, BLK), lambda i: (0, 0)),
+            pl.BlockSpec((count, width), lambda i: (0, i)),
+            pl.BlockSpec((count, width), lambda i: (0, i)),
+            pl.BlockSpec((count, count), lambda i: (0, 0)),
+            pl.BlockSpec((reps, pieces // steps, vecs, segment), lambda i: (0, i, 0, 0)),
             pl.BlockSpec((1, width), lambda i: (0, i)),
         ],
         out_specs=(
@@ -399,22 +447,21 @@
         ),
         scratch_shapes=[
             pltpu.VMEM((4 * count, 2 * count), jnp.float32),
-            pltpu.VMEM((3 * count, count), jnp.float32),
             pltpu.VMEM(packed, jnp.float32),
         ],
         compiler_params=pltpu.CompilerParams(vmem_limit_bytes=VMEM_LIMIT),
         cost_estimate=pl.CostEstimate(
-            flops=22 * count * count * rows, bytes_accessed=8 * count * rows, transcendentals=0
-        ),
-    )(core, moved, pot, kinetic, precond)
+            flops=16 * count * count * rows, bytes_accessed=10 * count * rows, transcendentals=0
+        ),
+    )(core, vectors, kin, vector_sums, pot, precond)
 
 
 def solve_kernel(
-    full_rows, core_ref, mine_ref, other_ref, moved_ref, image_ref, precond_ref,
+    full_rows, reps, core_ref, mine_ref, other_ref, vectors_ref, image_ref, precond_ref,
     out_ref, rayleigh_ref, mix_ref, sums_ref
 ):
-    count = image_ref.shape[0]
-    reps, _, vecs, width = moved_ref.shape
+    count, width = image_ref.shape
+    vecs = count // reps
 
     @pl.when(pl.program_id(0) == 0)
     def _():
@@ -466,10 +513,7 @@
             mix_ref[k * count:(k + 1) * count, 0:count] = parts[k]
             mix_ref[k * count:(k + 1) * count, count:2 * count] = parts[3 + k]
 
-    vectors = jnp.concatenate(
-        [moved_ref[b, 0].astype(jnp.float32) for b in range(reps)], axis=0
-    ).astype(jnp.bfloat16)
-    both = jnp.concatenate([image_ref[...], vectors], axis=0)
+    both = jnp.concatenate([image_ref[...], vectors_ref[...]], axis=0)
     chunk = 512
     for s in range(0, width, chunk):
         parts = jnp.dot(mix_ref[...], both[:, s:s + chunk], preferred_element_type=jnp.float32)
@@ -477,12 +521,11 @@
         out_ref[:, 0, s:s + chunk] = total * precond_ref[0:1, s:s + chunk]
 
 
-def solved_of(core, mine, other, moved, image, precond, full_rows, steps):
-    reps, _, vecs, rows = moved.shape
+def solved_of(core, mine, other, vectors, image, precond, full_rows, reps, steps):
+    count, rows = image.shape
     width = rows // steps
-    count = reps * vecs
     return pl.pallas_call(
-        functools.partial(solve_kernel, full_rows),
+        functools.partial(solve_kernel, full_rows, reps),
         grid=(steps,),
         out_shape=(
             jax.ShapeDtypeStruct((count, 1, rows), jnp.float32),
@@ -492,7 +535,7 @@
             SCALARS,
             pl.BlockSpec(mine.shape, lambda i: (0, 0)),
             pl.BlockSpec(mine.shape, lambda i: (0, 0)),
-            pl.BlockSpec((reps, 1, vecs, width), lambda i: (0, 0, 0, i)),
+            pl.BlockSpec((count, width), lambda i: (0, i)),
             pl.BlockSpec((count, width), lambda i: (0, i)),
             pl.BlockSpec((1, width), lambda i: (0, i)),
         ],
@@ -508,7 +551,7 @@
         cost_estimate=pl.CostEstimate(
             flops=12 * count * count * rows, bytes_accessed=8 * count * rows, transcendentals=0
         ),
-    )(core, mine, other, moved, image, precond)
+    )(core, mine, other, vectors, image, precond)
 
 
 def sum_over_devices(keep, give):
@@ -541,20 +584,27 @@
     low = lax.ppermute(basis_vecs[:, rows - edge:], "row", forward)
     high = lax.ppermute(basis_vecs[:, :edge], "row", backward)
     by_piece = basis_vecs.reshape(vecs, pieces, width).transpose(1, 0, 2)
+    by_piece, low, high, perm = lax.optimization_barrier((by_piece, low, high, grid_perm))
     arrived = lax.all_to_all(by_piece, "row", split_axis=0, concat_axis=0, tiled=True)
     columns = couplings[:, 1] - (lax.axis_index("row") * blocks - HB)
-    by_rep = source_of(basis_vecs, low, high, columns, coupling_coefficient, reps)
-    out, back = index_streams(grid_perm, reps)
-    by_rep, out, back = lax.optimization_barrier((by_rep, out, back))
-    moved = lax.all_to_all(by_rep, "rep", split_axis=0, concat_axis=0, tiled=True)
+    rep = lax.axis_index("rep").reshape(1)
+    core = (lax.axis_index("row") % 2).reshape(1)
+    parts = source_of(rep, basis_vecs, low, high, columns, coupling_coefficient, reps)
+    parts = [
+        part if s == 0 else lax.ppermute(part, "rep", [(i, (i - s) % reps) for i in range(reps)])
+        for s, part in enumerate(parts)
+    ]
+    out, back = index_streams(perm, reps)
     restored = surface_pass(arrived, out, back, potential, surface, reps)
     pot = lax.all_to_all(restored, ("rep", "row"), split_axis=0, concat_axis=0, tiled=True)
     pot = pot.reshape(reps, pieces, vecs, width // reps)
     scale = precond.reshape(1, -1)
-    core = (lax.axis_index("row") % 2).reshape(1)
-    image, keep, give = image_of(core, moved, pot, kinetic, scale, 8)
+    vectors, kin, vector_sums = vectors_of(rep, parts, kinetic, scale, 8)
+    image, keep, give = image_of(core, vectors, kin, vector_sums, pot, scale, 8)
     mine, other = sum_over_devices(keep, give)
-    solved, rayleigh = solved_of(core, mine, other, moved, image, scale, float(rows * pieces), 8)
+    solved, rayleigh = solved_of(
+        core, mine, other, vectors, image, scale, float(rows * pieces), reps, 8
+    )
     return (solved.reshape(reps * vecs, 1, 1, -1), rayleigh)
 
 

time: 300 us -> 369 us (1.23)
  waiting for transfers between devices: 67.4 us -> 124 us
  Pallas kernels: 178 us -> 187 us
    ppermute x0 -> x3, waiting for transfers between devices: none -> 93.2 us  [body(): lax.ppermute(part, 'rep', [(i, (i - s) % reps) for i in range(reps)])]
    all_to_all x1, waiting for transfers between devices: 41.9 us -> 0.01 us  [body(): lax.all_to_all(restored, ('rep', 'row'), split_axis=0, concat_axis=0, til...]
    all_to_all x1, waiting for transfers between devices: 0.01 us -> 18.3 us  [body(): lax.all_to_all(by_piece, 'row', split_axis=0, concat_axis=0, tiled=True)]
    pallas_call x2 -> x3, Pallas kernels: 27.7 us -> 39.2 us  [the longest x1 20.4 us: solved_of(): pl.pallas_call(functools.partial(solve_kernel, full_rows, reps), grid=(st...]
    ppermute x1, waiting for transfers between devices: 10.8 us -> 0.01 us  [body(): high = lax.ppermute(basis_vecs[:, :edge], 'row', backward)]
    all_to_all x1 -> x0, starting transfers between devices: 5.27 us -> none  [body(): lax.all_to_all(by_rep, 'rep', split_axis=0, concat_axis=0, tiled=True)]
    ppermute x0 -> x3, starting transfers between devices: none -> 4.14 us  [body(): lax.ppermute(part, 'rep', [(i, (i - s) % reps) for i in range(reps)])]
  transfers between devices with their start and end apart: 16 -> 18, of which waited for: 13 -> 11; matrix products, arithmetic and copies ran while one was open for 1% -> 2% of each run, Pallas kernels for 48% -> 10%
where the time goes in v4:
time: 369 us; the launch traced here: 368 us
  Pallas kernels  187 us (51%)
  waiting for transfers between devices  124 us (34%)
  starting transfers between devices  42.7 us (12%)
  local copies, waits for them, and re-layouts  11.8 us (3%)
    pallas_call x1, Pallas kernels, surface_pass(): pl.pallas_call(surface_kernel, out_shape=jax.ShapeDtypeStruct((pieces * r...  118 us
    ppermute x3, waiting for transfers between devices, body(): lax.ppermute(part, 'rep', [(i, (i - s) % reps) for i in range(reps)])  93.2 us
    pallas_call x1, Pallas kernels, solved_of(): pl.pallas_call(functools.partial(solve_kernel, full_rows, reps), grid=(st...  20.4 us
    pallas_call x1, Pallas kernels, index_streams(): pl.pallas_call(functools.partial(inverse_kernel, reps), out_shape=(stream...  19 us
    all_to_all x1, waiting for transfers between devices, body(): lax.all_to_all(by_piece, 'row', split_axis=0, concat_axis=0, tiled=True)  18.3 us
    pallas_call x1, Pallas kernels, vectors_of(): pl.pallas_call(vector_kernel, grid=(steps,), out_shape=(jax.ShapeDtypeStr...  11.1 us
    pallas_call x1, Pallas kernels, image_of(): pl.pallas_call(image_kernel, grid=(steps,), out_shape=(jax.ShapeDtypeStru...  10.6 us
    ppermute x9, waiting for transfers between devices, turned(): return lax.ppermute(x, axis, pairs)  10.5 us
  transfers between devices with their start and end apart: 18, of which 11 were waited for; matrix products, arithmetic and copies ran while one was open for 2% of the time, Pallas kernels for 10%

profile of v4, /device:TPU:1, one launch (start us, length us, event | category | flops | bytes accessed | tf_op | source)
XLA Modules:
  0.0 367.9 jit_solution(8145535901091037509)
XLA Ops:
  0.6 0.8 fusion
  1.4 3.3 collective-permute-start.1
  4.7 3.2 collective-permute-start
  7.9 4.0 %copy.16 = bf16[3,32,8,2048]{3,2,0,1:T(8,128)(2,1)} copy(bf16[3,32,8,2048]{3,2,1,0:T(8,128)(2,1)} %bitcast.16) | data formatting | bytes 6291456 | tf_op jit(solution)/shard_map/reshape | solution.py:586
  11.9 0.0 collective-permute-done.1.high_ref
  11.9 0.0 copy-start.4
  11.9 0.0 collective-permute-done.low_ref
  11.9 0.0 copy-start.5
  11.9 0.0 copy-start.2
  11.9 0.6 copy-done.4
  12.5 0.0 copy-done.5
  12.5 9.0 %all-to-all-start = ((bf16[32,24,2048]{2,1,0:T(8,128)(2,1)}), bf16[32,24,2048]{2,1,0:T(8,128)(2,1)S(1)}, u32[]{:S(2)}, u32[]{:S(2)}) async-start(bf16[32,24,2048]{2,1,0:T(8,128)(2,1)} %bitcast.17), calls=%async_computation | async-start | bytes 6291456 | tf_op jit(solution)/shard_map/all_to_all | solution.py:588
  21.5 0.0 copy-done.2
  21.5 0.8 reshape.43.pot_ref
  22.3 1.7 reshape.40.perm_ref
  24.0 19.0 %shard_map.106 = (s32[512,128]{1,0:T(8,128)}, s32[512,128]{1,0:T(8,128)}) custom-call(s32[256,256]{1,0:T(8,128)} %reshape.40.perm_ref, f32[128]{0:T(128)} %constant.28.clone.power_ref), custom_call_target="tpu_custom_call" | custom-call | flops 8589934592 | bytes 524288 | tf_op jit(solution)/shard_map/pallas_call | solution.py:102
  43.0 18.3 %all-to-all-done.x_ref = bf16[32,24,2048]{2,1,0:T(8,128)(2,1)S(1)} async-done(((bf16[32,24,2048]{2,1,0:T(8,128)(2,1)}), bf16[32,24,2048]{2,1,0:T(8,128)(2,1)S(1)}, u32[]{:S(2)}, u32[]{:S(2)}) %all-to-all-start) | async-done | bytes 3145760 | tf_op jit(solution)/shard_map/all_to_all | solution.py:588
  61.3 0.0 copy-start
  61.3 1.7 copy-done
  62.9 118.3 %shard_map.107 = bf16[128,24,512]{2,1,0:T(8,128)(2,1)} custom-call(bf16[32,24,2048]{2,1,0:T(8,128)(2,1)} %copy-done, s32[65536]{0:T(1024)} %bitcast.19, s32[65536]{0:T(1024)} %bitcast.20, f32[256,256]{1,0:T(8,128)} %reshape.43.pot_ref, bf16[256,256]{1,0:T(8,128)(2,1)} %surf_ref.1), custom_call_target="tpu_custom_call" | custom-call | flops 1610612736 | bytes 300000000 | tf_op jit(solution)/shard_map/pallas_call | solution.py:242
  181.3 0.0 copy-start.6
  181.3 7.9 %all-to-all-start.1 = ((bf16[128,24,512]{2,1,0:T(8,128)(2,1)}), bf16[128,24,512]{2,1,0:T(8,128)(2,1)S(1)}, u32[]{:S(2)}, u32[]{:S(2)}) async-start(bf16[128,24,512]{2,1,0:T(8,128)(2,1)} %shard_map.107), calls=%async_computation.1 | async-start | bytes 6291456 | tf_op jit(solution)/shard_map/all_to_all | solution.py:599
  189.2 0.0 copy-done.6
  189.3 0.6 subtract_reduce_fusion.column_ref
  189.9 7.7 %shard_map.104 = (bf16[2,24,16384]{2,1,0:T(8,128)(2,1)}, bf16[2,24,16384]{2,1,0:T(8,128)(2,1)}, bf16[2,24,16384]{2,1,0:T(8,128)(2,1)}, bf16[2,24,16384]{2,1,0:T(8,128)(2,1)}) custom-call(s32[1]{0:T(128)} %bitcast.1.rep_ref, bf16[24,65536]{1,0:T(8,128)(2,1)} %vecs_ref.1, bf16[24,512]{1,0:T(8,128)(2,1)} %copy-done.5, bf16[24,512]{1,0:T(8,128)(2,1)} %copy-done.4, ...), custom_call_target="tpu_custom_call" | custom-call | flops 9437184 | bytes 18874368 | tf_op jit(solution)/shard_map/pallas_call | solution.py:295
  197.6 3.3 collective-permute-start.2
  200.8 0.0 collective-permute-start.3
  200.8 0.8 collective-permute-start.4
  201.7 57.5 %collective-permute-done.2.refs_1_ = bf16[2,24,16384]{2,1,0:T(8,128)(2,1)} collective-permute-done((bf16[2,24,16384]{2,1,0:T(8,128)(2,1)}, bf16[2,24,16384]{2,1,0:T(8,128)(2,1)}, u32[]{:S(2)}, u32[]{:S(2)}) %collective-permute-start.2) | collective-permute-done | bytes 1572896 | tf_op jit(solution)/shard_map/ppermute | solution.py:594
  259.2 2.0 collective-permute-done.3.refs_2_
  261.2 33.7 %collective-permute-done.4.refs_3_ = bf16[2,24,16384]{2,1,0:T(8,128)(2,1)} collective-permute-done((bf16[2,24,16384]{2,1,0:T(8,128)(2,1)}, bf16[2,24,16384]{2,1,0:T(8,128)(2,1)}, u32[]{:S(2)}, u32[]{:S(2)}) %collective-permute-start.4) | collective-permute-done | bytes 1572896 | tf_op jit(solution)/shard_map/ppermute | solution.py:594
  294.9 11.1 %shard_map.105 = (bf16[96,16384]{1,0:T(8,128)(2,1)}, f32[96,16384]{1,0:T(8,128)}, f32[96,96]{1,0:T(8,128)}) custom-call(s32[1]{0:T(128)} %bitcast.1.rep_ref, bf16[2,24,16384]{2,1,0:T(8,128)(2,1)} %get-tuple-element.22.refs_0_, bf16[2,24,16384]{2,1,0:T(8,128)(2,1)} %collective-permute-done.2.refs_1_, bf16[2,24,16384]{2,1,0:T(8,128)(2,1)} %collective-permute-done.3.refs_2_, ...), custom_call_target="tpu_custom_call" | custom-call | flops 1811939328 | bytes 12582912 | tf_op jit(solution)/shard_map/pallas_call | solution.py:351
  306.0 0.0 all-to-all-done.1
  306.0 0.0 copy-start.1
  306.0 1.7 copy-done.1
  307.7 10.6 %shard_map.108 = (bf16[96,16384]{1,0:T(8,128)(2,1)}, f32[112,128]{1,0:T(8,128)}, f32[112,128]{1,0:T(8,128)}) custom-call(s32[1]{0:T(128)} %bitcast.core_ref, bf16[96,16384]{1,0:T(8,128)(2,1)} %get-tuple-element.26.vectors_ref, f32[96,16384]{1,0:T(8,128)} %get-tuple-element.27.kin_ref, f32[96,96]{1,0:T(8,128)} %get-tuple-element.28.vector_sums_ref, ...), custom_call_target="tpu_custom_call" | custom-call | flops 2415919104 | bytes 15728640 | tf_op jit(solution)/shard_map/pallas_call | solution.py:427
  318.3 0.5 collective-permute-start.5
  318.8 1.1 collective-permute-done.5
  319.9 0.8 add.36
  320.7 0.5 collective-permute-start.8
  321.2 1.0 collective-permute-start.7
  322.2 0.8 collective-permute-start.6
  323.0 0.8 collective-permute-done.8
  323.8 1.7 collective-permute-done.7
  325.5 1.4 collective-permute-done.6
  326.9 2.9 collective-permute-start.11
  329.8 0.0 collective-permute-start.10
  329.8 1.3 collective-permute-start.9
  331.0 0.0 collective-permute-done.11
  331.0 3.6 collective-permute-done.10
  334.6 0.0 collective-permute-done.9
  334.7 1.5 collective-permute-start.14
  336.1 0.1 collective-permute-start.13
  336.2 1.7 collective-permute-start.12
  337.9 0.0 collective-permute-done.14
  337.9 3.1 collective-permute-done.13
  341.0 0.0 collective-permute-done.12
  341.0 0.0 copy-start.3
  341.0 4.9 %collective-permute-start.15 = (f32[112,128]{1,0:T(8,128)S(1)}, f32[112,128]{1,0:T(8,128)S(1)}, u32[]{:S(2)}, u32[]{:S(2)}) collective-permute-start(f32[112,128]{1,0:T(8,128)S(1)} %add_add_fusion.mine_ref), channel_id=1, source_target_pairs={{0,1},{1,0},{2,3},{3,2},{4,5},{5,4},{6,7},{7,6},{8,9},{9,8},{10,11... | collective-permute-start | bytes 172040 | tf_op jit(solution)/shard_map/ppermute | solution.py:570
  345.9 0.9 collective-permute-done.15.other_ref
  346.8 0.0 copy-start.7
  346.8 0.0 copy-done.3
  346.8 0.6 copy-done.7
  347.4 20.4 %shard_map.109 = (f32[96,1,16384]{2,1,0:T(1,128)}, f32[96,96]{1,0:T(8,128)}) custom-call(s32[1]{0:T(128)} %bitcast.core_ref, f32[112,128]{1,0:T(8,128)} %copy-done.3, f32[112,128]{1,0:T(8,128)} %copy-done.7, bf16[96,16384]{1,0:T(8,128)(2,1)} %get-tuple-element.26.vectors_ref, bf16[96,16384]{1,0:T(8,128)(2,1)} %get-tuple-element.35.image_ref, f32[1,16384]{1,0:T(1,128)} %bitcast.23), custom_call_target="tpu_custom_call" | custom-call | flops 1811939328 | bytes 12582912 | tf_op jit(solution)/shard_map/pallas_call | solution.py:527
  (3 shorter events, 0.0 us)
Async XLA Ops:
  1.4 10.5 %collective-permute-start.1 = (bf16[24,512]{1,0:T(8,128)(2,1)S(1)}, bf16[24,512]{1,0:T(8,128)(2,1)S(1)}, u32[]{:S(2)}, u32[]{:S(2)}) collective-permute-start(bf16[24,512]{1,0:T(8,128)(2,1)S(1)} %get-tuple-element.42), channel_id=1, source_target_pairs={{1,0},{2,1},{3,2},{4,3},{5,4},{6,5},{7,6},{8,7},{9,8},{10,9},{11,1... | collective-permute-start | bytes 73736 | tf_op jit(solution)/shard_map/ppermute | solution.py:585
  4.7 7.2 %collective-permute-start = (bf16[24,512]{1,0:T(8,128)(2,1)S(1)}, bf16[24,512]{1,0:T(8,128)(2,1)S(1)}, u32[]{:S(2)}, u32[]{:S(2)}) collective-permute-start(bf16[24,512]{1,0:T(8,128)(2,1)S(1)} %get-tuple-element.43), channel_id=1, source_target_pairs={{0,1},{1,2},{2,3},{3,4},{4,5},{5,6},{6,7},{7,8},{8,9},{9,10},{10,1... | collective-permute-start | bytes 73736 | tf_op jit(solution)/shard_map/ppermute | solution.py:584
  11.9 0.6 copy-start.4
  11.9 0.6 copy-start.5
  11.9 9.6 %copy-start.2 = (f32[65536]{0:T(1024)S(1)}, f32[65536]{0:T(1024)}, u32[]{:S(2)}) copy-start(f32[65536]{0:T(1024)} %param.10) | copy-start | bytes 786436
  12.5 48.8 %all-to-all-start = ((bf16[32,24,2048]{2,1,0:T(8,128)(2,1)}), bf16[32,24,2048]{2,1,0:T(8,128)(2,1)S(1)}, u32[]{:S(2)}, u32[]{:S(2)}) async-start(bf16[32,24,2048]{2,1,0:T(8,128)(2,1)} %bitcast.17), calls=%async_computation | async-start | bytes 6291456 | tf_op jit(solution)/shard_map/all_to_all | solution.py:588
  61.3 1.7 copy-start
  181.3 8.0 %copy-start.6 = (s32[768,2]{0,1:T(2,128)S(1)}, s32[768,2]{0,1:T(2,128)}, u32[]{:S(2)}) copy-start(s32[768,2]{0,1:T(2,128)} %param.14) | copy-start | bytes 18436
  181.3 124.7 %all-to-all-start.1 = ((bf16[128,24,512]{2,1,0:T(8,128)(2,1)}), bf16[128,24,512]{2,1,0:T(8,128)(2,1)S(1)}, u32[]{:S(2)}, u32[]{:S(2)}) async-start(bf16[128,24,512]{2,1,0:T(8,128)(2,1)} %shard_map.107), calls=%async_computation.1 | async-start | bytes 6291456 | tf_op jit(solution)/shard_map/all_to_all | solution.py:599
  197.6 61.7 %collective-permute-start.2 = (bf16[2,24,16384]{2,1,0:T(8,128)(2,1)}, bf16[2,24,16384]{2,1,0:T(8,128)(2,1)}, u32[]{:S(2)}, u32[]{:S(2)}) collective-permute-start(bf16[2,24,16384]{2,1,0:T(8,128)(2,1)} %get-tuple-element.23), channel_id=1, source_target_pairs={{0,96},{32,0},{64,32},{96,64},{1,97},{33,1},{65,33},{97,65},{2,98}... | collective-permute-start | bytes 4718600 | tf_op jit(solution)/shard_map/ppermute | solution.py:594
  200.8 60.4 %collective-permute-start.3 = (bf16[2,24,16384]{2,1,0:T(8,128)(2,1)}, bf16[2,24,16384]{2,1,0:T(8,128)(2,1)}, u32[]{:S(2)}, u32[]{:S(2)}) collective-permute-start(bf16[2,24,16384]{2,1,0:T(8,128)(2,1)} %get-tuple-element.24), channel_id=1, source_target_pairs={{0,64},{32,96},{64,0},{96,32},{1,65},{33,97},{65,1},{97,33},{2,66}... | collective-permute-start | bytes 4718600 | tf_op jit(solution)/shard_map/ppermute | solution.py:594
  200.8 94.0 %collective-permute-start.4 = (bf16[2,24,16384]{2,1,0:T(8,128)(2,1)}, bf16[2,24,16384]{2,1,0:T(8,128)(2,1)}, u32[]{:S(2)}, u32[]{:S(2)}) collective-permute-start(bf16[2,24,16384]{2,1,0:T(8,128)(2,1)} %get-tuple-element.25), channel_id=1, source_target_pairs={{0,32},{32,64},{64,96},{96,0},{1,33},{33,65},{65,97},{97,1},{2,34}... | collective-permute-start | bytes 4718600 | tf_op jit(solution)/shard_map/ppermute | solution.py:594
  306.0 1.7 copy-start.1
  318.3 1.6 collective-permute-start.5
  320.7 3.0 collective-permute-start.8
  321.2 4.2 %collective-permute-start.7 = (f32[112,128]{1,0:T(8,128)S(1)}, f32[112,128]{1,0:T(8,128)S(1)}, u32[]{:S(2)}, u32[]{:S(2)}) collective-permute-start(f32[112,128]{1,0:T(8,128)S(1)} %add.36), channel_id=1, source_target_pairs={{0,32},{32,64},{64,96},{96,0},{1,33},{33,65},{65,97},{97,1},{2,34}... | collective-permute-start | bytes 172040 | tf_op jit(solution)/shard_map/ppermute | solution.py:563
  322.2 4.6 %collective-permute-start.6 = (f32[112,128]{1,0:T(8,128)S(1)}, f32[112,128]{1,0:T(8,128)S(1)}, u32[]{:S(2)}, u32[]{:S(2)}) collective-permute-start(f32[112,128]{1,0:T(8,128)S(1)} %add.36), channel_id=1, source_target_pairs={{0,64},{32,96},{64,0},{96,32},{1,65},{33,97},{65,1},{97,33},{2,66}... | collective-permute-start | bytes 172040 | tf_op jit(solution)/shard_map/ppermute | solution.py:563
  326.9 4.2 %collective-permute-start.11 = (f32[112,128]{1,0:T(8,128)S(1)}, f32[112,128]{1,0:T(8,128)S(1)}, u32[]{:S(2)}, u32[]{:S(2)}) collective-permute-start(f32[112,128]{1,0:T(8,128)S(1)} %add_add_fusion.2), channel_id=1, source_target_pairs={{0,24},{1,25},{2,26},{3,27},{4,28},{5,29},{6,30},{7,31},{8,0},{9,1... | collective-permute-start | bytes 172040 | tf_op jit(solution)/shard_map/ppermute | solution.py:563
  329.8 4.9 %collective-permute-start.10 = (f32[112,128]{1,0:T(8,128)S(1)}, f32[112,128]{1,0:T(8,128)S(1)}, u32[]{:S(2)}, u32[]{:S(2)}) collective-permute-start(f32[112,128]{1,0:T(8,128)S(1)} %add_add_fusion.2), channel_id=1, source_target_pairs={{0,8},{1,9},{2,10},{3,11},{4,12},{5,13},{6,14},{7,15},{8,16},{9,17... | collective-permute-start | bytes 172040 | tf_op jit(solution)/shard_map/ppermute | solution.py:563
  329.8 4.9 %collective-permute-start.9 = (f32[112,128]{1,0:T(8,128)S(1)}, f32[112,128]{1,0:T(8,128)S(1)}, u32[]{:S(2)}, u32[]{:S(2)}) collective-permute-start(f32[112,128]{1,0:T(8,128)S(1)} %add_add_fusion.2), channel_id=1, source_target_pairs={{0,16},{1,17},{2,18},{3,19},{4,20},{5,21},{6,22},{7,23},{8,24},{9,... | collective-permute-start | bytes 172040 | tf_op jit(solution)/shard_map/ppermute | solution.py:563
  334.7 3.2 collective-permute-start.14
  336.1 4.9 %collective-permute-start.13 = (f32[112,128]{1,0:T(8,128)S(1)}, f32[112,128]{1,0:T(8,128)S(1)}, u32[]{:S(2)}, u32[]{:S(2)}) collective-permute-start(f32[112,128]{1,0:T(8,128)S(1)} %add_add_fusion.1), channel_id=1, source_target_pairs={{0,2},{1,3},{2,4},{3,5},{4,6},{5,7},{6,0},{7,1},{8,10},{9,11},{10,... | collective-permute-start | bytes 172040 | tf_op jit(solution)/shard_map/ppermute | solution.py:563
  336.2 4.8 %collective-permute-start.12 = (f32[112,128]{1,0:T(8,128)S(1)}, f32[112,128]{1,0:T(8,128)S(1)}, u32[]{:S(2)}, u32[]{:S(2)}) collective-permute-start(f32[112,128]{1,0:T(8,128)S(1)} %add_add_fusion.1), channel_id=1, source_target_pairs={{0,4},{1,5},{2,6},{3,7},{4,0},{5,1},{6,2},{7,3},{8,12},{9,13},{10,... | collective-permute-start | bytes 172040 | tf_op jit(solution)/shard_map/ppermute | solution.py:563
  341.0 5.8 %copy-start.3 = (f32[112,128]{1,0:T(8,128)}, f32[112,128]{1,0:T(8,128)S(1)}, u32[]{:S(2)}) copy-start(f32[112,128]{1,0:T(8,128)S(1)} %add_add_fusion.mine_ref) | copy-start | bytes 172036
  341.0 5.8 %collective-permute-start.15 = (f32[112,128]{1,0:T(8,128)S(1)}, f32[112,128]{1,0:T(8,128)S(1)}, u32[]{:S(2)}, u32[]{:S(2)}) collective-permute-start(f32[112,128]{1,0:T(8,128)S(1)} %add_add_fusion.mine_ref), channel_id=1, source_target_pairs={{0,1},{1,0},{2,3},{3,2},{4,5},{5,4},{6,7},{7,6},{8,9},{9,8},{10,11... | collective-permute-start | bytes 172040 | tf_op jit(solution)/shard_map/ppermute | solution.py:570
  346.8 0.6 copy-start.7

commit v5 on v4

--- a/solution.py
+++ b/solution.py
@@ -145,13 +145,17 @@
     def run():
         for copy in copies:
             copy.wait()
-        gather(0, rows_refs[0])
-
-        @pl.loop(0, count // 2)
+        def gather_pair(i, rows_ref):
+            for k in range(2):
+                gather(2 * jnp.minimum(i, count // 2 - 1) + k, rows_ref.at[pl.ds(k * SPAN, SPAN), :])
+
+        gather_pair(0, rows_refs[0])
+
+        @pl.loop(0, count // 4)
         def _(j):
             for s in range(2):
                 i = j * 2 + s
-                gather(jnp.minimum(i + 1, count - 1), rows_refs[(s + 1) % 2])
+                gather_pair(i + 1, rows_refs[(s + 1) % 2])
                 work(i, rows_refs[s % 2])
 
     return begin, run
@@ -162,10 +166,12 @@
 
 
 def surface_kernel(
-    x_ref, perm_ref, back_ref, pot_ref, surf_ref, out_ref,
-    table_ref, packed_ref, even_ref, odd_ref, *rest
+    arrived_ref, perm_ref, back_ref, pot_ref, surf_ref, out_ref,
+    x_ref, x_sem, table_ref, packed_ref, even_ref, odd_ref, *rest
 ):
     streams, sem = rest[:-1], rest[-1]
+    arrival = pltpu.make_async_copy(arrived_ref, x_ref, x_sem)
+    arrival.start()
     pieces, vecs, width = x_ref.shape
     points = table_ref.shape[0]
     per_group = pieces // GROUPS
@@ -179,9 +185,11 @@
     count = points // SPAN
     blocks = points // BLK
 
-    def folded(rows_ref):
-        wide = jnp.concatenate([rows_ref[q * BLK:(q + 1) * BLK, :] for q in range(GROUPS)], axis=1)
-        return dot_nt(fold, wide)
+    def folded(rows_ref, k):
+        wide = jnp.concatenate([
+            rows_ref[k * SPAN + q * BLK:k * SPAN + (q + 1) * BLK, :] for q in range(GROUPS)
+        ], axis=1)
+        return dot_nt(fold, wide).astype(jnp.bfloat16)
 
     def spread(rows, starts):
         for q in range(GROUPS):
@@ -190,26 +198,30 @@
             )
 
     def to_grid_and_back(i, rows_ref):
-        values = folded(rows_ref).astype(jnp.bfloat16)
+        values = jnp.concatenate([folded(rows_ref, k) for k in range(2)], axis=0)
         projected = jnp.dot(values, surf_ref[...], preferred_element_type=jnp.float32)
+        held = blocks_of(2 * i, blocks) + blocks_of(2 * i + 1, blocks)
         weighted = jnp.concatenate([
             projected[q * PAD:(q + 1) * PAD] * pot_ref[pl.ds(block, 1), :]
-            for q, block in enumerate(blocks_of(i, blocks))
+            for q, block in enumerate(held)
         ], axis=0).astype(jnp.bfloat16)
         returned = dot_nt(surf_ref[...], weighted).astype(jnp.bfloat16).astype(jnp.float32)
-        packed_ref[pl.ds(pl.multiple_of(i * BLK, BLK), BLK), :] = returned
+        for k in range(2):
+            start = pl.multiple_of((2 * i + k) * BLK, BLK)
+            packed_ref[pl.ds(start, BLK), :] = returned[:, k * LANES:(k + 1) * LANES]
 
     def to_basis(i, rows_ref):
-        values = folded(rows_ref).astype(jnp.bfloat16)
         per_piece = out_ref.shape[2] // BLK
-        for q in range(GROUPS):
-            at = (q // per_piece) * BLK
-            out_ref[i + (q % per_piece) * (out_ref.shape[0] // per_piece), :, at:at + BLK] = values[
-                q * PAD:q * PAD + vecs
-            ]
+        for k in range(2):
+            values = folded(rows_ref, k)
+            for q in range(GROUPS):
+                at = (q // per_piece) * BLK
+                piece = 2 * i + k + (q % per_piece) * (out_ref.shape[0] // per_piece)
+                out_ref[piece, :, at:at + BLK] = values[q * PAD:q * PAD + vecs]
 
     begin, run = stream(perm_ref, streams, sem, table_ref, (even_ref, odd_ref), to_grid_and_back)
     begin()
+    arrival.wait()
     chunk = 512
 
     @pl.loop(0, per_group)
@@ -242,13 +254,15 @@
     return pl.pallas_call(
         surface_kernel,
         out_shape=jax.ShapeDtypeStruct((pieces * reps, vecs, width // reps), jnp.bfloat16),
-        in_specs=[WHOLE] * 5,
+        in_specs=[pl.BlockSpec(memory_space=pl.ANY)] + [WHOLE] * 4,
         out_specs=WHOLE,
         scratch_shapes=[
+            pltpu.VMEM(arrived.shape, jnp.bfloat16),
+            pltpu.SemaphoreType.DMA,
             pltpu.VMEM((points, LANES), jnp.float32),
             pltpu.VMEM((points // GROUPS, LANES), jnp.float32),
-            pltpu.VMEM((SPAN, LANES), jnp.bfloat16),
-            pltpu.VMEM((SPAN, LANES), jnp.bfloat16),
+            pltpu.VMEM((2 * SPAN, LANES), jnp.bfloat16),
+            pltpu.VMEM((2 * SPAN, LANES), jnp.bfloat16),
         ] + [pltpu.SMEM((4 * BLK,), jnp.int32)] * 64 + [pltpu.SemaphoreType.DMA((64,))],
         compiler_params=pltpu.CompilerParams(vmem_limit_bytes=VMEM_LIMIT),
         cost_estimate=pl.CostEstimate(
@@ -257,12 +271,12 @@
     )(arrived, perm, back, potential.reshape(-1, BLK), surface)
 
 
-def source_kernel(rep_ref, vecs_ref, low_ref, high_ref, column_ref, weight_ref, *rest):
-    outs, wide_ref = rest[:-1], rest[-1]
-    reps = len(outs)
+def source_kernel(vecs_ref, low_ref, high_ref, column_ref, weight_ref, out_ref, wide_ref):
+    reps = out_ref.shape[0]
     edge = low_ref.shape[1]
     rows = vecs_ref.shape[1]
     blocks = rows // BLK
+    piece_blocks = out_ref.shape[3] * reps // (blocks * BLK)
     wide_ref[:, 0:edge] = low_ref[...]
     wide_ref[:, edge + rows:] = high_ref[...]
     per_piece = 8
@@ -275,42 +289,40 @@
 
     @pl.loop(0, blocks // per_piece)
     def _(j):
-        for s in range(reps):
-            to_rep = (rep_ref[0] + (reps - s)) % reps
-            for h in range(per_rep):
-                a = j * per_piece + to_rep * per_rep + h
-                total = None
-                for m in range(COUPLINGS_PER_ROW):
-                    c = a * COUPLINGS_PER_ROW + m
-                    at = pl.multiple_of(column_ref[c] * BLK, BLK)
-                    term = wide_ref[:, pl.ds(at, BLK)].astype(jnp.float32) * weight_ref[c]
-                    total = term if total is None else total + term
-                to = pl.ds(pl.multiple_of((j * per_rep + h) * BLK, BLK), BLK)
-                outs[s][0, :, to] = vecs_ref[:, pl.ds(pl.multiple_of(a * BLK, BLK), BLK)]
-                outs[s][1, :, to] = total.astype(jnp.bfloat16)
-
-
-def source_of(rep, basis_vecs, low, high, columns, weights, reps):
+        for k in range(per_piece):
+            a = j * per_piece + k
+            total = None
+            for m in range(COUPLINGS_PER_ROW):
+                c = a * COUPLINGS_PER_ROW + m
+                at = pl.multiple_of(column_ref[c] * BLK, BLK)
+                term = wide_ref[:, pl.ds(at, BLK)].astype(jnp.float32) * weight_ref[c]
+                total = term if total is None else total + term
+            to = pl.ds(pl.multiple_of(j * per_rep * BLK, per_rep * BLK) + (k % per_rep) * BLK, BLK)
+            here = pl.multiple_of(a * BLK, BLK)
+            out_ref[k // per_rep, 0, :, to] = vecs_ref[:, pl.ds(here, BLK)]
+            out_ref[k // per_rep, 1, :, to] = total.astype(jnp.bfloat16)
+
+
+def source_of(basis_vecs, low, high, columns, weights, reps):
     vecs, rows = basis_vecs.shape
     return pl.pallas_call(
         source_kernel,
-        out_shape=(jax.ShapeDtypeStruct((2, vecs, rows // reps), jnp.bfloat16),) * reps,
-        in_specs=[SCALARS, WHOLE, WHOLE, WHOLE, SCALARS, SCALARS],
-        out_specs=(WHOLE,) * reps,
+        out_shape=jax.ShapeDtypeStruct((reps, 2, vecs, rows // reps), jnp.bfloat16),
+        in_specs=[WHOLE, WHOLE, WHOLE, SCALARS, SCALARS],
+        out_specs=WHOLE,
         scratch_shapes=[pltpu.VMEM((vecs, rows + 2 * low.shape[1]), jnp.bfloat16)],
         compiler_params=pltpu.CompilerParams(vmem_limit_bytes=VMEM_LIMIT),
         cost_estimate=pl.CostEstimate(
             flops=6 * vecs * rows, bytes_accessed=12 * vecs * rows, transcendentals=0
         ),
-    )(rep, basis_vecs, low, high, columns, weights)
-
-
-def vector_kernel(rep_ref, *refs):
-    parts = refs[:-6]
-    kinetic_ref, precond_ref, vectors_ref, kin_ref, sums_ref, total_ref = refs[-6:]
+    )(basis_vecs, low, high, columns, weights)
+
+
+def vector_kernel(
+    moved_ref, kinetic_ref, precond_ref, vectors_ref, kin_ref, sums_ref, total_ref
+):
     step = pl.program_id(0)
-    reps = len(parts)
-    _, vecs, width = parts[0].shape
+    reps, _, vecs, width = moved_ref.shape
     count = reps * vecs
 
     @pl.when(step == 0)
@@ -318,11 +330,7 @@
         total_ref[...] = jnp.zeros_like(total_ref)
 
     def ordered(k):
-        for s, part in enumerate(parts):
-            group = (rep_ref[0] + s) % reps
-            start = pl.multiple_of(group * vecs, 8)
-            kin_ref[pl.ds(start, vecs), :] = part[k].astype(jnp.float32)
-        return kin_ref[...]
+        return jnp.concatenate([moved_ref[b, k].astype(jnp.float32) for b in range(reps)], axis=0)
 
     vectors = ordered(0)
     vectors_16 = vectors.astype(jnp.bfloat16)
@@ -343,9 +351,8 @@
         )
 
 
-def vectors_of(rep, parts, kinetic, precond, steps):
-    reps = len(parts)
-    _, vecs, rows = parts[0].shape
+def vectors_of(moved, kinetic, precond, steps):
+    reps, _, vecs, rows = moved.shape
     width = rows // steps
     count = reps * vecs
     return pl.pallas_call(
@@ -356,7 +363,8 @@
             jax.ShapeDtypeStruct((count, rows), jnp.float32),
             jax.ShapeDtypeStruct((count, count), jnp.float32),
         ),
-        in_specs=[SCALARS] + [pl.BlockSpec((2, vecs, width), lambda i: (0, 0, i))] * reps + [
+        in_specs=[
+            pl.BlockSpec((reps, 2, vecs, width), lambda i: (0, 0, 0, i)),
             pl.BlockSpec((BLK, BLK), lambda i: (0, 0)),
             pl.BlockSpec((1, width), lambda i: (0, i)),
         ],
@@ -370,7 +378,7 @@
         cost_estimate=pl.CostEstimate(
             flops=12 * count * count * rows, bytes_accessed=8 * count * rows, transcendentals=0
         ),
-    )(rep, *parts, kinetic, precond)
+    )(moved, kinetic, precond)
 
 
 def image_kernel(
@@ -488,26 +496,28 @@
         cross = dot_exact(mixed, rayleigh)
         last = dot_exact(turned, dot_exact(vector, rayleigh))
         gram = (own - cross - cross.T + last) / full_rows
-        pad = jnp.zeros((count, LANES - count), jnp.float32)
-        row, column = iota((count, LANES), 0), iota((count, LANES), 1)
-        left = jnp.concatenate([gram, pad], axis=1)
-        right = jnp.where(row == column, 1.0, 0.0)
-        for j in range(0, count, 2):
-            first, second = left[j:j + 1, :], left[j + 1:j + 2, :]
-            a, b, c = first[:, j:j + 1], first[:, j + 1:j + 2], second[:, j + 1:j + 2]
-            over = 1.0 / (a * c - b * b)
-            below = row[:, 0:1] > j + 1
-            one, two = left[:, j:j + 1], left[:, j + 1:j + 2]
-            ratio_one = jnp.where(below, (one * c - two * b) * over, 0.0)
-            ratio_two = jnp.where(below, (two * a - one * b) * over, 0.0)
-            left = left - (ratio_one * first + ratio_two * second)
-            right = right - (ratio_one * right[j:j + 1, :] + ratio_two * right[j + 1:j + 2, :])
-        diagonal = jnp.sum(jnp.where(row == column, left, 0.0), axis=1, keepdims=True)
-        beside = jnp.sum(jnp.where(row == column + 1, left, 0.0), axis=1, keepdims=True)
-        diagonal = jnp.broadcast_to(diagonal, left.shape)
-        ratio = jnp.where(row % 2 == 1, beside / pltpu.roll(diagonal, 1, 0), 0.0)
-        right = right - ratio * pltpu.roll(right, 1, 0)
-        inverse = (right * lax.rsqrt(diagonal - ratio * beside))[:, 0:count]
+        pad = jnp.zeros((8, LANES - count), jnp.float32)
+        row, column = iota((8, LANES), 0), iota((8, LANES), 1)
+        left, right = [], []
+        for k in range(0, count, 8):
+            left.append(jnp.concatenate([gram[k:k + 8, :], pad], axis=1))
+            right.append(jnp.where(row + k == column, 1.0, 0.0))
+        for j in range(count):
+            own, at = j // 8, j % 8
+            over = 1.0 / left[own][at:at + 1, j:j + 1]
+            pivot_left = left[own][at:at + 1, :] * over
+            pivot_right = right[own][at:at + 1, :] * over
+            for k in range(own, count // 8):
+                ratio = left[k][:, j:j + 1]
+                if k == own:
+                    ratio = jnp.where(row[:, 0:1] > at, ratio, 0.0)
+                left[k] = left[k] - ratio * pivot_left
+                right[k] = right[k] - ratio * pivot_right
+        scaled = []
+        for k in range(count // 8):
+            pivots = jnp.where(row + k * 8 == column, left[k], 0.0)
+            scaled.append(right[k] * lax.rsqrt(jnp.sum(pivots, axis=1, keepdims=True)))
+        inverse = jnp.concatenate(scaled, axis=0)[:, 0:count]
         parts = three_parts(inverse) + three_parts(-dot_exact(inverse, turned))
         for k in range(3):
             mix_ref[k * count:(k + 1) * count, 0:count] = parts[k]
@@ -584,26 +594,23 @@
     low = lax.ppermute(basis_vecs[:, rows - edge:], "row", forward)
     high = lax.ppermute(basis_vecs[:, :edge], "row", backward)
     by_piece = basis_vecs.reshape(vecs, pieces, width).transpose(1, 0, 2)
-    by_piece, low, high, perm = lax.optimization_barrier((by_piece, low, high, grid_perm))
     arrived = lax.all_to_all(by_piece, "row", split_axis=0, concat_axis=0, tiled=True)
     columns = couplings[:, 1] - (lax.axis_index("row") * blocks - HB)
-    rep = lax.axis_index("rep").reshape(1)
-    core = (lax.axis_index("row") % 2).reshape(1)
-    parts = source_of(rep, basis_vecs, low, high, columns, coupling_coefficient, reps)
-    parts = [
-        part if s == 0 else lax.ppermute(part, "rep", [(i, (i - s) % reps) for i in range(reps)])
-        for s, part in enumerate(parts)
-    ]
-    out, back = index_streams(perm, reps)
+    by_rep = source_of(basis_vecs, low, high, columns, coupling_coefficient, reps)
+    out, back = index_streams(grid_perm, reps)
+    by_rep, out, back = lax.optimization_barrier((by_rep, out, back))
+    moved = lax.all_to_all(by_rep, "rep", split_axis=0, concat_axis=0, tiled=True)
     restored = surface_pass(arrived, out, back, potential, surface, reps)
+    restored, moved = lax.optimization_barrier((restored, moved))
     pot = lax.all_to_all(restored, ("rep", "row"), split_axis=0, concat_axis=0, tiled=True)
     pot = pot.reshape(reps, pieces, vecs, width // reps)
     scale = precond.reshape(1, -1)
-    vectors, kin, vector_sums = vectors_of(rep, parts, kinetic, scale, 8)
-    image, keep, give = image_of(core, vectors, kin, vector_sums, pot, scale, 8)
+    core = (lax.axis_index("row") % 2).reshape(1)
+    vectors, kin, vector_sums = vectors_of(moved, kinetic, scale, 4)
+    image, keep, give = image_of(core, vectors, kin, vector_sums, pot, scale, 4)
     mine, other = sum_over_devices(keep, give)
     solved, rayleigh = solved_of(
-        core, mine, other, vectors, image, scale, float(rows * pieces), reps, 8
+        core, mine, other, vectors, image, scale, float(rows * pieces), reps, 4
     )
     return (solved.reshape(reps * vecs, 1, 1, -1), rayleigh)
 

time: 369 us -> 285 us (0.77)
  waiting for transfers between devices: 124 us -> 58.9 us
  Pallas kernels: 187 us -> 172 us
    ppermute x3 -> x0, waiting for transfers between devices: 93.2 us -> none  [body(): lax.ppermute(part, 'rep', [(i, (i - s) % reps) for i in range(reps)])]
    all_to_all x1, waiting for transfers between devices: 0.01 us -> 33.4 us  [body(): lax.all_to_all(restored, ('rep', 'row'), split_axis=0, concat_axis=0, til...]
    all_to_all x1, waiting for transfers between devices: 18.3 us -> 0.01 us  [body(): lax.all_to_all(by_piece, 'row', split_axis=0, concat_axis=0, tiled=True)]
    ppermute x1, waiting for transfers between devices: 0.01 us -> 10.8 us  [body(): high = lax.ppermute(basis_vecs[:, :edge], 'row', backward)]
    pallas_call x1, Pallas kernels: 118 us -> 111 us  [surface_pass(): pl.pallas_call(surface_kernel, out_shape=jax.ShapeDtypeStruct((pieces * r...]
    all_to_all x0 -> x1, starting transfers between devices: none -> 5.29 us  [body(): lax.all_to_all(by_rep, 'rep', split_axis=0, concat_axis=0, tiled=True)]
    ppermute x3 -> x0, starting transfers between devices: 4.14 us -> none  [body(): lax.ppermute(part, 'rep', [(i, (i - s) % reps) for i in range(reps)])]
    pallas_call x1, Pallas kernels: 20.4 us -> 16.5 us  [solved_of(): pl.pallas_call(functools.partial(solve_kernel, full_rows, reps), grid=(st...]
  transfers between devices with their start and end apart: 18 -> 16, of which waited for: 11 -> 13; matrix products, arithmetic and copies ran while one was open for 2% -> 1% of each run, Pallas kernels for 10% -> 51%
where the time goes in v5:
time: 285 us; the launch traced here: 284 us
  Pallas kernels  172 us (60%)
  waiting for transfers between devices  58.9 us (21%)
  starting transfers between devices  40.2 us (14%)
  local copies, waits for them, and re-layouts  11.5 us (4%)
    pallas_call x1, Pallas kernels, surface_pass(): pl.pallas_call(surface_kernel, out_shape=jax.ShapeDtypeStruct((pieces * r...  111 us
    all_to_all x1, waiting for transfers between devices, body(): lax.all_to_all(restored, ('rep', 'row'), split_axis=0, concat_axis=0, til...  33.4 us
    pallas_call x1, Pallas kernels, index_streams(): pl.pallas_call(functools.partial(inverse_kernel, reps), out_shape=(stream...  19.1 us
    pallas_call x1, Pallas kernels, solved_of(): pl.pallas_call(functools.partial(solve_kernel, full_rows, reps), grid=(st...  16.5 us
    ppermute x9, waiting for transfers between devices, turned(): return lax.ppermute(x, axis, pairs)  12.7 us
    ppermute x1, waiting for transfers between devices, body(): high = lax.ppermute(basis_vecs[:, :edge], 'row', backward)  10.8 us
    pallas_call x1, Pallas kernels, image_of(): pl.pallas_call(image_kernel, grid=(steps,), out_shape=(jax.ShapeDtypeStru...  8.93 us
    all_to_all x1, starting transfers between devices, body(): lax.all_to_all(restored, ('rep', 'row'), split_axis=0, concat_axis=0, til...  8.79 us
  transfers between devices with their start and end apart: 16, of which 13 were waited for; matrix products, arithmetic and copies ran while one was open for 1% of the time, Pallas kernels for 51%

profile of v5, /device:TPU:1, one launch (start us, length us, event | category | flops | bytes accessed | tf_op | source)
XLA Modules:
  0.0 284.5 jit_solution(4576147403824644494)
XLA Ops:
  0.6 3.9 %copy.16 = bf16[3,32,8,2048]{3,2,0,1:T(8,128)(2,1)} copy(bf16[3,32,8,2048]{3,2,1,0:T(8,128)(2,1)} %bitcast.15) | data formatting | bytes 6291456 | tf_op jit(solution)/shard_map/reshape | solution.py:596
  4.6 0.0 copy-start.2
  4.6 8.7 %all-to-all-start = ((bf16[32,24,2048]{2,1,0:T(8,128)(2,1)}), bf16[32,24,2048]{2,1,0:T(8,128)(2,1)S(1)}, u32[]{:S(2)}, u32[]{:S(2)}) async-start(bf16[32,24,2048]{2,1,0:T(8,128)(2,1)} %bitcast.16), calls=%async_computation | async-start | bytes 6291456 | tf_op jit(solution)/shard_map/all_to_all | solution.py:597
  13.3 0.8 fusion
  14.1 2.1 collective-permute-start.1
  16.2 3.4 %collective-permute-start = (bf16[24,512]{1,0:T(8,128)(2,1)S(1)}, bf16[24,512]{1,0:T(8,128)(2,1)S(1)}, u32[]{:S(2)}, u32[]{:S(2)}) collective-permute-start(bf16[24,512]{1,0:T(8,128)(2,1)S(1)} %get-tuple-element.37), channel_id=1, source_target_pairs={{0,1},{1,2},{2,3},{3,4},{4,5},{5,6},{6,7},{7,8},{8,9},{9,10},{10,1... | collective-permute-start | bytes 73736 | tf_op jit(solution)/shard_map/ppermute | solution.py:594
  19.6 0.0 copy-done.2
  19.6 0.8 reshape.35.perm_ref
  20.4 0.0 copy-start.7
  20.4 19.1 %shard_map.105 = (s32[512,128]{1,0:T(8,128)}, s32[512,128]{1,0:T(8,128)}) custom-call(s32[256,256]{1,0:T(8,128)} %reshape.35.perm_ref, f32[128]{0:T(128)} %constant.23.clone.power_ref), custom_call_target="tpu_custom_call" | custom-call | flops 8589934592 | bytes 524288 | tf_op jit(solution)/shard_map/pallas_call | solution.py:102
  39.5 0.0 copy-done.7
  39.5 0.6 subtract_reduce_fusion.column_ref
  40.1 10.8 %collective-permute-done.1.high_ref = bf16[24,512]{1,0:T(8,128)(2,1)S(1)} collective-permute-done((bf16[24,512]{1,0:T(8,128)(2,1)S(1)}, bf16[24,512]{1,0:T(8,128)(2,1)S(1)}, u32[]{:S(2)}, u32[]{:S(2)}) %collective-permute-start.1) | collective-permute-done | bytes 24608 | tf_op jit(solution)/shard_map/ppermute | solution.py:595
  50.9 0.0 copy-start.5
  50.9 0.0 collective-permute-done.low_ref
  50.9 0.6 copy-done.5
  51.5 0.0 copy-start.6
  51.5 0.6 copy-done.6
  52.1 7.4 %shard_map.104 = bf16[4,2,24,16384]{3,2,1,0:T(8,128)(2,1)} custom-call(bf16[24,65536]{1,0:T(8,128)(2,1)} %vecs_ref.1, bf16[24,512]{1,0:T(8,128)(2,1)} %copy-done.6, bf16[24,512]{1,0:T(8,128)(2,1)} %copy-done.5, s32[768]{0:T(1024)} %subtract_reduce_fusion.column_ref, f32[768]{0:T(1024)} %weight_ref.1), custom_call_target="tpu_custom_call" | custom-call | flops 9437184 | bytes 18874368 | tf_op jit(solution)/shard_map/pallas_call | solution.py:308
  59.4 0.0 copy-start.3
  59.4 0.0 all-to-all-done.arrived_ref
  59.4 0.0 copy-start
  59.5 1.7 copy-done
  61.2 5.3 %all-to-all-start.1 = ((bf16[4,2,24,16384]{3,2,1,0:T(8,128)(2,1)}), bf16[4,2,24,16384]{3,2,1,0:T(8,128)(2,1)}, u32[]{:S(2)}, u32[]{:S(2)}) async-start(bf16[4,2,24,16384]{3,2,1,0:T(8,128)(2,1)} %shard_map.104), calls=%async_computation.1 | async-start | bytes 12582912 | tf_op jit(solution)/shard_map/all_to_all | solution.py:602
  66.5 0.0 copy-done.3
  66.5 0.8 reshape.38.pot_ref
  67.2 111.3 %shard_map.106 = bf16[128,24,512]{2,1,0:T(8,128)(2,1)} custom-call(bf16[32,24,2048]{2,1,0:T(8,128)(2,1)} %copy-done, s32[65536]{0:T(1024)} %bitcast.18, s32[65536]{0:T(1024)} %bitcast.19, f32[256,256]{1,0:T(8,128)} %reshape.38.pot_ref, bf16[256,256]{1,0:T(8,128)(2,1)} %surf_ref.1), custom_call_target="tpu_custom_call" | custom-call | flops 1610612736 | bytes 300000000 | tf_op jit(solution)/shard_map/pallas_call | solution.py:254
  178.5 0.0 all-to-all-done.1.moved_ref
  178.5 8.8 %all-to-all-start.2 = ((bf16[128,24,512]{2,1,0:T(8,128)(2,1)}), bf16[128,24,512]{2,1,0:T(8,128)(2,1)S(1)}, u32[]{:S(2)}, u32[]{:S(2)}) async-start(bf16[128,24,512]{2,1,0:T(8,128)(2,1)} %shard_map.106), calls=%async_computation.2 | async-start | bytes 6291456 | tf_op jit(solution)/shard_map/all_to_all | solution.py:605
  187.3 8.5 %shard_map.107 = (bf16[96,16384]{1,0:T(8,128)(2,1)}, f32[96,16384]{1,0:T(8,128)}, f32[96,96]{1,0:T(8,128)}) custom-call(bf16[4,2,24,16384]{3,2,1,0:T(8,128)(2,1)} %all-to-all-done.1.moved_ref, bf16[256,256]{1,0:T(8,128)(2,1)} %kinetic_ref.1, f32[1,16384]{1,0:T(1,128)} %bitcast.20), custom_call_target="tpu_custom_call" | custom-call | flops 1811939328 | bytes 12582912 | tf_op jit(solution)/shard_map/pallas_call | solution.py:358
  195.8 33.4 %all-to-all-done.2 = bf16[128,24,512]{2,1,0:T(8,128)(2,1)S(1)} async-done(((bf16[128,24,512]{2,1,0:T(8,128)(2,1)}), bf16[128,24,512]{2,1,0:T(8,128)(2,1)S(1)}, u32[]{:S(2)}, u32[]{:S(2)}) %all-to-all-start.2) | async-done | bytes 3145760 | tf_op jit(solution)/shard_map/all_to_all | solution.py:605
  229.2 0.0 copy-start.1
  229.2 1.7 copy-done.1
  230.9 8.9 %shard_map.108 = (bf16[96,16384]{1,0:T(8,128)(2,1)}, f32[112,128]{1,0:T(8,128)}, f32[112,128]{1,0:T(8,128)}) custom-call(s32[1]{0:T(128)} %bitcast.core_ref, bf16[96,16384]{1,0:T(8,128)(2,1)} %get-tuple-element.23.vectors_ref, f32[96,16384]{1,0:T(8,128)} %get-tuple-element.24.kin_ref, f32[96,96]{1,0:T(8,128)} %get-tuple-element.25.vector_sums_ref, ...), custom_call_target="tpu_custom_call" | custom-call | flops 2415919104 | bytes 15728640 | tf_op jit(solution)/shard_map/pallas_call | solution.py:435
  239.8 0.9 collective-permute-start.2
  240.7 1.1 collective-permute-done.2
  241.8 0.8 add.36
  242.7 0.4 collective-permute-start.5
  243.0 1.1 collective-permute-start.4
  244.1 0.7 collective-permute-start.3
  244.8 0.9 collective-permute-done.5
  245.7 1.6 collective-permute-done.4
  247.3 1.5 collective-permute-done.3
  248.8 0.9 collective-permute-start.8
  249.7 0.7 collective-permute-start.7
  250.3 0.6 collective-permute-start.6
  250.9 0.9 collective-permute-done.8
  251.9 2.0 collective-permute-done.7
  253.9 1.5 collective-permute-done.6
  255.4 0.1 collective-permute-start.11
  255.5 1.5 collective-permute-start.10
  256.9 0.2 collective-permute-start.9
  257.2 1.3 collective-permute-done.11
  258.5 1.3 collective-permute-done.10
  259.8 1.7 collective-permute-done.9
  261.5 0.0 copy-start.4
  261.5 4.9 %collective-permute-start.12 = (f32[112,128]{1,0:T(8,128)S(1)}, f32[112,128]{1,0:T(8,128)S(1)}, u32[]{:S(2)}, u32[]{:S(2)}) collective-permute-start(f32[112,128]{1,0:T(8,128)S(1)} %add_add_fusion.mine_ref), channel_id=1, source_target_pairs={{0,1},{1,0},{2,3},{3,2},{4,5},{5,4},{6,7},{7,6},{8,9},{9,8},{10,11... | collective-permute-start | bytes 172040 | tf_op jit(solution)/shard_map/ppermute | solution.py:580
  266.4 0.9 collective-permute-done.12.other_ref
  267.3 0.0 copy-start.8
  267.3 0.0 copy-done.4
  267.3 0.6 copy-done.8
  267.9 16.5 %shard_map.109 = (f32[96,1,16384]{2,1,0:T(1,128)}, f32[96,96]{1,0:T(8,128)}) custom-call(s32[1]{0:T(128)} %bitcast.core_ref, f32[112,128]{1,0:T(8,128)} %copy-done.4, f32[112,128]{1,0:T(8,128)} %copy-done.8, bf16[96,16384]{1,0:T(8,128)(2,1)} %get-tuple-element.23.vectors_ref, bf16[96,16384]{1,0:T(8,128)(2,1)} %get-tuple-element.29.image_ref, f32[1,16384]{1,0:T(1,128)} %bitcast.22), custom_call_target="tpu_custom_call" | custom-call | flops 1811939328 | bytes 12582912 | tf_op jit(solution)/shard_map/pallas_call | solution.py:537
  (3 shorter events, 0.0 us)
Async XLA Ops:
  4.6 15.1 %copy-start.2 = (s32[65536]{0:T(1024)S(1)}, s32[65536]{0:T(1024)}, u32[]{:S(2)}) copy-start(s32[65536]{0:T(1024)} %param.12) | copy-start | bytes 786436
  4.6 54.9 %all-to-all-start = ((bf16[32,24,2048]{2,1,0:T(8,128)(2,1)}), bf16[32,24,2048]{2,1,0:T(8,128)(2,1)S(1)}, u32[]{:S(2)}, u32[]{:S(2)}) async-start(bf16[32,24,2048]{2,1,0:T(8,128)(2,1)} %bitcast.16), calls=%async_computation | async-start | bytes 6291456 | tf_op jit(solution)/shard_map/all_to_all | solution.py:597
  14.1 36.8 %collective-permute-start.1 = (bf16[24,512]{1,0:T(8,128)(2,1)S(1)}, bf16[24,512]{1,0:T(8,128)(2,1)S(1)}, u32[]{:S(2)}, u32[]{:S(2)}) collective-permute-start(bf16[24,512]{1,0:T(8,128)(2,1)S(1)} %get-tuple-element.36), channel_id=1, source_target_pairs={{1,0},{2,1},{3,2},{4,3},{5,4},{6,5},{7,6},{8,7},{9,8},{10,9},{11,1... | collective-permute-start | bytes 73736 | tf_op jit(solution)/shard_map/ppermute | solution.py:595
  16.2 34.7 %collective-permute-start = (bf16[24,512]{1,0:T(8,128)(2,1)S(1)}, bf16[24,512]{1,0:T(8,128)(2,1)S(1)}, u32[]{:S(2)}, u32[]{:S(2)}) collective-permute-start(bf16[24,512]{1,0:T(8,128)(2,1)S(1)} %get-tuple-element.37), channel_id=1, source_target_pairs={{0,1},{1,2},{2,3},{3,4},{4,5},{5,6},{6,7},{7,8},{8,9},{9,10},{10,1... | collective-permute-start | bytes 73736 | tf_op jit(solution)/shard_map/ppermute | solution.py:594
  20.4 19.1 %copy-start.7 = (s32[768,2]{0,1:T(2,128)S(1)}, s32[768,2]{0,1:T(2,128)}, u32[]{:S(2)}) copy-start(s32[768,2]{0,1:T(2,128)} %param.14) | copy-start | bytes 18436
  50.9 0.6 copy-start.5
  51.5 0.6 copy-start.6
  59.4 7.0 %copy-start.3 = (f32[65536]{0:T(1024)S(1)}, f32[65536]{0:T(1024)}, u32[]{:S(2)}) copy-start(f32[65536]{0:T(1024)} %param.10) | copy-start | bytes 786436
  59.4 1.7 copy-start
  61.2 117.3 %all-to-all-start.1 = ((bf16[4,2,24,16384]{3,2,1,0:T(8,128)(2,1)}), bf16[4,2,24,16384]{3,2,1,0:T(8,128)(2,1)}, u32[]{:S(2)}, u32[]{:S(2)}) async-start(bf16[4,2,24,16384]{3,2,1,0:T(8,128)(2,1)} %shard_map.104), calls=%async_computation.1 | async-start | bytes 12582912 | tf_op jit(solution)/shard_map/all_to_all | solution.py:602
  178.5 50.7 %all-to-all-start.2 = ((bf16[128,24,512]{2,1,0:T(8,128)(2,1)}), bf16[128,24,512]{2,1,0:T(8,128)(2,1)S(1)}, u32[]{:S(2)}, u32[]{:S(2)}) async-start(bf16[128,24,512]{2,1,0:T(8,128)(2,1)} %shard_map.106), calls=%async_computation.2 | async-start | bytes 6291456 | tf_op jit(solution)/shard_map/all_to_all | solution.py:605
  229.2 1.7 copy-start.1
  239.8 2.0 collective-permute-start.2
  242.7 3.0 %collective-permute-start.5 = (f32[112,128]{1,0:T(8,128)S(1)}, f32[112,128]{1,0:T(8,128)S(1)}, u32[]{:S(2)}, u32[]{:S(2)}) collective-permute-start(f32[112,128]{1,0:T(8,128)S(1)} %add.36), channel_id=1, source_target_pairs={{0,96},{32,0},{64,32},{96,64},{1,97},{33,1},{65,33},{97,65},{2,98}... | collective-permute-start | bytes 172040 | tf_op jit(solution)/shard_map/ppermute | solution.py:573
  243.0 4.2 %collective-permute-start.4 = (f32[112,128]{1,0:T(8,128)S(1)}, f32[112,128]{1,0:T(8,128)S(1)}, u32[]{:S(2)}, u32[]{:S(2)}) collective-permute-start(f32[112,128]{1,0:T(8,128)S(1)} %add.36), channel_id=1, source_target_pairs={{0,32},{32,64},{64,96},{96,0},{1,33},{33,65},{65,97},{97,1},{2,34}... | collective-permute-start | bytes 172040 | tf_op jit(solution)/shard_map/ppermute | solution.py:573
  244.1 4.6 %collective-permute-start.3 = (f32[112,128]{1,0:T(8,128)S(1)}, f32[112,128]{1,0:T(8,128)S(1)}, u32[]{:S(2)}, u32[]{:S(2)}) collective-permute-start(f32[112,128]{1,0:T(8,128)S(1)} %add.36), channel_id=1, source_target_pairs={{0,64},{32,96},{64,0},{96,32},{1,65},{33,97},{65,1},{97,33},{2,66}... | collective-permute-start | bytes 172040 | tf_op jit(solution)/shard_map/ppermute | solution.py:573
  248.8 3.1 %collective-permute-start.8 = (f32[112,128]{1,0:T(8,128)S(1)}, f32[112,128]{1,0:T(8,128)S(1)}, u32[]{:S(2)}, u32[]{:S(2)}) collective-permute-start(f32[112,128]{1,0:T(8,128)S(1)} %add_add_fusion.2), channel_id=1, source_target_pairs={{0,24},{1,25},{2,26},{3,27},{4,28},{5,29},{6,30},{7,31},{8,0},{9,1... | collective-permute-start | bytes 172040 | tf_op jit(solution)/shard_map/ppermute | solution.py:573
  249.7 4.2 %collective-permute-start.7 = (f32[112,128]{1,0:T(8,128)S(1)}, f32[112,128]{1,0:T(8,128)S(1)}, u32[]{:S(2)}, u32[]{:S(2)}) collective-permute-start(f32[112,128]{1,0:T(8,128)S(1)} %add_add_fusion.2), channel_id=1, source_target_pairs={{0,8},{1,9},{2,10},{3,11},{4,12},{5,13},{6,14},{7,15},{8,16},{9,17... | collective-permute-start | bytes 172040 | tf_op jit(solution)/shard_map/ppermute | solution.py:573
  250.3 5.1 %collective-permute-start.6 = (f32[112,128]{1,0:T(8,128)S(1)}, f32[112,128]{1,0:T(8,128)S(1)}, u32[]{:S(2)}, u32[]{:S(2)}) collective-permute-start(f32[112,128]{1,0:T(8,128)S(1)} %add_add_fusion.2), channel_id=1, source_target_pairs={{0,16},{1,17},{2,18},{3,19},{4,20},{5,21},{6,22},{7,23},{8,24},{9,... | collective-permute-start | bytes 172040 | tf_op jit(solution)/shard_map/ppermute | solution.py:573
  255.4 3.1 %collective-permute-start.11 = (f32[112,128]{1,0:T(8,128)S(1)}, f32[112,128]{1,0:T(8,128)S(1)}, u32[]{:S(2)}, u32[]{:S(2)}) collective-permute-start(f32[112,128]{1,0:T(8,128)S(1)} %add_add_fusion.1), channel_id=1, source_target_pairs={{0,6},{1,7},{2,0},{3,1},{4,2},{5,3},{6,4},{7,5},{8,14},{9,15},{10,... | collective-permute-start | bytes 172040 | tf_op jit(solution)/shard_map/ppermute | solution.py:573
  255.5 4.3 %collective-permute-start.10 = (f32[112,128]{1,0:T(8,128)S(1)}, f32[112,128]{1,0:T(8,128)S(1)}, u32[]{:S(2)}, u32[]{:S(2)}) collective-permute-start(f32[112,128]{1,0:T(8,128)S(1)} %add_add_fusion.1), channel_id=1, source_target_pairs={{0,2},{1,3},{2,4},{3,5},{4,6},{5,7},{6,0},{7,1},{8,10},{9,11},{10,... | collective-permute-start | bytes 172040 | tf_op jit(solution)/shard_map/ppermute | solution.py:573
  256.9 4.5 %collective-permute-start.9 = (f32[112,128]{1,0:T(8,128)S(1)}, f32[112,128]{1,0:T(8,128)S(1)}, u32[]{:S(2)}, u32[]{:S(2)}) collective-permute-start(f32[112,128]{1,0:T(8,128)S(1)} %add_add_fusion.1), channel_id=1, source_target_pairs={{0,4},{1,5},{2,6},{3,7},{4,0},{5,1},{6,2},{7,3},{8,12},{9,13},{10,... | collective-permute-start | bytes 172040 | tf_op jit(solution)/shard_map/ppermute | solution.py:573
  261.5 5.8 %copy-start.4 = (f32[112,128]{1,0:T(8,128)}, f32[112,128]{1,0:T(8,128)S(1)}, u32[]{:S(2)}) copy-start(f32[112,128]{1,0:T(8,128)S(1)} %add_add_fusion.mine_ref) | copy-start | bytes 172036
  261.5 5.8 %collective-permute-start.12 = (f32[112,128]{1,0:T(8,128)S(1)}, f32[112,128]{1,0:T(8,128)S(1)}, u32[]{:S(2)}, u32[]{:S(2)}) collective-permute-start(f32[112,128]{1,0:T(8,128)S(1)} %add_add_fusion.mine_ref), channel_id=1, source_target_pairs={{0,1},{1,0},{2,3},{3,2},{4,5},{5,4},{6,7},{7,6},{8,9},{9,8},{10,11... | collective-permute-start | bytes 172040 | tf_op jit(solution)/shard_map/ppermute | solution.py:580
  267.3 0.6 copy-start.8

commit v6 on v5

--- a/solution.py
+++ b/solution.py
@@ -14,7 +14,7 @@
 GROUPS = 4
 LANES = 128
 SPAN = GROUPS * BLK
-VMEM_LIMIT = 60 * 2**20
+VMEM_LIMIT = 62 * 2**20
 NT = (((1,), (1,)), ((), ()))
 WHOLE = pl.BlockSpec(memory_space=pltpu.VMEM)
 SCALARS = pl.BlockSpec(memory_space=pltpu.SMEM)
@@ -607,10 +607,10 @@
     scale = precond.reshape(1, -1)
     core = (lax.axis_index("row") % 2).reshape(1)
     vectors, kin, vector_sums = vectors_of(moved, kinetic, scale, 4)
-    image, keep, give = image_of(core, vectors, kin, vector_sums, pot, scale, 4)
+    image, keep, give = image_of(core, vectors, kin, vector_sums, pot, scale, 2)
     mine, other = sum_over_devices(keep, give)
     solved, rayleigh = solved_of(
-        core, mine, other, vectors, image, scale, float(rows * pieces), reps, 4
+        core, mine, other, vectors, image, scale, float(rows * pieces), reps, 2
     )
     return (solved.reshape(reps * vecs, 1, 1, -1), rayleigh)
 

time: 285 us -> 282 us (0.989)
  local copies, waits for them, and re-layouts: 11.5 us -> 8.11 us
    unnamed x18 -> x14, local copies, waits for them, and re-layouts: 5.22 us -> 1.86 us
  transfers between devices with their start and end apart: 16 -> 16, of which waited for: 13 -> 13; matrix products, arithmetic and copies ran while one was open for 1% -> 1% of each run, Pallas kernels for 51% -> 52%
where the time goes in v6:
time: 282 us; the launch traced here: 281 us
  Pallas kernels  171 us (61%)
  waiting for transfers between devices  58.7 us (21%)
  starting transfers between devices  40.8 us (14%)
  local copies, waits for them, and re-layouts  8.11 us (3%)
    pallas_call x1, Pallas kernels, surface_pass(): pl.pallas_call(surface_kernel, out_shape=jax.ShapeDtypeStruct((pieces * r...  111 us
    all_to_all x1, waiting for transfers between devices, body(): lax.all_to_all(restored, ('rep', 'row'), split_axis=0, concat_axis=0, til...  33.1 us
    pallas_call x1, Pallas kernels, index_streams(): pl.pallas_call(functools.partial(inverse_kernel, reps), out_shape=(stream...  19.1 us
    pallas_call x1, Pallas kernels, solved_of(): pl.pallas_call(functools.partial(solve_kernel, full_rows, reps), grid=(st...  16.3 us
    ppermute x9, waiting for transfers between devices, turned(): return lax.ppermute(x, axis, pairs)  12.7 us
    ppermute x1, waiting for transfers between devices, body(): high = lax.ppermute(basis_vecs[:, :edge], 'row', backward)  10.8 us
    all_to_all x1, starting transfers between devices, body(): lax.all_to_all(restored, ('rep', 'row'), split_axis=0, concat_axis=0, til...  9.25 us
    all_to_all x1, starting transfers between devices, body(): lax.all_to_all(by_piece, 'row', split_axis=0, concat_axis=0, tiled=True)  8.77 us
  transfers between devices with their start and end apart: 16, of which 13 were waited for; matrix products, arithmetic and copies ran while one was open for 1% of the time, Pallas kernels for 52%

profile of v6, /device:TPU:1, one launch (start us, length us, event | category | flops | bytes accessed | tf_op | source)
XLA Modules:
  0.0 280.9 jit_solution(16043113562370432278)
XLA Ops:
  0.6 3.9 %copy.16 = bf16[3,32,8,2048]{3,2,0,1:T(8,128)(2,1)} copy(bf16[3,32,8,2048]{3,2,1,0:T(8,128)(2,1)} %bitcast.15) | data formatting | bytes 6291456 | tf_op jit(solution)/shard_map/reshape | solution.py:596
  4.6 0.0 copy-start
  4.6 8.8 %all-to-all-start = ((bf16[32,24,2048]{2,1,0:T(8,128)(2,1)}), bf16[32,24,2048]{2,1,0:T(8,128)(2,1)}, u32[]{:S(2)}, u32[]{:S(2)}) async-start(bf16[32,24,2048]{2,1,0:T(8,128)(2,1)} %bitcast.14), calls=%async_computation | async-start | bytes 6291456 | tf_op jit(solution)/shard_map/all_to_all | solution.py:597
  13.4 0.8 fusion
  14.1 2.2 collective-permute-start.1
  16.3 3.4 %collective-permute-start = (bf16[24,512]{1,0:T(8,128)(2,1)S(1)}, bf16[24,512]{1,0:T(8,128)(2,1)S(1)}, u32[]{:S(2)}, u32[]{:S(2)}) collective-permute-start(bf16[24,512]{1,0:T(8,128)(2,1)S(1)} %get-tuple-element.37), channel_id=1, source_target_pairs={{0,1},{1,2},{2,3},{3,4},{4,5},{5,6},{6,7},{7,8},{8,9},{9,10},{10,1... | collective-permute-start | bytes 73736 | tf_op jit(solution)/shard_map/ppermute | solution.py:594
  19.7 0.0 copy-done
  19.7 0.8 reshape.35.perm_ref
  20.5 0.0 copy-start.5
  20.5 19.1 %shard_map.105 = (s32[512,128]{1,0:T(8,128)}, s32[512,128]{1,0:T(8,128)}) custom-call(s32[256,256]{1,0:T(8,128)} %reshape.35.perm_ref, f32[128]{0:T(128)} %constant.23.clone.power_ref), custom_call_target="tpu_custom_call" | custom-call | flops 8589934592 | bytes 524288 | tf_op jit(solution)/shard_map/pallas_call | solution.py:102
  39.5 0.0 copy-done.5
  39.5 0.6 subtract_reduce_fusion.column_ref
  40.1 10.8 %collective-permute-done.1.high_ref = bf16[24,512]{1,0:T(8,128)(2,1)S(1)} collective-permute-done((bf16[24,512]{1,0:T(8,128)(2,1)S(1)}, bf16[24,512]{1,0:T(8,128)(2,1)S(1)}, u32[]{:S(2)}, u32[]{:S(2)}) %collective-permute-start.1) | collective-permute-done | bytes 24608 | tf_op jit(solution)/shard_map/ppermute | solution.py:595
  51.0 0.0 copy-start.3
  51.0 0.0 collective-permute-done.low_ref
  51.0 0.6 copy-done.3
  51.6 0.0 copy-start.4
  51.6 0.6 copy-done.4
  52.2 7.4 %shard_map.104 = bf16[4,2,24,16384]{3,2,1,0:T(8,128)(2,1)} custom-call(bf16[24,65536]{1,0:T(8,128)(2,1)} %vecs_ref.1, bf16[24,512]{1,0:T(8,128)(2,1)} %copy-done.4, bf16[24,512]{1,0:T(8,128)(2,1)} %copy-done.3, s32[768]{0:T(1024)} %subtract_reduce_fusion.column_ref, f32[768]{0:T(1024)} %weight_ref.1), custom_call_target="tpu_custom_call" | custom-call | flops 9437184 | bytes 18874368 | tf_op jit(solution)/shard_map/pallas_call | solution.py:308
  59.6 0.0 copy-start.1
  59.6 0.0 all-to-all-done.arrived_ref
  59.6 5.4 %all-to-all-start.1 = ((bf16[4,2,24,16384]{3,2,1,0:T(8,128)(2,1)}), bf16[4,2,24,16384]{3,2,1,0:T(8,128)(2,1)}, u32[]{:S(2)}, u32[]{:S(2)}) async-start(bf16[4,2,24,16384]{3,2,1,0:T(8,128)(2,1)} %shard_map.104), calls=%async_computation.1 | async-start | bytes 12582912 | tf_op jit(solution)/shard_map/all_to_all | solution.py:602
  65.0 0.0 copy-done.1
  65.0 0.8 reshape.38.pot_ref
  65.7 111.2 %shard_map.106 = bf16[128,24,512]{2,1,0:T(8,128)(2,1)} custom-call(bf16[32,24,2048]{2,1,0:T(8,128)(2,1)} %all-to-all-done.arrived_ref, s32[65536]{0:T(1024)} %bitcast.16, s32[65536]{0:T(1024)} %bitcast.17, f32[256,256]{1,0:T(8,128)} %reshape.38.pot_ref, bf16[256,256]{1,0:T(8,128)(2,1)} %surf_ref.1), custom_call_target="tpu_custom_call" | custom-call | flops 1610612736 | bytes 300000000 | tf_op jit(solution)/shard_map/pallas_call | solution.py:254
  177.0 0.0 all-to-all-done.1.moved_ref
  177.0 9.3 %all-to-all-start.2 = ((bf16[128,24,512]{2,1,0:T(8,128)(2,1)}), bf16[128,24,512]{2,1,0:T(8,128)(2,1)}, u32[]{:S(2)}, u32[]{:S(2)}) async-start(bf16[128,24,512]{2,1,0:T(8,128)(2,1)} %shard_map.106), calls=%async_computation.2 | async-start | bytes 6291456 | tf_op jit(solution)/shard_map/all_to_all | solution.py:605
  186.2 8.5 %shard_map.107 = (bf16[96,16384]{1,0:T(8,128)(2,1)}, f32[96,16384]{1,0:T(8,128)}, f32[96,96]{1,0:T(8,128)}) custom-call(bf16[4,2,24,16384]{3,2,1,0:T(8,128)(2,1)} %all-to-all-done.1.moved_ref, bf16[256,256]{1,0:T(8,128)(2,1)} %kinetic_ref.1, f32[1,16384]{1,0:T(1,128)} %bitcast.18), custom_call_target="tpu_custom_call" | custom-call | flops 1811939328 | bytes 12582912 | tf_op jit(solution)/shard_map/pallas_call | solution.py:358
  194.7 33.1 %all-to-all-done.2 = bf16[128,24,512]{2,1,0:T(8,128)(2,1)} async-done(((bf16[128,24,512]{2,1,0:T(8,128)(2,1)}), bf16[128,24,512]{2,1,0:T(8,128)(2,1)}, u32[]{:S(2)}, u32[]{:S(2)}) %all-to-all-start.2) | async-done | bytes 3145760 | tf_op jit(solution)/shard_map/all_to_all | solution.py:605
  227.8 8.6 %shard_map.108 = (bf16[96,16384]{1,0:T(8,128)(2,1)}, f32[112,128]{1,0:T(8,128)}, f32[112,128]{1,0:T(8,128)}) custom-call(s32[1]{0:T(128)} %bitcast.core_ref, bf16[96,16384]{1,0:T(8,128)(2,1)} %get-tuple-element.23.vectors_ref, f32[96,16384]{1,0:T(8,128)} %get-tuple-element.24.kin_ref, f32[96,96]{1,0:T(8,128)} %get-tuple-element.25.vector_sums_ref, ...), custom_call_target="tpu_custom_call" | custom-call | flops 2415919104 | bytes 15728640 | tf_op jit(solution)/shard_map/pallas_call | solution.py:435
  236.4 0.9 collective-permute-start.2
  237.3 1.1 collective-permute-done.2
  238.4 0.8 add.36
  239.2 0.4 collective-permute-start.5
  239.6 1.1 collective-permute-start.4
  240.7 0.7 collective-permute-start.3
  241.4 0.9 collective-permute-done.5
  242.3 1.6 collective-permute-done.4
  243.9 1.5 collective-permute-done.3
  245.4 0.9 collective-permute-start.8
  246.3 0.7 collective-permute-start.7
  246.9 0.6 collective-permute-start.6
  247.5 0.9 collective-permute-done.8
  248.5 2.0 collective-permute-done.7
  250.5 1.5 collective-permute-done.6
  252.0 0.1 collective-permute-start.11
  252.1 1.5 collective-permute-start.10
  253.5 0.2 collective-permute-start.9
  253.8 1.3 collective-permute-done.11
  255.1 1.3 collective-permute-done.10
  256.4 1.7 collective-permute-done.9
  258.1 0.0 copy-start.2
  258.1 4.9 %collective-permute-start.12 = (f32[112,128]{1,0:T(8,128)S(1)}, f32[112,128]{1,0:T(8,128)S(1)}, u32[]{:S(2)}, u32[]{:S(2)}) collective-permute-start(f32[112,128]{1,0:T(8,128)S(1)} %add_add_fusion.mine_ref), channel_id=1, source_target_pairs={{0,1},{1,0},{2,3},{3,2},{4,5},{5,4},{6,7},{7,6},{8,9},{9,8},{10,11... | collective-permute-start | bytes 172040 | tf_op jit(solution)/shard_map/ppermute | solution.py:580
  263.0 0.9 collective-permute-done.12.other_ref
  263.9 0.0 copy-start.6
  263.9 0.0 copy-done.2
  263.9 0.6 copy-done.6
  264.5 16.3 %shard_map.109 = (f32[96,1,16384]{2,1,0:T(1,128)}, f32[96,96]{1,0:T(8,128)}) custom-call(s32[1]{0:T(128)} %bitcast.core_ref, f32[112,128]{1,0:T(8,128)} %copy-done.2, f32[112,128]{1,0:T(8,128)} %copy-done.6, bf16[96,16384]{1,0:T(8,128)(2,1)} %get-tuple-element.23.vectors_ref, bf16[96,16384]{1,0:T(8,128)(2,1)} %get-tuple-element.29.image_ref, f32[1,16384]{1,0:T(1,128)} %bitcast.20), custom_call_target="tpu_custom_call" | custom-call | flops 1811939328 | bytes 12582912 | tf_op jit(solution)/shard_map/pallas_call | solution.py:537
  (3 shorter events, 0.0 us)
Async XLA Ops:
  4.6 15.1 %copy-start = (s32[65536]{0:T(1024)S(1)}, s32[65536]{0:T(1024)}, u32[]{:S(2)}) copy-start(s32[65536]{0:T(1024)} %param.12) | copy-start | bytes 786436
  4.6 55.0 %all-to-all-start = ((bf16[32,24,2048]{2,1,0:T(8,128)(2,1)}), bf16[32,24,2048]{2,1,0:T(8,128)(2,1)}, u32[]{:S(2)}, u32[]{:S(2)}) async-start(bf16[32,24,2048]{2,1,0:T(8,128)(2,1)} %bitcast.14), calls=%async_computation | async-start | bytes 6291456 | tf_op jit(solution)/shard_map/all_to_all | solution.py:597
  14.1 36.9 %collective-permute-start.1 = (bf16[24,512]{1,0:T(8,128)(2,1)S(1)}, bf16[24,512]{1,0:T(8,128)(2,1)S(1)}, u32[]{:S(2)}, u32[]{:S(2)}) collective-permute-start(bf16[24,512]{1,0:T(8,128)(2,1)S(1)} %get-tuple-element.36), channel_id=1, source_target_pairs={{1,0},{2,1},{3,2},{4,3},{5,4},{6,5},{7,6},{8,7},{9,8},{10,9},{11,1... | collective-permute-start | bytes 73736 | tf_op jit(solution)/shard_map/ppermute | solution.py:595
  16.3 34.7 %collective-permute-start = (bf16[24,512]{1,0:T(8,128)(2,1)S(1)}, bf16[24,512]{1,0:T(8,128)(2,1)S(1)}, u32[]{:S(2)}, u32[]{:S(2)}) collective-permute-start(bf16[24,512]{1,0:T(8,128)(2,1)S(1)} %get-tuple-element.37), channel_id=1, source_target_pairs={{0,1},{1,2},{2,3},{3,4},{4,5},{5,6},{6,7},{7,8},{8,9},{9,10},{10,1... | collective-permute-start | bytes 73736 | tf_op jit(solution)/shard_map/ppermute | solution.py:594
  20.5 19.1 %copy-start.5 = (s32[768,2]{0,1:T(2,128)S(1)}, s32[768,2]{0,1:T(2,128)}, u32[]{:S(2)}) copy-start(s32[768,2]{0,1:T(2,128)} %param.14) | copy-start | bytes 18436
  51.0 0.6 copy-start.3
  51.6 0.6 copy-start.4
  59.6 5.4 %copy-start.1 = (f32[65536]{0:T(1024)S(1)}, f32[65536]{0:T(1024)}, u32[]{:S(2)}) copy-start(f32[65536]{0:T(1024)} %param.10) | copy-start | bytes 786436
  59.6 117.4 %all-to-all-start.1 = ((bf16[4,2,24,16384]{3,2,1,0:T(8,128)(2,1)}), bf16[4,2,24,16384]{3,2,1,0:T(8,128)(2,1)}, u32[]{:S(2)}, u32[]{:S(2)}) async-start(bf16[4,2,24,16384]{3,2,1,0:T(8,128)(2,1)} %shard_map.104), calls=%async_computation.1 | async-start | bytes 12582912 | tf_op jit(solution)/shard_map/all_to_all | solution.py:602
  177.0 50.9 %all-to-all-start.2 = ((bf16[128,24,512]{2,1,0:T(8,128)(2,1)}), bf16[128,24,512]{2,1,0:T(8,128)(2,1)}, u32[]{:S(2)}, u32[]{:S(2)}) async-start(bf16[128,24,512]{2,1,0:T(8,128)(2,1)} %shard_map.106), calls=%async_computation.2 | async-start | bytes 6291456 | tf_op jit(solution)/shard_map/all_to_all | solution.py:605
  236.4 2.0 collective-permute-start.2
  239.2 3.0 %collective-permute-start.5 = (f32[112,128]{1,0:T(8,128)S(1)}, f32[112,128]{1,0:T(8,128)S(1)}, u32[]{:S(2)}, u32[]{:S(2)}) collective-permute-start(f32[112,128]{1,0:T(8,128)S(1)} %add.36), channel_id=1, source_target_pairs={{0,96},{32,0},{64,32},{96,64},{1,97},{33,1},{65,33},{97,65},{2,98}... | collective-permute-start | bytes 172040 | tf_op jit(solution)/shard_map/ppermute | solution.py:573
  239.6 4.2 %collective-permute-start.4 = (f32[112,128]{1,0:T(8,128)S(1)}, f32[112,128]{1,0:T(8,128)S(1)}, u32[]{:S(2)}, u32[]{:S(2)}) collective-permute-start(f32[112,128]{1,0:T(8,128)S(1)} %add.36), channel_id=1, source_target_pairs={{0,32},{32,64},{64,96},{96,0},{1,33},{33,65},{65,97},{97,1},{2,34}... | collective-permute-start | bytes 172040 | tf_op jit(solution)/shard_map/ppermute | solution.py:573
  240.7 4.6 %collective-permute-start.3 = (f32[112,128]{1,0:T(8,128)S(1)}, f32[112,128]{1,0:T(8,128)S(1)}, u32[]{:S(2)}, u32[]{:S(2)}) collective-permute-start(f32[112,128]{1,0:T(8,128)S(1)} %add.36), channel_id=1, source_target_pairs={{0,64},{32,96},{64,0},{96,32},{1,65},{33,97},{65,1},{97,33},{2,66}... | collective-permute-start | bytes 172040 | tf_op jit(solution)/shard_map/ppermute | solution.py:573
  245.4 3.1 %collective-permute-start.8 = (f32[112,128]{1,0:T(8,128)S(1)}, f32[112,128]{1,0:T(8,128)S(1)}, u32[]{:S(2)}, u32[]{:S(2)}) collective-permute-start(f32[112,128]{1,0:T(8,128)S(1)} %add_add_fusion.2), channel_id=1, source_target_pairs={{0,24},{1,25},{2,26},{3,27},{4,28},{5,29},{6,30},{7,31},{8,0},{9,1... | collective-permute-start | bytes 172040 | tf_op jit(solution)/shard_map/ppermute | solution.py:573
  246.3 4.2 %collective-permute-start.7 = (f32[112,128]{1,0:T(8,128)S(1)}, f32[112,128]{1,0:T(8,128)S(1)}, u32[]{:S(2)}, u32[]{:S(2)}) collective-permute-start(f32[112,128]{1,0:T(8,128)S(1)} %add_add_fusion.2), channel_id=1, source_target_pairs={{0,8},{1,9},{2,10},{3,11},{4,12},{5,13},{6,14},{7,15},{8,16},{9,17... | collective-permute-start | bytes 172040 | tf_op jit(solution)/shard_map/ppermute | solution.py:573
  246.9 5.1 %collective-permute-start.6 = (f32[112,128]{1,0:T(8,128)S(1)}, f32[112,128]{1,0:T(8,128)S(1)}, u32[]{:S(2)}, u32[]{:S(2)}) collective-permute-start(f32[112,128]{1,0:T(8,128)S(1)} %add_add_fusion.2), channel_id=1, source_target_pairs={{0,16},{1,17},{2,18},{3,19},{4,20},{5,21},{6,22},{7,23},{8,24},{9,... | collective-permute-start | bytes 172040 | tf_op jit(solution)/shard_map/ppermute | solution.py:573
  252.0 3.1 %collective-permute-start.11 = (f32[112,128]{1,0:T(8,128)S(1)}, f32[112,128]{1,0:T(8,128)S(1)}, u32[]{:S(2)}, u32[]{:S(2)}) collective-permute-start(f32[112,128]{1,0:T(8,128)S(1)} %add_add_fusion.1), channel_id=1, source_target_pairs={{0,6},{1,7},{2,0},{3,1},{4,2},{5,3},{6,4},{7,5},{8,14},{9,15},{10,... | collective-permute-start | bytes 172040 | tf_op jit(solution)/shard_map/ppermute | solution.py:573
  252.1 4.3 %collective-permute-start.10 = (f32[112,128]{1,0:T(8,128)S(1)}, f32[112,128]{1,0:T(8,128)S(1)}, u32[]{:S(2)}, u32[]{:S(2)}) collective-permute-start(f32[112,128]{1,0:T(8,128)S(1)} %add_add_fusion.1), channel_id=1, source_target_pairs={{0,2},{1,3},{2,4},{3,5},{4,6},{5,7},{6,0},{7,1},{8,10},{9,11},{10,... | collective-permute-start | bytes 172040 | tf_op jit(solution)/shard_map/ppermute | solution.py:573
  253.5 4.5 %collective-permute-start.9 = (f32[112,128]{1,0:T(8,128)S(1)}, f32[112,128]{1,0:T(8,128)S(1)}, u32[]{:S(2)}, u32[]{:S(2)}) collective-permute-start(f32[112,128]{1,0:T(8,128)S(1)} %add_add_fusion.1), channel_id=1, source_target_pairs={{0,4},{1,5},{2,6},{3,7},{4,0},{5,1},{6,2},{7,3},{8,12},{9,13},{10,... | collective-permute-start | bytes 172040 | tf_op jit(solution)/shard_map/ppermute | solution.py:573
  258.1 5.8 %copy-start.2 = (f32[112,128]{1,0:T(8,128)}, f32[112,128]{1,0:T(8,128)S(1)}, u32[]{:S(2)}) copy-start(f32[112,128]{1,0:T(8,128)S(1)} %add_add_fusion.mine_ref) | copy-start | bytes 172036
  258.1 5.8 %collective-permute-start.12 = (f32[112,128]{1,0:T(8,128)S(1)}, f32[112,128]{1,0:T(8,128)S(1)}, u32[]{:S(2)}, u32[]{:S(2)}) collective-permute-start(f32[112,128]{1,0:T(8,128)S(1)} %add_add_fusion.mine_ref), channel_id=1, source_target_pairs={{0,1},{1,0},{2,3},{3,2},{4,5},{5,4},{6,7},{7,6},{8,9},{9,8},{10,11... | collective-permute-start | bytes 172040 | tf_op jit(solution)/shard_map/ppermute | solution.py:580
  263.9 0.6 copy-start.6
